TPU v7x, 32 devices: a whole 2x2x4 slice. The times are simulated.
32 devices in a mesh: slab: 2 (over x), iface: 4 (over y, core), mech: 4 (over z).
Axes of the slice: x: 2, y: 2, z: 4, core: 2. Of those that a mesh axis runs over, the one named last changes fastest.
Arguments:
- temp_start: float32 [16, 4, 8, 512], P(('slab', 'mech'), 'iface'), may hold values from 0.5 to 3
- conductivity: float32 [16, 4, 8, 512], P(('slab', 'mech'), 'iface'), may hold values from 0.3 to 2.8
- gap_conductance: float32 [16, 4, 8], P(('slab', 'mech'), 'iface'), may hold values from 10 to 20
- partner: int32 [32], P('iface'), may hold values from 0 to 31, each once
- row_order: int32 [4, 8], P('iface'), may hold values from 0 to 7, each once within a row
- active_layers: int32 [4, 8], P('iface', ('slab', 'mech')), may hold values from 1 to 2, as said below
- trial_stress: float32 [16, 4, 8, 512], P(None, 'iface', ('slab', 'mech')), may hold values from 0.5 to 2
Outputs:
- stress: float32 [16, 4, 8, 512], P(None, 'iface', ('slab', 'mech'))
- element_strain: float32 [2, 4, 8, 512], P(None, 'iface', ('slab', 'mech'))
Inputs may be any that keep to these rules, and one draw needn't show every extreme that they name: `active_layers`: element layers that creep in one element row; some row has all 2.
All inputs are finite; a program needn't handle non-finite values.
Results may differ from a plain program's by a relative error of at most 0.00005.
Values sent between devices are 32-bit elements; how exact they have to be, the bound alone decides.
No kernel may reach another device: no remote copies, remote signals or barrier semaphores. Data moves between devices by JAX's collectives and lax.ppermute only.
A program may use at most 64 MiB of HBM per device.

v0:
```python
import jax
import jax.numpy as jnp
from jax import lax
from jax.sharding import PartitionSpec as P

SWEEPS = 2
NEWTON = 4


FLUX_STEP = 0.03
CREEP_RATE = 200.0
ACTIVATION = 12.0
REFERENCE_TEMP = 1.0


def padded(block, sides, width):
    for axis, dim in sides:
        count = lax.axis_size(axis)
        forward = [(i, i + 1) for i in range(count - 1)]
        backward = [(target, source) for source, target in forward]
        low = lax.ppermute(
            lax.slice_in_dim(block, block.shape[dim] - width, None, axis=dim), axis, forward
        )
        high = lax.ppermute(lax.slice_in_dim(block, 0, width, axis=dim), axis, backward)
        block = jnp.concatenate([low, block, high], axis=dim)
    return block


def neighbour_weight(shift_z, shift_a, shift_r):
    reach = abs(shift_z) + abs(shift_a) + abs(shift_r)
    return [0.0, 1.0, 0.5, 0.25][reach]


def conduction(padded_temp, padded_cond):
    center_temp = padded_temp[1:-1, 1:-1, 1:-1]
    center_cond = padded_cond[1:-1, 1:-1, 1:-1]
    depth, across, radial = center_temp.shape
    radial_index = jnp.arange(radial, dtype=jnp.int32)
    gap_row = radial // 2
    outward_open = (radial_index != gap_row - 1).astype(jnp.float32)
    inward_open = (radial_index != gap_row).astype(jnp.float32)
    total = jnp.zeros(center_temp.shape, jnp.float32)
    for shift_z in (-1, 0, 1):
        for shift_a in (-1, 0, 1):
            for shift_r in (-1, 0, 1):
                if shift_z == 0 and shift_a == 0 and (shift_r == 0):
                    continue
                near_temp = padded_temp[
                    1 + shift_z : 1 + shift_z + depth,
                    1 + shift_a : 1 + shift_a + across,
                    1 + shift_r : 1 + shift_r + radial,
                ]
                near_cond = padded_cond[
                    1 + shift_z : 1 + shift_z + depth,
                    1 + shift_a : 1 + shift_a + across,
                    1 + shift_r : 1 + shift_r + radial,
                ]
                face = neighbour_weight(shift_z, shift_a, shift_r) * 0.5 * (center_cond + near_cond)
                if shift_r == 1:
                    face = face * outward_open
                elif shift_r == -1:
                    face = face * inward_open
                total = total + face * (near_temp - center_temp)
    return FLUX_STEP * total


def creep_return(mech_temp, trial, active_layers):
    rate = CREEP_RATE * jnp.exp(-ACTIVATION / (mech_temp + REFERENCE_TEMP))
    slip = jnp.zeros(trial.shape, jnp.float32)
    for newton_step in range(NEWTON):
        left = trial - slip
        residue = slip - rate * left**3
        slope = 1.0 + 3.0 * rate * left**2
        slip = slip - residue / slope
    depth = trial.shape[0]
    layer = jnp.arange(depth, dtype=jnp.int32) // 8
    live = (layer[:, None, None] < active_layers[None, :, :]).astype(jnp.float32)[..., None]
    creep = live * slip
    stress = trial - creep
    strain = jnp.sum(creep.reshape((depth // 8, 8) + trial.shape[1:]), axis=1) * 0.125
    return (stress, strain)


def on_device(
    temp_start, conductivity, gap_conductance, partner, row_order, active_layers, trial_stress
):
    depth = temp_start.shape[0]
    rows = temp_start.shape[2]
    radial = temp_start.shape[3]
    temp = temp_start.reshape(depth, rows, radial)
    cond = conductivity.reshape(depth, rows, radial)
    gap = gap_conductance.reshape(depth, rows)
    gap_row = radial // 2
    sections = lax.axis_size("iface")
    across = rows * sections
    all_cols = jnp.arange(across, dtype=jnp.int32)
    cond_rim = padded(cond, ((("slab", "mech"), 0), ("iface", 1)), 1)
    padded_cond = jnp.pad(cond_rim, ((0, 0), (0, 0), (1, 1)))
    spread_table = (partner[:, None] == all_cols[None, :]).astype(jnp.float32)
    for sweep in range(SWEEPS):
        temp_rim = padded(temp, ((("slab", "mech"), 0), ("iface", 1)), 1)
        padded_temp = jnp.pad(temp_rim, ((0, 0), (0, 0), (1, 1)))
        compact = temp[:, :, gap_row - 1]
        canister = temp[:, :, gap_row]
        compact_all = lax.all_gather(compact, "iface", axis=1, tiled=True)
        facing = jnp.take(compact_all, partner, axis=1)
        flux = gap * (facing - canister)
        spread = jnp.dot(
            flux, spread_table, precision=lax.Precision.HIGHEST, preferred_element_type=jnp.float32
        )
        returned = lax.psum_scatter(spread, "iface", scatter_dimension=1, tiled=True)
        fresh = temp + conduction(padded_temp, padded_cond)
        temp = (
            fresh.at[:, :, gap_row]
            .add(FLUX_STEP * flux)
            .at[:, :, gap_row - 1]
            .add(-FLUX_STEP * returned)
        )
    permuted = jnp.take(temp, row_order[0], axis=1)
    mech_temp = lax.all_to_all(permuted, ("slab", "mech"), split_axis=1, concat_axis=0, tiled=True)
    mech_temp = mech_temp.reshape(mech_temp.shape[0], 1, mech_temp.shape[1], radial)
    return creep_return(mech_temp, trial_stress, active_layers)


def solution(mesh):
    placed = (
        P(("slab", "mech"), "iface", None, None),
        P(("slab", "mech"), "iface", None, None),
        P(("slab", "mech"), "iface", None),
        P("iface"),
        P("iface", None),
        P("iface", ("slab", "mech")),
        P(None, "iface", ("slab", "mech"), None),
    )
    return jax.shard_map(
        on_device,
        mesh=mesh,
        in_specs=placed,
        out_specs=(
            P(None, "iface", ("slab", "mech"), None),
            P(None, "iface", ("slab", "mech"), None),
        ),
        check_vma=False,
    )
```

profile of v0, /device:TPU:0, one launch (start us, length us, event | category | flops | bytes accessed | tf_op | source)
XLA Modules:
  0.0 90.7 jit_solution(18342003587583639605)
XLA Ops:
  0.6 0.7 slice_bitcast_fusion.2
  1.4 4.9 %collective-permute-start = (f32[1,8,512]{2,1,0:T(8,128)S(1)}, f32[1,8,512]{2,1,0:T(8,128)S(1)}, u32[]{:S(2)}, u32[]{:S(2)}) collective-permute-start(f32[1,8,512]{2,1,0:T(8,128)S(1)} %get-tuple-element.78), channel_id=1, source_target_pairs={{0,1},{1,2},{2,3},{3,16},{16,17},{17,18},{18,19},{4,5},{5,6},{6,7}... | collective-permute-start | bytes 49160 | tf_op jit(solution)/shard_map/ppermute | solution.py:21
  6.3 1.3 %collective-permute-start.1 = (f32[1,8,512]{2,1,0:T(8,128)S(1)}, f32[1,8,512]{2,1,0:T(8,128)S(1)}, u32[]{:S(2)}, u32[]{:S(2)}) collective-permute-start(f32[1,8,512]{2,1,0:T(8,128)S(1)} %get-tuple-element.77), channel_id=1, source_target_pairs={{1,0},{2,1},{3,2},{16,3},{17,16},{18,17},{19,18},{5,4},{6,5},{7,6}... | collective-permute-start | bytes 49160 | tf_op jit(solution)/shard_map/ppermute | solution.py:24
  7.6 4.5 %collective-permute-start.4 = (f32[1,8,512]{2,1,0:T(8,128)S(1)}, f32[1,8,512]{2,1,0:T(8,128)S(1)}, u32[]{:S(2)}, u32[]{:S(2)}) collective-permute-start(f32[1,8,512]{2,1,0:T(8,128)S(1)} %get-tuple-element.79), channel_id=1, source_target_pairs={{0,1},{1,2},{2,3},{3,16},{16,17},{17,18},{18,19},{4,5},{5,6},{6,7}... | collective-permute-start | bytes 49160 | tf_op jit(solution)/shard_map/ppermute | solution.py:21
  12.2 1.3 %collective-permute-start.5 = (f32[1,8,512]{2,1,0:T(8,128)S(1)}, f32[1,8,512]{2,1,0:T(8,128)S(1)}, u32[]{:S(2)}, u32[]{:S(2)}) collective-permute-start(f32[1,8,512]{2,1,0:T(8,128)S(1)} %get-tuple-element.80), channel_id=1, source_target_pairs={{1,0},{2,1},{3,2},{16,3},{17,16},{18,17},{19,18},{5,4},{6,5},{7,6}... | collective-permute-start | bytes 49160 | tf_op jit(solution)/shard_map/ppermute | solution.py:24
  13.5 0.6 copy-done.5
  14.2 0.6 copy-done.4
  14.9 0.1 copy.118
  15.1 5.2 %all-gather = f32[2,32,1]{0,2,1:T(1,128)S(1)} all-gather(f32[2,8,1]{0,2,1:T(1,128)S(1)} %copy.118), channel_id=2, replica_groups=mesh['slab'=2,'iface'=4,'mech'=4] {'iface'}, dimensions={1}, use_global_device_ids=true | all-gather | bytes 320 | tf_op jit(solution)/shard_map/all_gather | solution.py:105
  20.2 0.1 copy.152
  20.4 0.7 copy-done.3
  21.1 0.6 gather_fusion.1
  21.8 0.2 fusion.169
  22.0 7.2 %all-reduce.3 = f32[2,32]{1,0:T(2,128)S(1)} all-reduce(f32[2,32]{1,0:T(2,128)S(1)} %fusion.169), channel_id=4, replica_groups=mesh['slab'=2,'iface'=4,'mech'=4] {'iface'}, use_global_device_ids=true, to_apply=%region_0.2.clone | all-reduce | flops 64 | bytes 512
  29.2 0.6 dynamic-slice.32
  30.5 0.1 copy.124
  30.6 0.1 copy.125
  31.4 1.3 %collective-permute-start.2 = (f32[4,1,512]{2,1,0:T(1,128)S(1)}, f32[4,1,512]{2,1,0:T(1,128)S(1)}, u32[]{:S(2)}, u32[]{:S(2)}) collective-permute-start(f32[4,1,512]{2,1,0:T(1,128)S(1)} %get-tuple-element.69), channel_id=1, source_target_pairs={{0,4},{4,8},{8,12},{1,5},{5,9},{9,13},{2,6},{6,10},{10,14},{3,7},{... | collective-permute-start | bytes 24584 | tf_op jit(solution)/shard_map/ppermute | solution.py:21
  32.7 1.3 %collective-permute-start.3 = (f32[4,1,512]{2,1,0:T(1,128)S(1)}, f32[4,1,512]{2,1,0:T(1,128)S(1)}, u32[]{:S(2)}, u32[]{:S(2)}) collective-permute-start(f32[4,1,512]{2,1,0:T(1,128)S(1)} %get-tuple-element.70), channel_id=1, source_target_pairs={{4,0},{8,4},{12,8},{5,1},{9,5},{13,9},{6,2},{10,6},{14,10},{7,3},{... | collective-permute-start | bytes 24584 | tf_op jit(solution)/shard_map/ppermute | solution.py:24
  34.1 3.8 %collective-permute-start.6 = (f32[4,1,512]{2,1,0:T(1,128)S(1)}, f32[4,1,512]{2,1,0:T(1,128)S(1)}, u32[]{:S(2)}, u32[]{:S(2)}) collective-permute-start(f32[4,1,512]{2,1,0:T(1,128)S(1)} %get-tuple-element.71), channel_id=1, source_target_pairs={{0,4},{4,8},{8,12},{1,5},{5,9},{9,13},{2,6},{6,10},{10,14},{3,7},{... | collective-permute-start | bytes 24584 | tf_op jit(solution)/shard_map/ppermute | solution.py:21
  37.8 1.3 %collective-permute-start.7 = (f32[4,1,512]{2,1,0:T(1,128)S(1)}, f32[4,1,512]{2,1,0:T(1,128)S(1)}, u32[]{:S(2)}, u32[]{:S(2)}) collective-permute-start(f32[4,1,512]{2,1,0:T(1,128)S(1)} %get-tuple-element.72), channel_id=1, source_target_pairs={{4,0},{8,4},{12,8},{5,1},{9,5},{13,9},{6,2},{10,6},{14,10},{7,3},{... | collective-permute-start | bytes 24584 | tf_op jit(solution)/shard_map/ppermute | solution.py:24
  39.2 0.2 select_maximum_fusion.8
  39.3 2.8 %collective-permute-done.7 = f32[4,1,512]{2,1,0:T(1,128)S(1)} collective-permute-done((f32[4,1,512]{2,1,0:T(1,128)S(1)}, f32[4,1,512]{2,1,0:T(1,128)S(1)}, u32[]{:S(2)}, u32[]{:S(2)}) %collective-permute-start.7) | collective-permute-done | bytes 8224 | tf_op jit(solution)/shard_map/ppermute | solution.py:24
  42.1 0.2 select_maximum_fusion.4
  42.3 0.3 fusion.82
  42.8 0.1 copy.126
  42.9 0.2 scatter-add.15
  43.1 0.1 copy.156
  43.2 6.2 %all-gather.1 = f32[2,32,1]{0,2,1:T(1,128)S(1)} all-gather(f32[2,8,1]{0,2,1:T(1,128)S(1)} %copy.126), channel_id=3, replica_groups=mesh['slab'=2,'iface'=4,'mech'=4] {'iface'}, dimensions={1}, use_global_device_ids=true | all-gather | bytes 320 | tf_op jit(solution)/shard_map/all_gather | solution.py:105
  49.4 0.6 gather_fusion.2
  50.0 4.5 %collective-permute-start.8 = (f32[1,8,512]{2,1,0:T(8,128)S(1)}, f32[1,8,512]{2,1,0:T(8,128)S(1)}, u32[]{:S(2)}, u32[]{:S(2)}) collective-permute-start(f32[1,8,512]{2,1,0:T(8,128)S(1)} %get-tuple-element.73), channel_id=1, source_target_pairs={{0,1},{1,2},{2,3},{3,16},{16,17},{17,18},{18,19},{4,5},{5,6},{6,7}... | collective-permute-start | bytes 49160 | tf_op jit(solution)/shard_map/ppermute | solution.py:21
  54.5 1.3 %collective-permute-start.9 = (f32[1,8,512]{2,1,0:T(8,128)S(1)}, f32[1,8,512]{2,1,0:T(8,128)S(1)}, u32[]{:S(2)}, u32[]{:S(2)}) collective-permute-start(f32[1,8,512]{2,1,0:T(8,128)S(1)} %get-tuple-element.74), channel_id=1, source_target_pairs={{1,0},{2,1},{3,2},{16,3},{17,16},{18,17},{19,18},{5,4},{6,5},{7,6}... | collective-permute-start | bytes 49160 | tf_op jit(solution)/shard_map/ppermute | solution.py:24
  55.9 0.2 fusion.168
  56.1 6.7 %all-reduce.4 = f32[2,32]{1,0:T(2,128)S(1)} all-reduce(f32[2,32]{1,0:T(2,128)S(1)} %fusion.168), channel_id=5, replica_groups=mesh['slab'=2,'iface'=4,'mech'=4] {'iface'}, use_global_device_ids=true, to_apply=%region_1.3.clone | all-reduce | flops 64 | bytes 512
  62.8 1.3 %collective-permute-start.10 = (f32[4,1,512]{2,1,0:T(1,128)S(1)}, f32[4,1,512]{2,1,0:T(1,128)S(1)}, u32[]{:S(2)}, u32[]{:S(2)}) collective-permute-start(f32[4,1,512]{2,1,0:T(1,128)S(1)} %get-tuple-element.67), channel_id=1, source_target_pairs={{0,4},{4,8},{8,12},{1,5},{5,9},{9,13},{2,6},{6,10},{10,14},{3,7},{... | collective-permute-start | bytes 24584 | tf_op jit(solution)/shard_map/ppermute | solution.py:21
  64.1 1.3 %collective-permute-start.11 = (f32[4,1,512]{2,1,0:T(1,128)S(1)}, f32[4,1,512]{2,1,0:T(1,128)S(1)}, u32[]{:S(2)}, u32[]{:S(2)}) collective-permute-start(f32[4,1,512]{2,1,0:T(1,128)S(1)} %get-tuple-element.68), channel_id=1, source_target_pairs={{4,0},{8,4},{12,8},{5,1},{9,5},{13,9},{6,2},{10,6},{14,10},{7,3},{... | collective-permute-start | bytes 24584 | tf_op jit(solution)/shard_map/ppermute | solution.py:24
  65.5 0.1 copy.132
  65.7 2.4 %collective-permute-done.11 = f32[4,1,512]{2,1,0:T(1,128)S(1)} collective-permute-done((f32[4,1,512]{2,1,0:T(1,128)S(1)}, f32[4,1,512]{2,1,0:T(1,128)S(1)}, u32[]{:S(2)}, u32[]{:S(2)}) %collective-permute-start.11) | collective-permute-done | bytes 8224 | tf_op jit(solution)/shard_map/ppermute | solution.py:24
  68.1 0.2 select_maximum_fusion
  68.3 0.3 fusion.25
  68.7 0.2 scatter-add.19
  68.9 0.6 gather_fusion
  69.5 0.7 select_bitcast_fusion
  70.2 11.5 %all-to-all-start = ((f32[2,8,512]{2,0,1:T(2,128)}), f32[2,8,512]{2,0,1:T(2,128)S(1)}, u32[]{:S(2)}, u32[]{:S(2)}) async-start(f32[2,8,512]{2,0,1:T(2,128)} %select_bitcast_fusion), calls=%async_computation | async-start | bytes 65536 | tf_op jit(solution)/shard_map/all_to_all | solution.py:120
  81.7 6.7 %all-to-all-done = f32[2,8,512]{2,0,1:T(2,128)S(1)} async-done(((f32[2,8,512]{2,0,1:T(2,128)}), f32[2,8,512]{2,0,1:T(2,128)S(1)}, u32[]{:S(2)}, u32[]{:S(2)}) %all-to-all-start) | async-done | bytes 32800 | tf_op jit(solution)/shard_map/all_to_all | solution.py:120
  88.6 0.7 copy-done.2
  89.4 0.6 copy.150
  90.1 0.6 mul.710
  (57 shorter events, 1.2 us)
Async XLA Ops:
  0.6 7.0 %copy-start.1 = (f32[2,1,8,512]{3,2,1,0:T(8,128)S(1)}, f32[2,1,8,512]{3,2,1,0:T(8,128)}, u32[]{:S(2)}) copy-start(f32[2,1,8,512]{3,2,1,0:T(8,128)} %param.17) | copy-start | bytes 98308
  1.4 30.0 %collective-permute-start = (f32[1,8,512]{2,1,0:T(8,128)S(1)}, f32[1,8,512]{2,1,0:T(8,128)S(1)}, u32[]{:S(2)}, u32[]{:S(2)}) collective-permute-start(f32[1,8,512]{2,1,0:T(8,128)S(1)} %get-tuple-element.78), channel_id=1, source_target_pairs={{0,1},{1,2},{2,3},{3,16},{16,17},{17,18},{18,19},{4,5},{5,6},{6,7}... | collective-permute-start | bytes 49160 | tf_op jit(solution)/shard_map/ppermute | solution.py:21
  6.3 25.1 %collective-permute-start.1 = (f32[1,8,512]{2,1,0:T(8,128)S(1)}, f32[1,8,512]{2,1,0:T(8,128)S(1)}, u32[]{:S(2)}, u32[]{:S(2)}) collective-permute-start(f32[1,8,512]{2,1,0:T(8,128)S(1)} %get-tuple-element.77), channel_id=1, source_target_pairs={{1,0},{2,1},{3,2},{16,3},{17,16},{18,17},{19,18},{5,4},{6,5},{7,6}... | collective-permute-start | bytes 49160 | tf_op jit(solution)/shard_map/ppermute | solution.py:24
  7.6 26.4 %collective-permute-start.4 = (f32[1,8,512]{2,1,0:T(8,128)S(1)}, f32[1,8,512]{2,1,0:T(8,128)S(1)}, u32[]{:S(2)}, u32[]{:S(2)}) collective-permute-start(f32[1,8,512]{2,1,0:T(8,128)S(1)} %get-tuple-element.79), channel_id=1, source_target_pairs={{0,1},{1,2},{2,3},{3,16},{16,17},{17,18},{18,19},{4,5},{5,6},{6,7}... | collective-permute-start | bytes 49160 | tf_op jit(solution)/shard_map/ppermute | solution.py:21
  12.2 21.8 %collective-permute-start.5 = (f32[1,8,512]{2,1,0:T(8,128)S(1)}, f32[1,8,512]{2,1,0:T(8,128)S(1)}, u32[]{:S(2)}, u32[]{:S(2)}) collective-permute-start(f32[1,8,512]{2,1,0:T(8,128)S(1)} %get-tuple-element.80), channel_id=1, source_target_pairs={{1,0},{2,1},{3,2},{16,3},{17,16},{18,17},{19,18},{5,4},{6,5},{7,6}... | collective-permute-start | bytes 49160 | tf_op jit(solution)/shard_map/ppermute | solution.py:24
  13.5 0.7 copy-start.5
  14.2 0.7 copy-start.4
  20.4 0.7 copy-start.3
  21.8 7.4 %copy-start.6 = (u32[32]{0:T(128)S(1)}, u32[32]{0:T(128)}, u32[]{:S(2)}) copy-start(u32[32]{0:T(128)} %constant.186) | copy-start | bytes 388
  22.0 9.4 %copy-start = (f32[2,1,8,512]{3,2,1,0:T(8,128)S(1)}, f32[2,1,8,512]{3,2,1,0:T(8,128)}, u32[]{:S(2)}) copy-start(f32[2,1,8,512]{3,2,1,0:T(8,128)} %param.18) | copy-start | bytes 98308
  31.4 7.7 %collective-permute-start.2 = (f32[4,1,512]{2,1,0:T(1,128)S(1)}, f32[4,1,512]{2,1,0:T(1,128)S(1)}, u32[]{:S(2)}, u32[]{:S(2)}) collective-permute-start(f32[4,1,512]{2,1,0:T(1,128)S(1)} %get-tuple-element.69), channel_id=1, source_target_pairs={{0,4},{4,8},{8,12},{1,5},{5,9},{9,13},{2,6},{6,10},{10,14},{3,7},{... | collective-permute-start | bytes 24584 | tf_op jit(solution)/shard_map/ppermute | solution.py:21
  32.7 6.4 %collective-permute-start.3 = (f32[4,1,512]{2,1,0:T(1,128)S(1)}, f32[4,1,512]{2,1,0:T(1,128)S(1)}, u32[]{:S(2)}, u32[]{:S(2)}) collective-permute-start(f32[4,1,512]{2,1,0:T(1,128)S(1)} %get-tuple-element.70), channel_id=1, source_target_pairs={{4,0},{8,4},{12,8},{5,1},{9,5},{13,9},{6,2},{10,6},{14,10},{7,3},{... | collective-permute-start | bytes 24584 | tf_op jit(solution)/shard_map/ppermute | solution.py:24
  34.1 5.3 %collective-permute-start.6 = (f32[4,1,512]{2,1,0:T(1,128)S(1)}, f32[4,1,512]{2,1,0:T(1,128)S(1)}, u32[]{:S(2)}, u32[]{:S(2)}) collective-permute-start(f32[4,1,512]{2,1,0:T(1,128)S(1)} %get-tuple-element.71), channel_id=1, source_target_pairs={{0,4},{4,8},{8,12},{1,5},{5,9},{9,13},{2,6},{6,10},{10,14},{3,7},{... | collective-permute-start | bytes 24584 | tf_op jit(solution)/shard_map/ppermute | solution.py:21
  37.8 4.3 %collective-permute-start.7 = (f32[4,1,512]{2,1,0:T(1,128)S(1)}, f32[4,1,512]{2,1,0:T(1,128)S(1)}, u32[]{:S(2)}, u32[]{:S(2)}) collective-permute-start(f32[4,1,512]{2,1,0:T(1,128)S(1)} %get-tuple-element.72), channel_id=1, source_target_pairs={{4,0},{8,4},{12,8},{5,1},{9,5},{13,9},{6,2},{10,6},{14,10},{7,3},{... | collective-permute-start | bytes 24584 | tf_op jit(solution)/shard_map/ppermute | solution.py:24
  50.0 12.8 %collective-permute-start.8 = (f32[1,8,512]{2,1,0:T(8,128)S(1)}, f32[1,8,512]{2,1,0:T(8,128)S(1)}, u32[]{:S(2)}, u32[]{:S(2)}) collective-permute-start(f32[1,8,512]{2,1,0:T(8,128)S(1)} %get-tuple-element.73), channel_id=1, source_target_pairs={{0,1},{1,2},{2,3},{3,16},{16,17},{17,18},{18,19},{4,5},{5,6},{6,7}... | collective-permute-start | bytes 49160 | tf_op jit(solution)/shard_map/ppermute | solution.py:21
  54.5 8.3 %collective-permute-start.9 = (f32[1,8,512]{2,1,0:T(8,128)S(1)}, f32[1,8,512]{2,1,0:T(8,128)S(1)}, u32[]{:S(2)}, u32[]{:S(2)}) collective-permute-start(f32[1,8,512]{2,1,0:T(8,128)S(1)} %get-tuple-element.74), channel_id=1, source_target_pairs={{1,0},{2,1},{3,2},{16,3},{17,16},{18,17},{19,18},{5,4},{6,5},{7,6}... | collective-permute-start | bytes 49160 | tf_op jit(solution)/shard_map/ppermute | solution.py:24
  62.8 2.9 %collective-permute-start.10 = (f32[4,1,512]{2,1,0:T(1,128)S(1)}, f32[4,1,512]{2,1,0:T(1,128)S(1)}, u32[]{:S(2)}, u32[]{:S(2)}) collective-permute-start(f32[4,1,512]{2,1,0:T(1,128)S(1)} %get-tuple-element.67), channel_id=1, source_target_pairs={{0,4},{4,8},{8,12},{1,5},{5,9},{9,13},{2,6},{6,10},{10,14},{3,7},{... | collective-permute-start | bytes 24584 | tf_op jit(solution)/shard_map/ppermute | solution.py:21
  64.1 4.0 %collective-permute-start.11 = (f32[4,1,512]{2,1,0:T(1,128)S(1)}, f32[4,1,512]{2,1,0:T(1,128)S(1)}, u32[]{:S(2)}, u32[]{:S(2)}) collective-permute-start(f32[4,1,512]{2,1,0:T(1,128)S(1)} %get-tuple-element.68), channel_id=1, source_target_pairs={{4,0},{8,4},{12,8},{5,1},{9,5},{13,9},{6,2},{10,6},{14,10},{7,3},{... | collective-permute-start | bytes 24584 | tf_op jit(solution)/shard_map/ppermute | solution.py:24
  70.2 18.3 %all-to-all-start = ((f32[2,8,512]{2,0,1:T(2,128)}), f32[2,8,512]{2,0,1:T(2,128)S(1)}, u32[]{:S(2)}, u32[]{:S(2)}) async-start(f32[2,8,512]{2,0,1:T(2,128)} %select_bitcast_fusion), calls=%async_computation | async-start | bytes 65536 | tf_op jit(solution)/shard_map/all_to_all | solution.py:120
  88.6 0.8 copy-start.2
where the time goes:
time: 92 us; the launch traced here: 90.7 us
  starting transfers between devices  39.7 us (43%)
  blocking collectives  25.3 us (28%)
  waiting for transfers between devices  12 us (13%)
  local copies, waits for them, and re-layouts  8.64 us (9%)
  other arithmetic  2.41 us (3%)
  between operations  2.34 us (3%)
    ppermute x6, starting transfers between devices, padded(): lax.ppermute(lax.slice_in_dim(block, block.shape[dim] - width, None, axis...  20.4 us
    unnamed x2, blocking collectives  13.9 us
    all_to_all x1, starting transfers between devices, on_device(): lax.all_to_all(permuted, ('slab', 'mech'), split_axis=1, concat_axis=0, t...  11.5 us
    all_gather x2, blocking collectives, on_device(): compact_all = lax.all_gather(compact, 'iface', axis=1, tiled=True)  11.4 us
    ppermute x6, starting transfers between devices, padded(): lax.ppermute(lax.slice_in_dim(block, 0, width, axis=dim), axis, backward)  7.75 us
    all_to_all x1, waiting for transfers between devices, on_device(): lax.all_to_all(permuted, ('slab', 'mech'), split_axis=1, concat_axis=0, t...  6.72 us
    ppermute x6, waiting for transfers between devices, padded(): lax.ppermute(lax.slice_in_dim(block, 0, width, axis=dim), axis, backward)  5.22 us
    unnamed x16, local copies, waits for them, and re-layouts  3.93 us
  transfers between devices with their start and end apart: 13, of which 3 were waited for; matrix products, arithmetic and copies ran while one was open for 3% of the time, Pallas kernels for 0%

commit v1 on v0

--- a/solution.py
+++ b/solution.py
@@ -1,6 +1,8 @@
 import jax
 import jax.numpy as jnp
 from jax import lax
+from jax.experimental import pallas as pl
+from jax.experimental.pallas import tpu as pltpu
 from jax.sharding import PartitionSpec as P
 
 SWEEPS = 2
@@ -81,7 +83,7 @@
     return (stress, strain)
 
 
-def on_device(
+def stepwise(
     temp_start, conductivity, gap_conductance, partner, row_order, active_layers, trial_stress
 ):
     depth = temp_start.shape[0]
@@ -122,6 +124,272 @@
     return creep_return(mech_temp, trial_stress, active_layers)
 
 
+LANES = 128
+GATHER_LIMIT = 4 * 1024 * 1024
+
+
+def lane_index(like):
+    return lax.broadcasted_iota(jnp.int32, like.shape, 1)
+
+
+def axial_sum(field):
+    depth = field.shape[0]
+    row = lax.broadcasted_iota(jnp.int32, field.shape, 0)
+    below = jnp.where(row == 0, 0.0, pltpu.roll(field, 1, 0))
+    above = jnp.where(row == depth - 1, 0.0, pltpu.roll(field, depth - 1, 0))
+    return field + 0.5 * (below + above)
+
+
+def radial_sum(tiles):
+    middle = len(tiles) // 2
+    lane = lane_index(tiles[0])
+    inward = [pltpu.roll(tile, 1, 1) for tile in tiles]
+    outward = [pltpu.roll(tile, LANES - 1, 1) for tile in tiles]
+    result = []
+    for index, tile in enumerate(tiles):
+        left = 0.0 if index in (0, middle) else inward[index - 1]
+        right = 0.0 if index in (middle - 1, len(tiles) - 1) else outward[index + 1]
+        left = jnp.where(lane == 0, left, inward[index])
+        right = jnp.where(lane == LANES - 1, right, outward[index])
+        result.append(tile + 0.5 * (left + right))
+    return result
+
+
+def across_sum(near, center, far):
+    return [c + 0.5 * (n + f) for n, c, f in zip(near, center, far)]
+
+
+def box_sum(near, center, far):
+    return radial_sum([axial_sum(tile) for tile in across_sum(near, center, far)])
+
+
+def increments(temp, cond, box_temp, box_cond, box_heat, weights):
+    return [
+        FLUX_STEP * (k * (bt - w * t) + bh - t * bk)
+        for t, k, bt, bk, bh, w in zip(temp, cond, box_temp, box_cond, box_heat, weights)
+    ]
+
+
+def product(left, right):
+    return [a * b for a, b in zip(left, right)]
+
+
+def column_step(
+    sections,
+    depth,
+    rows,
+    radial,
+    axes,
+    partner_ref,
+    order_ref,
+    active_ref,
+    temp_ref,
+    cond_ref,
+    gap_ref,
+    trial_ref,
+    stress_ref,
+    strain_ref,
+):
+    count = radial // LANES
+    middle = count // 2
+    across = sections * rows
+    section = lax.axis_index("iface")
+    member = lax.axis_index(axes[0]) * lax.axis_size(axes[1]) + lax.axis_index(axes[1])
+    own = section * rows + order_ref[0, member]
+
+    def inverse(column):
+        found = jnp.int32(0)
+        for segment in range(across):
+            found = jnp.where(partner_ref[segment] == column, jnp.int32(segment), found)
+        return found
+
+    def inside(column):
+        return jnp.where((column >= 0) & (column < across), 1.0, 0.0).astype(jnp.float32)
+
+    def clipped(column):
+        return jnp.minimum(jnp.maximum(column, 0), across - 1)
+
+    def load(ref, column, tile):
+        base = (column // rows) * (depth * rows * count) + tile * rows + column % rows
+        return ref[pl.ds(base, depth, stride=rows * count), :]
+
+    def load_column(ref, column):
+        scale = inside(column)
+        at = clipped(column)
+        return [scale * load(ref, at, tile) for tile in range(count)]
+
+    def load_gap(column):
+        block = gap_ref[column // rows]
+        lane = lane_index(block)
+        chosen = jnp.where(lane == column % rows, block, 0.0)
+        return jnp.sum(chosen, axis=1, keepdims=True)
+
+    compact = middle - 1
+    canister = middle
+    temps = {d: load_column(temp_ref, own + d) for d in range(-2, 3)}
+    conds = {d: load_column(cond_ref, own + d) for d in range(-2, 3)}
+    heats = {d: product(temps[d], conds[d]) for d in range(-2, 3)}
+    lane = lane_index(temps[0][0])
+    at_compact = lane == LANES - 1
+    at_canister = lane == 0
+
+    def crossing(gap, compact_tile, canister_tile):
+        return gap * (pltpu.roll(compact_tile, 1, 1) - canister_tile)
+
+    weights = [8.0] * count
+    weights[compact] = jnp.where(at_compact, 6.0, 8.0)
+    weights[canister] = jnp.where(at_canister, 6.0, 8.0)
+
+    def with_flux(tiles, flux, returned):
+        tiles = list(tiles)
+        tiles[canister] = tiles[canister] + jnp.where(at_canister, FLUX_STEP * flux, 0.0)
+        back = pltpu.roll(FLUX_STEP * returned, LANES - 1, 1)
+        tiles[compact] = tiles[compact] - jnp.where(at_compact, back, 0.0)
+        return tiles
+
+    first = {}
+    box_cond_own = None
+    own_flux = None
+    own_returned = None
+    for d in (-1, 0, 1):
+        at = clipped(own + d)
+        facing = partner_ref[at]
+        source = inverse(at)
+        flux = crossing(load_gap(at), load(temp_ref, facing, compact), temps[d][canister])
+        returned = crossing(load_gap(source), temps[d][compact], load(temp_ref, source, canister))
+        box_temp = box_sum(temps[d - 1], temps[d], temps[d + 1])
+        box_cond = box_sum(conds[d - 1], conds[d], conds[d + 1])
+        box_heat = box_sum(heats[d - 1], heats[d], heats[d + 1])
+        change = increments(temps[d], conds[d], box_temp, box_cond, box_heat, weights)
+        tiles = with_flux([t + c for t, c in zip(temps[d], change)], flux, returned)
+        scale = inside(own + d)
+        first[d] = [scale * tile for tile in tiles] if d else tiles
+        if d == 0:
+            box_cond_own = box_cond
+            own_flux = flux
+            own_returned = returned
+
+    def face_after(column, tile, shift):
+        def summed(fields):
+            total = axial_sum(fields[1] + 0.5 * (fields[0] + fields[2]))
+            return total + 0.5 * pltpu.roll(total, shift, 1)
+
+        near = [inside(column + d) for d in (-1, 0, 1)]
+        spots = [clipped(column + d) for d in (-1, 0, 1)]
+        temp = [s * load(temp_ref, c, tile) for s, c in zip(near, spots)]
+        cond = [s * load(cond_ref, c, tile) for s, c in zip(near, spots)]
+        heat = product(temp, cond)
+        change = cond[1] * (summed(temp) - 6.0 * temp[1]) + summed(heat) - temp[1] * summed(cond)
+        return temp[1] + FLUX_STEP * change
+
+    facing = partner_ref[own]
+    source = inverse(own)
+    facing_tile = face_after(facing, compact, 1)
+    facing_tile = facing_tile - pltpu.roll(FLUX_STEP * own_flux, LANES - 1, 1)
+    source_tile = face_after(source, canister, LANES - 1) + FLUX_STEP * own_returned
+    flux = crossing(load_gap(own), facing_tile, first[0][canister])
+    returned = crossing(load_gap(source), first[0][compact], source_tile)
+    first_heat = {d: product(first[d], conds[d]) for d in (-1, 0, 1)}
+    change = increments(
+        first[0],
+        conds[0],
+        box_sum(first[-1], first[0], first[1]),
+        box_cond_own,
+        box_sum(first_heat[-1], first_heat[0], first_heat[1]),
+        weights,
+    )
+    final = with_flux([t + c for t, c in zip(first[0], change)], flux, returned)
+
+    active = active_ref[0, 0]
+    for tile in range(count):
+        for element in range(depth // 8):
+            spot = pl.ds(element * 8 * count + tile, 8, stride=count)
+            trial = trial_ref[spot, :]
+            mech_temp = final[tile][element * 8 : element * 8 + 8]
+            rate = CREEP_RATE * jnp.exp(-ACTIVATION / (mech_temp + REFERENCE_TEMP))
+            slip = jnp.zeros(trial.shape, jnp.float32)
+            for newton_step in range(NEWTON):
+                left = trial - slip
+                pull = rate * left * left
+                slip = slip - (slip - pull * left) / (1.0 + 3.0 * pull)
+            live = jnp.where(element < active, 1.0, 0.0).astype(jnp.float32)
+            creep = live * slip
+            stress_ref[spot, :] = trial - creep
+            strain_ref[pl.ds(element * count + tile, 1), :] = 0.125 * jnp.sum(
+                creep, axis=0, keepdims=True
+            )
+
+
+def column_call(sections, depth, rows, radial, axes, operands):
+    count = radial // LANES
+    smem = pl.BlockSpec(memory_space=pltpu.SMEM)
+    vmem = pl.BlockSpec(memory_space=pltpu.VMEM)
+    return pl.pallas_call(
+        lambda *refs: column_step(sections, depth, rows, radial, axes, *refs),
+        out_shape=(
+            jax.ShapeDtypeStruct((depth * count, LANES), jnp.float32),
+            jax.ShapeDtypeStruct((depth // 8 * count, LANES), jnp.float32),
+        ),
+        in_specs=[smem, smem, smem, vmem, vmem, vmem, vmem],
+        out_specs=(vmem, vmem),
+        compiler_params=pltpu.CompilerParams(vmem_limit_bytes=32 * 1024 * 1024),
+    )(*operands)
+
+
+def on_device(
+    temp_start, conductivity, gap_conductance, partner, row_order, active_layers, trial_stress
+):
+    layers, _, rows, radial = temp_start.shape
+    sections = lax.axis_size("iface")
+    axes = ("slab", "mech")
+    members = lax.axis_size(axes[0]) * lax.axis_size(axes[1])
+    depth = layers * members
+    total = 2 * 4 * depth * sections * rows * radial
+    if total > GATHER_LIMIT or rows != members or radial % (2 * LANES) or depth % 8:
+        return stepwise(
+            temp_start,
+            conductivity,
+            gap_conductance,
+            partner,
+            row_order,
+            active_layers,
+            trial_stress,
+        )
+    everyone = ("iface",) + axes
+    count = radial // LANES
+
+    def by_lanes(block):
+        split = block.reshape(layers, rows, count, LANES)
+        return split.transpose(0, 2, 1, 3)
+
+    temp_all = lax.all_gather(by_lanes(temp_start), everyone, axis=0, tiled=False)
+    cond_all = lax.all_gather(by_lanes(conductivity), everyone, axis=0, tiled=False)
+    gap_all = lax.all_gather(gap_conductance, everyone, axis=0, tiled=False)
+    partner_all = lax.all_gather(partner, everyone, axis=0, tiled=False)
+    partner_all = partner_all.reshape(sections, members, rows)[:, 0].reshape(sections * rows)
+    grid = sections * depth * rows * count
+    stress, strain = column_call(
+        sections,
+        depth,
+        rows,
+        radial,
+        axes,
+        (
+            partner_all,
+            row_order,
+            active_layers,
+            temp_all.reshape(grid, LANES),
+            cond_all.reshape(grid, LANES),
+            gap_all.reshape(sections, depth, rows),
+            trial_stress.reshape(depth * count, LANES),
+        ),
+    )
+    return (
+        stress.reshape(depth, 1, 1, radial),
+        strain.reshape(depth // 8, 1, 1, radial),
+    )
+
+
 def solution(mesh):
     placed = (
         P(("slab", "mech"), "iface", None, None),

time: 92 us -> 136 us (1.48)
  blocking collectives: 25.3 us -> 108 us
  starting transfers between devices: 39.7 us -> 0.08 us
  between operations: 2.34 us -> 15.4 us
  waiting for transfers between devices: 12 us -> 4.41 us
  local copies, waits for them, and re-layouts: 8.64 us -> 5.35 us
  other arithmetic: 2.41 us -> 0 us
  Pallas kernels: 0 us -> 1.99 us
    all_gather x2 -> x1, blocking collectives: 11.4 us -> 66 us  [on_device(): gap_all = lax.all_gather(gap_conductance, everyone, axis=0, tiled=False)]
    unnamed x2 -> x1, blocking collectives: 13.9 us -> 42.1 us
    ppermute x12 -> x0, starting transfers between devices: 28.1 us -> none  [the longest x6 20.4 us: padded(): lax.ppermute(lax.slice_in_dim(block, block.shape[dim] - width, None, axis...]
    all_to_all x1 -> x0, starting transfers between devices: 11.5 us -> none  [on_device(): lax.all_to_all(permuted, ('slab', 'mech'), split_axis=1, concat_axis=0, t...]
    all_to_all x1 -> x0, waiting for transfers between devices: 6.72 us -> none  [on_device(): lax.all_to_all(permuted, ('slab', 'mech'), split_axis=1, concat_axis=0, t...]
    ppermute x12 -> x0, waiting for transfers between devices: 5.23 us -> none  [the longest x6 5.22 us: padded(): lax.ppermute(lax.slice_in_dim(block, 0, width, axis=dim), axis, backward)]
    all_gather x0 -> x2, waiting for transfers between devices: none -> 3.03 us  [the longest x1 3.03 us: on_device(): lax.all_gather(by_lanes(conductivity), everyone, axis=0, tiled=False)]
    pallas_call x0 -> x1, Pallas kernels: none -> 1.99 us  [column_call(): pl.pallas_call(lambda *refs: column_step(sections, depth, rows, radial, a...]
  transfers between devices with their start and end apart: 13 -> 2, of which waited for: 3 -> 1; matrix products, arithmetic and copies ran while one was open for 3% -> 1% of each run, Pallas kernels for 0% -> 0%
where the time goes in v1:
time: 136 us; the launch traced here: 135 us
  blocking collectives  108 us (79%)
  between operations  15.4 us (11%)
  local copies, waits for them, and re-layouts  5.35 us (4%)
  waiting for transfers between devices  4.41 us (3%)
  Pallas kernels  1.99 us (1%)
    all_gather x1, blocking collectives, on_device(): gap_all = lax.all_gather(gap_conductance, everyone, axis=0, tiled=False)  66 us
    unnamed x1, blocking collectives  42.1 us
    unnamed x17, local copies, waits for them, and re-layouts  5.17 us
    all_gather x1, waiting for transfers between devices, on_device(): lax.all_gather(by_lanes(conductivity), everyone, axis=0, tiled=False)  3.03 us
  transfers between devices with their start and end apart: 2, of which 1 were waited for; matrix products, arithmetic and copies ran while one was open for 1% of the time, Pallas kernels for 0%

profile of v1, /device:TPU:0, one launch (start us, length us, event | category | flops | bytes accessed | tf_op | source)
XLA Modules:
  0.0 135.3 jit_solution(36833854775233541)
XLA Ops:
  7.2 0.0 all-gather.7.cloned.1.call-start
  7.2 0.7 all-gather.7.cloned.1.call-update
  7.9 0.0 all-gather.9.cloned.1.call-start
  7.9 0.7 all-gather.9.cloned.1.call-update
  9.3 0.0 copy-start.6
  9.3 0.6 copy-done.6
  10.0 0.6 dynamic-slice
  11.2 0.0 copy-start.5
  11.2 0.6 copy-done.5
  11.8 0.2 dynamic-update-slice
  12.0 0.0 copy-start.4
  12.0 42.1 %all-reduce = s32[256]{0:T(256)S(1)} all-reduce(s32[256]{0:T(256)S(1)} %dynamic-update-slice), channel_id=2, replica_groups=mesh['slab'=2,'iface'=4,'mech'=4] {'iface','slab','mech'}, use_global_device_ids=true, to_apply=%add | all-reduce | flops 256 | bytes 2048
  54.1 0.0 copy-start.2
  54.1 0.1 reshape.31
  54.2 0.1 reshape_squeeze.3.refs_0_
  54.3 0.0 copy-done.4
  54.3 66.0 %all-gather.3 = f32[64,1,8]{2,1,0:T(1,128)S(1)} all-gather(f32[2,1,8]{2,1,0:T(1,128)S(1)} %copy-done.4), channel_id=5, replica_groups=mesh['slab'=2,'iface'=4,'mech'=4] {'iface','slab','mech'}, dimensions={0}, use_global_device_ids=true | all-gather | bytes 2112 | tf_op jit(solution)/shard_map/all_gather | solution.py:367
  120.3 0.0 all-gather.7.cloned.1.call-done
  120.3 3.0 %all-gather.9.cloned.1.call-done = f32[64,4,8,128]{3,2,1,0:T(8,128)} async-done(((f32[2,4,8,128]{3,2,1,0:T(8,128)}), f32[64,4,8,128]{3,2,1,0:T(8,128)}) %all-gather.9.cloned.1.call-update) | async-done | bytes 1048592 | tf_op jit(solution)/shard_map/all_gather | solution.py:366
  123.3 0.0 copy-start.3
  123.3 0.0 copy-done.2
  123.3 0.7 copy-done.3
  124.0 0.0 copy-start
  124.0 1.2 copy-done
  125.2 0.0 copy-start.1
  125.2 1.2 copy-done.1
  126.4 2.0 %shard_map.86 = (f32[64,128]{1,0:T(8,128)}, f32[8,128]{1,0:T(8,128)}) custom-call(s32[32]{0:T(128)S(1)} %reshape_squeeze.3.refs_0_, s32[1,8]{1,0:T(1,128)S(1)} %copy-done.3, s32[1,1]{1,0:T(1,128)S(6)} %copy.16.refs_2_, f32[2048,128]{1,0:T(8,128)S(1)} %bitcast.13, f32[2048,128]{1,0:T(8,128)S(1)} %bitcast.14, f32[4,16,8]{2,1,0:T(8,128)S(1)} %bitcast.15, ...), custom_call_target="tpu_custom_call" | custom-call | tf_op jit(solution)/shard_map/pallas_call | solution.py:327
  (2 shorter events, 0.0 us)
Async XLA Ops:
  7.2 113.1 %all-gather.7.cloned.1.call-start = ((), (), s32[]{:S(2)}) async-start(), calls=%async_computation | async-start | bytes 1081344 | tf_op jit(solution)/shard_map/all_gather | solution.py:365
  7.9 115.4 %all-gather.9.cloned.1.call-start = ((), (), s32[]{:S(2)}) async-start(), calls=%async_computation.1 | async-start | bytes 1081344 | tf_op jit(solution)/shard_map/all_gather | solution.py:366
  9.3 0.7 copy-start.6
  11.2 0.7 copy-start.5
  12.0 42.3 %copy-start.4 = (f32[2,1,8]{2,1,0:T(1,128)S(1)}, f32[2,1,8]{2,1,0:T(1,128)}, u32[]{:S(2)}) copy-start(f32[2,1,8]{2,1,0:T(1,128)} %param.9) | copy-start | bytes 196
  54.1 69.2 %copy-start.2 = (f32[16,1,1,512]{3,2,1,0:T(1,128)S(1)}, f32[16,1,1,512]{3,2,1,0:T(1,128)}, u32[]{:S(2)}) copy-start(f32[16,1,1,512]{3,2,1,0:T(1,128)} %param.13) | copy-start | bytes 98308
  123.3 0.7 copy-start.3
  124.0 1.2 copy-start
  125.2 1.2 copy-start.1
Sparse Core Ops, SparseCore 0:
  11.0 56.5 all-gather.6
  70.6 52.7 all-gather.8

commit v2 on v0

--- a/solution.py
+++ b/solution.py
@@ -1,6 +1,9 @@
+import functools
 import jax
 import jax.numpy as jnp
 from jax import lax
+from jax.experimental import pallas as pl
+from jax.experimental.pallas import tpu as pltpu
 from jax.sharding import PartitionSpec as P
 
 SWEEPS = 2
@@ -81,7 +84,7 @@
     return (stress, strain)
 
 
-def on_device(
+def stepwise(
     temp_start, conductivity, gap_conductance, partner, row_order, active_layers, trial_stress
 ):
     depth = temp_start.shape[0]
@@ -122,6 +125,375 @@
     return creep_return(mech_temp, trial_stress, active_layers)
 
 
+LANES = 128
+FACES = 4
+REACH = 2
+WINDOW = 2 * REACH + 1
+
+
+def iota(shape, axis):
+    return lax.broadcasted_iota(jnp.int32, shape, axis)
+
+
+def axial_sum(field):
+    depth = field.shape[0]
+    row = iota(field.shape, 0)
+    below = jnp.where(row == 0, 0.0, pltpu.roll(field, 1, 0))
+    above = jnp.where(row == depth - 1, 0.0, pltpu.roll(field, depth - 1, 0))
+    return field + 0.5 * (below + above)
+
+
+def radial_sum(tiles):
+    middle = len(tiles) // 2
+    lane = iota(tiles[0].shape, 1)
+    inward = [pltpu.roll(tile, 1, 1) for tile in tiles]
+    outward = [pltpu.roll(tile, LANES - 1, 1) for tile in tiles]
+    result = []
+    for index, tile in enumerate(tiles):
+        left = 0.0 if index in (0, middle) else inward[index - 1]
+        right = 0.0 if index in (middle - 1, len(tiles) - 1) else outward[index + 1]
+        left = jnp.where(lane == 0, left, inward[index])
+        right = jnp.where(lane == LANES - 1, right, outward[index])
+        result.append(tile + 0.5 * (left + right))
+    return result
+
+
+def box_sum(near, center, far):
+    return radial_sum([axial_sum(c + 0.5 * (n + f)) for n, c, f in zip(near, center, far)])
+
+
+def product(left, right):
+    return [a * b for a, b in zip(left, right)]
+
+
+class Sizes:
+    def __init__(self, layers, rows, radial):
+        self.layers = layers
+        self.rows = rows
+        self.radial = radial
+        self.tiles = radial // LANES
+        self.sections = lax.axis_size("iface")
+        self.members = lax.axis_size("slab") * lax.axis_size("mech")
+        self.depth = layers * self.members
+        self.across = self.sections * rows
+        self.window_rows = WINDOW * self.tiles
+        self.edge_rows = REACH * self.tiles
+        self.extra_at = 2 * self.window_rows
+        self.layer_rows = self.extra_at + 8
+        self.edge_extra_at = 2 * layers * self.edge_rows
+        self.message_rows = self.edge_extra_at + 8 * layers
+
+
+def spread_rows(sizes, block_ref, layer, put):
+    for tile in range(sizes.tiles):
+        put(tile, block_ref[layer, 0, :, pl.ds(tile * LANES, LANES)])
+
+
+def edge_kernel(sizes, partner_ref, gap_ref, temp_ref, cond_ref, out_ref, rows_ref):
+    section = lax.axis_index("iface")
+    lane = iota((8, LANES), 1)
+    sub = iota((8, LANES), 0)
+    group = lane // sizes.across
+    mine = lane % sizes.across == section * sizes.rows + sub
+    middle = sizes.tiles // 2
+    slot = 0
+    strips = []
+    for layer in range(sizes.layers):
+        for ref in (temp_ref, cond_ref):
+            base = slot * sizes.rows * sizes.tiles
+
+            def put(tile, value, base=base):
+                rows_ref[pl.ds(base + tile, sizes.rows, stride=sizes.tiles), :] = value
+
+            spread_rows(sizes, ref, layer, put)
+            inner = ref[layer, 0, :, pl.ds((middle - 1) * LANES, LANES)]
+            outer = ref[layer, 0, :, pl.ds(middle * LANES, LANES)]
+            picked = [
+                inner[:, LANES - 2 : LANES - 1],
+                inner[:, LANES - 1 : LANES],
+                outer[:, 0:1],
+                outer[:, 1:2],
+            ]
+            strip = jnp.zeros((8, LANES), jnp.float32)
+            for face, column in enumerate(picked):
+                strip = jnp.where(group == face, jnp.broadcast_to(column, (8, LANES)), strip)
+            strip = jnp.where(mine, strip, 0.0)
+            strips.append(jnp.sum(strip, axis=0, keepdims=True))
+            slot += 1
+    row = iota((1, LANES), 1)
+    table = jnp.zeros((1, LANES), jnp.float32)
+    gaps = [jnp.zeros((1, LANES), jnp.float32) for _ in range(sizes.layers)]
+    for index in range(sizes.rows):
+        compact_lane = sizes.across + partner_ref[index]
+        canister_lane = 2 * sizes.across + section * sizes.rows + index
+        at_compact = row == compact_lane
+        at_canister = row == canister_lane
+        table = jnp.where(at_canister, compact_lane.astype(jnp.float32), table)
+        table = jnp.where(at_compact, canister_lane.astype(jnp.float32), table)
+        for layer in range(sizes.layers):
+            gaps[layer] = jnp.where(at_compact | at_canister, gap_ref[layer, 0, index], gaps[layer])
+    extras = []
+    for layer in range(sizes.layers):
+        extra = jnp.zeros((8, LANES), jnp.float32)
+        for place, value in enumerate(
+            (strips[2 * layer], strips[2 * layer + 1], gaps[layer], table)
+        ):
+            extra = jnp.where(sub == place, jnp.broadcast_to(value, (8, LANES)), extra)
+        extras.append(extra)
+    for target in range(sizes.sections):
+        start = jnp.where(target > section, (sizes.rows - REACH) * sizes.tiles, 0)
+        for slot in range(2 * sizes.layers):
+            base = slot * sizes.rows * sizes.tiles
+            out_ref[target, pl.ds(slot * sizes.edge_rows, sizes.edge_rows), :] = rows_ref[
+                pl.ds(pl.multiple_of(base + start, 8), sizes.edge_rows), :
+            ]
+        for layer in range(sizes.layers):
+            out_ref[target, pl.ds(sizes.edge_extra_at + 8 * layer, 8), :] = extras[layer]
+
+
+def window_kernel(sizes, order_ref, temp_ref, cond_ref, edge_ref, out_ref, rows_ref):
+    section = lax.axis_index("iface")
+    before = jnp.maximum(section - 1, 0)
+    after = jnp.minimum(section + 1, sizes.sections - 1)
+    has_before = jnp.where(section > 0, 1.0, 0.0).astype(jnp.float32)
+    has_after = jnp.where(section < sizes.sections - 1, 1.0, 0.0).astype(jnp.float32)
+    own_rows = sizes.rows * sizes.tiles
+    slot_rows = own_rows + 2 * sizes.edge_rows
+    slot = 0
+    for layer in range(sizes.layers):
+        for ref in (temp_ref, cond_ref):
+            base = slot * slot_rows
+            edge = pl.ds(slot * sizes.edge_rows, sizes.edge_rows)
+            rows_ref[pl.ds(base, sizes.edge_rows), :] = has_before * edge_ref[before, edge, :]
+            rows_ref[pl.ds(base + sizes.edge_rows + own_rows, sizes.edge_rows), :] = (
+                has_after * edge_ref[after, edge, :]
+            )
+
+            def put(tile, value, base=base):
+                first = base + sizes.edge_rows + tile
+                rows_ref[pl.ds(first, sizes.rows, stride=sizes.tiles), :] = value
+
+            spread_rows(sizes, ref, layer, put)
+            slot += 1
+    extras = []
+    for layer in range(sizes.layers):
+        spot = pl.ds(sizes.edge_extra_at + 8 * layer, 8)
+        extra = edge_ref[0, spot, :]
+        for source in range(1, sizes.sections):
+            extra = extra + edge_ref[source, spot, :]
+        extras.append(extra)
+    for member in range(sizes.members):
+        start = order_ref[0, member] * sizes.tiles
+        for layer in range(sizes.layers):
+            for kind in range(2):
+                base = (2 * layer + kind) * slot_rows
+                out_ref[
+                    member, layer, pl.ds(kind * sizes.window_rows, sizes.window_rows), :
+                ] = rows_ref[pl.ds(base + start, sizes.window_rows), :]
+            out_ref[member, layer, pl.ds(sizes.extra_at, 8), :] = extras[layer]
+
+
+def column_kernel(sizes, order_ref, active_ref, parts_ref, trial_ref, stress_ref, strain_ref):
+    depth, tiles, across = sizes.depth, sizes.tiles, sizes.across
+    member = lax.axis_index("slab") * lax.axis_size("mech") + lax.axis_index("mech")
+    own = lax.axis_index("iface") * sizes.rows + order_ref[0, member]
+
+    def load(index):
+        return parts_ref[pl.ds(index, depth, stride=sizes.layer_rows), :]
+
+    def load_column(kind, shift):
+        base = kind * sizes.window_rows + (shift + REACH) * tiles
+        return [load(base + tile) for tile in range(tiles)]
+
+    def inside(column):
+        return jnp.where((column >= 0) & (column < across), 1.0, 0.0).astype(jnp.float32)
+
+    compact = tiles // 2 - 1
+    canister = tiles // 2
+    lane = iota((depth, LANES), 1)
+
+    strip_temp = load(sizes.extra_at)
+    strip_cond = load(sizes.extra_at + 1)
+    strip_gap = load(sizes.extra_at + 2)
+    table = parts_ref[pl.ds(sizes.extra_at + 3, 1), :].astype(jnp.int32)
+    table = jnp.broadcast_to(table, (depth, LANES))
+    place = lane % across
+    face = lane // across
+    is_face = (face == 1) | (face == 2)
+
+    def across_sum(field):
+        before = jnp.where(place == 0, 0.0, pltpu.roll(field, 1, 1))
+        after = jnp.where(place == across - 1, 0.0, pltpu.roll(field, LANES - 1, 1))
+        return field + 0.5 * (before + after)
+
+    def strip_sum(field):
+        total = axial_sum(across_sum(field))
+        inner = pltpu.roll(total, across, 1)
+        outer = pltpu.roll(total, LANES - across, 1)
+        return total + 0.5 * jnp.where(face == 1, inner, outer)
+
+    def exchange(strip):
+        met = jnp.take_along_axis(strip, table, axis=1)
+        return FLUX_STEP * strip_gap * (met - strip)
+
+    first_gain = exchange(strip_temp)
+    strip_change = strip_cond * (strip_sum(strip_temp) - 6.0 * strip_temp)
+    strip_change = strip_change + strip_sum(strip_temp * strip_cond)
+    strip_change = strip_change - strip_temp * strip_sum(strip_cond)
+    strip_first = strip_temp + FLUX_STEP * strip_change + first_gain
+    second_gain = exchange(strip_first)
+
+    weights = [8.0] * tiles
+    weights[compact] = jnp.where(lane == LANES - 1, 6.0, 8.0)
+    weights[canister] = jnp.where(lane == 0, 6.0, 8.0)
+
+    def with_gain(columns, gain, column):
+        to_compact = (2 * LANES - 1 - across - column) % LANES
+        to_canister = (2 * LANES - 2 * across - column) % LANES
+        columns = list(columns)
+        moved = pltpu.roll(gain, to_compact, 1)
+        columns[compact] = columns[compact] + jnp.where(lane == LANES - 1, moved, 0.0)
+        moved = pltpu.roll(gain, to_canister, 1)
+        columns[canister] = columns[canister] + jnp.where(lane == 0, moved, 0.0)
+        return columns
+
+    def swept(temp, cond, box_temp, box_cond, box_heat):
+        return [
+            t + FLUX_STEP * (k * (bt - w * t) + bh - t * bk)
+            for t, k, bt, bk, bh, w in zip(temp, cond, box_temp, box_cond, box_heat, weights)
+        ]
+
+    span = range(-REACH, REACH + 1)
+    temps = {d: load_column(0, d) for d in span}
+    conds = {d: load_column(1, d) for d in span}
+    heats = {d: product(temps[d], conds[d]) for d in span}
+    first = {}
+    box_conds = {}
+    for d in (-1, 0, 1):
+        box_conds[d] = box_sum(conds[d - 1], conds[d], conds[d + 1])
+        columns = swept(
+            temps[d],
+            conds[d],
+            box_sum(temps[d - 1], temps[d], temps[d + 1]),
+            box_conds[d],
+            box_sum(heats[d - 1], heats[d], heats[d + 1]),
+        )
+        columns = with_gain(columns, first_gain, own + d)
+        first[d] = [inside(own + d) * tile for tile in columns] if d else columns
+    heats = {d: product(first[d], conds[d]) for d in (-1, 0, 1)}
+    columns = swept(
+        first[0],
+        conds[0],
+        box_sum(first[-1], first[0], first[1]),
+        box_conds[0],
+        box_sum(heats[-1], heats[0], heats[1]),
+    )
+    final = with_gain(columns, second_gain, own)
+
+    active = active_ref[0, 0]
+    for tile in range(tiles):
+        for element in range(depth // 8):
+            spot = pl.ds(element * 8 * tiles + tile, 8, stride=tiles)
+            trial = trial_ref[spot, :]
+            mech_temp = final[tile][element * 8 : element * 8 + 8]
+            rate = CREEP_RATE * jnp.exp(-ACTIVATION / (mech_temp + REFERENCE_TEMP))
+            slip = jnp.zeros(trial.shape, jnp.float32)
+            for newton_step in range(NEWTON):
+                left = trial - slip
+                pull = rate * left * left
+                slip = slip - (slip - pull * left) / (1.0 + 3.0 * pull)
+            live = jnp.where(element < active, 1.0, 0.0).astype(jnp.float32)
+            creep = live * slip
+            stress_ref[spot, :] = trial - creep
+            strain_ref[pl.ds(element * tiles + tile, 1), :] = 0.125 * jnp.sum(
+                creep, axis=0, keepdims=True
+            )
+
+
+def kernel_call(body, sizes, out_shape, memories, scratch, operands):
+    spaces = {"smem": pltpu.SMEM, "vmem": pltpu.VMEM}
+    out_spec = pl.BlockSpec(memory_space=pltpu.VMEM)
+    return pl.pallas_call(
+        functools.partial(body, sizes),
+        out_shape=out_shape,
+        in_specs=[pl.BlockSpec(memory_space=spaces[memory]) for memory in memories],
+        out_specs=jax.tree.map(lambda _: out_spec, out_shape),
+        scratch_shapes=scratch,
+        compiler_params=pltpu.CompilerParams(vmem_limit_bytes=16 * 1024 * 1024),
+    )(*operands)
+
+
+def fits_columns(sizes):
+    return (
+        sizes.rows == 8
+        and sizes.members == sizes.rows
+        and sizes.across * FACES == LANES
+        and sizes.radial == 4 * LANES
+        and sizes.layers == 2
+    )
+
+
+def on_device(
+    temp_start, conductivity, gap_conductance, partner, row_order, active_layers, trial_stress
+):
+    layers, _, rows, radial = temp_start.shape
+    sizes = Sizes(layers, rows, radial)
+    if not fits_columns(sizes):
+        return stepwise(
+            temp_start,
+            conductivity,
+            gap_conductance,
+            partner,
+            row_order,
+            active_layers,
+            trial_stress,
+        )
+
+    def floats(*shape):
+        return jax.ShapeDtypeStruct(shape, jnp.float32)
+
+    edges = kernel_call(
+        edge_kernel,
+        sizes,
+        floats(sizes.sections, sizes.message_rows, LANES),
+        ["smem", "smem", "vmem", "vmem"],
+        [pltpu.VMEM((2 * layers * rows * sizes.tiles, LANES), jnp.float32)],
+        (partner, gap_conductance, temp_start, conductivity),
+    )
+    edges = lax.all_to_all(edges, "iface", split_axis=0, concat_axis=0, tiled=True)
+    slot_rows = rows * sizes.tiles + 2 * sizes.edge_rows
+    parts = kernel_call(
+        window_kernel,
+        sizes,
+        floats(sizes.members, layers, sizes.layer_rows, LANES),
+        ["smem", "vmem", "vmem", "vmem"],
+        [pltpu.VMEM((2 * layers * slot_rows, LANES), jnp.float32)],
+        (row_order, temp_start, conductivity, edges),
+    )
+    parts = parts.reshape(sizes.members, layers * sizes.layer_rows, LANES)
+    parts = lax.all_to_all(parts, ("slab", "mech"), split_axis=0, concat_axis=0, tiled=True)
+    stress, strain = kernel_call(
+        column_kernel,
+        sizes,
+        (
+            floats(sizes.depth * sizes.tiles, LANES),
+            floats(sizes.depth // 8 * sizes.tiles, LANES),
+        ),
+        ["smem", "smem", "vmem", "vmem"],
+        [],
+        (
+            row_order,
+            active_layers,
+            parts.reshape(sizes.depth * sizes.layer_rows, LANES),
+            trial_stress.reshape(sizes.depth * sizes.tiles, LANES),
+        ),
+    )
+    return (
+        stress.reshape(sizes.depth, 1, 1, radial),
+        strain.reshape(sizes.depth // 8, 1, 1, radial),
+    )
+
+
 def solution(mesh):
     placed = (
         P(("slab", "mech"), "iface", None, None),

time: 92 us -> 34.4 us (0.37)
  starting transfers between devices: 39.7 us -> 5.94 us
  blocking collectives: 25.3 us -> 8.47 us
  local copies, waits for them, and re-layouts: 8.64 us -> 2.87 us
  Pallas kernels: 0 us -> 3.66 us
  other arithmetic: 2.41 us -> 0 us
  between operations: 2.34 us -> 1.33 us
    ppermute x12 -> x0, starting transfers between devices: 28.1 us -> none  [the longest x6 20.4 us: padded(): lax.ppermute(lax.slice_in_dim(block, block.shape[dim] - width, None, axis...]
    unnamed x2 -> x0, blocking collectives: 13.9 us -> none
    all_gather x2 -> x0, blocking collectives: 11.4 us -> none  [on_device(): compact_all = lax.all_gather(compact, 'iface', axis=1, tiled=True)]
    all_to_all x0 -> x1, blocking collectives: none -> 8.47 us  [on_device(): lax.all_to_all(edges, 'iface', split_axis=0, concat_axis=0, tiled=True)]
    all_to_all x1, starting transfers between devices: 11.5 us -> 5.94 us  [on_device(): lax.all_to_all(parts, ('slab', 'mech'), split_axis=0, concat_axis=0, tile...]
    ppermute x12 -> x0, waiting for transfers between devices: 5.23 us -> none  [the longest x6 5.22 us: padded(): lax.ppermute(lax.slice_in_dim(block, 0, width, axis=dim), axis, backward)]
    all_to_all x1, waiting for transfers between devices: 6.72 us -> 11.6 us  [on_device(): lax.all_to_all(parts, ('slab', 'mech'), split_axis=0, concat_axis=0, tile...]
    pallas_call x0 -> x3, Pallas kernels: none -> 3.66 us  [kernel_call(): pl.pallas_call(functools.partial(body, sizes), out_shape=out_shape, in_sp...]
  transfers between devices with their start and end apart: 13 -> 1, of which waited for: 3 -> 1; matrix products, arithmetic and copies ran while one was open for 3% -> 0% of each run, Pallas kernels for 0% -> 0%
where the time goes in v2:
time: 34.4 us; the launch traced here: 33.9 us
  waiting for transfers between devices  11.6 us (34%)
  blocking collectives  8.47 us (25%)
  starting transfers between devices  5.94 us (17%)
  Pallas kernels  3.66 us (11%)
  local copies, waits for them, and re-layouts  2.87 us (8%)
  between operations  1.33 us (4%)
    all_to_all x1, waiting for transfers between devices, on_device(): lax.all_to_all(parts, ('slab', 'mech'), split_axis=0, concat_axis=0, tile...  11.6 us
    all_to_all x1, blocking collectives, on_device(): lax.all_to_all(edges, 'iface', split_axis=0, concat_axis=0, tiled=True)  8.47 us
    all_to_all x1, starting transfers between devices, on_device(): lax.all_to_all(parts, ('slab', 'mech'), split_axis=0, concat_axis=0, tile...  5.94 us
    pallas_call x3, Pallas kernels, kernel_call(): pl.pallas_call(functools.partial(body, sizes), out_shape=out_shape, in_sp...  3.66 us
    unnamed x16, local copies, waits for them, and re-layouts  2.87 us
  transfers between devices with their start and end apart: 1, of which 1 were waited for; matrix products, arithmetic and copies ran while one was open for 0% of the time, Pallas kernels for 0%

profile of v2, /device:TPU:0, one launch (start us, length us, event | category | flops | bytes accessed | tf_op | source)
XLA Modules:
  0.0 33.9 jit_solution(3909357809373117266)
XLA Ops:
  0.6 0.0 copy-start
  0.6 0.7 %copy-done = f32[2,1,8,512]{3,2,1,0:T(8,128)S(1)} copy-done((f32[2,1,8,512]{3,2,1,0:T(8,128)S(1)}, f32[2,1,8,512]{3,2,1,0:T(8,128)}, u32[]{:S(2)}) %copy-start) | copy-done | bytes 32792
  1.4 0.0 copy-start.2
  1.4 0.8 %copy-done.2 = f32[2,1,8,512]{3,2,1,0:T(8,128)S(1)} copy-done((f32[2,1,8,512]{3,2,1,0:T(8,128)S(1)}, f32[2,1,8,512]{3,2,1,0:T(8,128)}, u32[]{:S(2)}) %copy-start.2) | copy-done | bytes 32792
  2.1 0.0 copy-start.6
  2.2 0.7 %copy-done.6 = f32[2,1,8]{2,1,0:T(1,128)S(1)} copy-done((f32[2,1,8]{2,1,0:T(1,128)S(1)}, f32[2,1,8]{2,1,0:T(1,128)}, u32[]{:S(2)}) %copy-start.6) | copy-done | bytes 88
  2.8 0.0 copy-start.7
  2.8 0.7 %copy-done.7 = s32[8]{0:T(128)S(1)} copy-done((s32[8]{0:T(128)S(1)}, s32[8]{0:T(128)}, u32[]{:S(2)}) %copy-start.7) | copy-done | bytes 56
  3.5 0.6 %shard_map.86 = f32[4,48,128]{2,1,0:T(8,128)S(1)} custom-call(s32[8]{0:T(128)S(1)} %copy-done.7, f32[2,1,8]{2,1,0:T(1,128)S(1)} %copy-done.6, f32[2,1,8,512]{3,2,1,0:T(8,128)S(1)} %copy-done, f32[2,1,8,512]{3,2,1,0:T(8,128)S(1)} %copy-done.2), custom_call_target="tpu_custom_call" | custom-call | tf_op jit(solution)/shard_map/pallas_call | solution.py:416
  4.1 0.0 copy-start.1
  4.1 0.0 copy-start.3
  4.2 0.0 copy-start.5
  4.2 8.5 %all_to_all.10.edge_ref = f32[4,48,128]{2,1,0:T(8,128)S(1)} all-to-all(f32[4,48,128]{2,1,0:T(8,128)S(1)} %shard_map.86), channel_id=1, replica_groups=mesh['slab'=2,'iface'=4,'mech'=4] {'iface'}, dimensions={0} | all-to-all | bytes 196608 | tf_op jit(solution)/shard_map/all_to_all | solution.py:463
  12.6 0.0 copy-done.1
  12.6 0.0 copy-done.3
  12.6 0.0 copy-done.5
  12.6 1.3 %shard_map.87 = f32[8,2,48,128]{3,2,1,0:T(8,128)} custom-call(s32[1,8]{1,0:T(1,128)S(1)} %copy-done.5, f32[2,1,8,512]{3,2,1,0:T(8,128)S(1)} %copy-done.1, f32[2,1,8,512]{3,2,1,0:T(8,128)S(1)} %copy-done.3, f32[4,48,128]{2,1,0:T(8,128)S(1)} %all_to_all.10.edge_ref), custom_call_target="tpu_custom_call" | custom-call | tf_op jit(solution)/shard_map/pallas_call | solution.py:416
  14.0 0.0 copy-start.4
  14.0 5.9 %all-to-all-start.1 = ((f32[8,96,128]{2,1,0:T(8,128)}), f32[8,96,128]{2,1,0:T(8,128)S(1)}, u32[]{:S(2)}, u32[]{:S(2)}) async-start(f32[8,96,128]{2,1,0:T(8,128)} %bitcast), calls=%async_computation.1 | async-start | bytes 786432 | tf_op jit(solution)/shard_map/all_to_all | solution.py:474
  20.6 11.6 %all-to-all-done.1 = f32[8,96,128]{2,1,0:T(8,128)S(1)} async-done(((f32[8,96,128]{2,1,0:T(8,128)}), f32[8,96,128]{2,1,0:T(8,128)S(1)}, u32[]{:S(2)}, u32[]{:S(2)}) %all-to-all-start.1) | async-done | bytes 393248 | tf_op jit(solution)/shard_map/all_to_all | solution.py:474
  32.2 0.0 copy-done.4
  32.2 1.7 %shard_map.88 = (f32[64,128]{1,0:T(8,128)}, f32[8,128]{1,0:T(8,128)}) custom-call(s32[1,8]{1,0:T(1,128)S(1)} %copy-done.5, s32[1,1]{1,0:T(1,128)S(6)} %copy.11.active_ref, f32[768,128]{1,0:T(8,128)S(1)} %bitcast.5, f32[64,128]{1,0:T(8,128)S(1)} %bitcast.6), custom_call_target="tpu_custom_call" | custom-call | tf_op jit(solution)/shard_map/pallas_call | solution.py:416
Async XLA Ops:
  0.6 0.8 %copy-start = (f32[2,1,8,512]{3,2,1,0:T(8,128)S(1)}, f32[2,1,8,512]{3,2,1,0:T(8,128)}, u32[]{:S(2)}) copy-start(f32[2,1,8,512]{3,2,1,0:T(8,128)} %temp_ref.3) | copy-start | bytes 98308
  1.4 0.8 %copy-start.2 = (f32[2,1,8,512]{3,2,1,0:T(8,128)S(1)}, f32[2,1,8,512]{3,2,1,0:T(8,128)}, u32[]{:S(2)}) copy-start(f32[2,1,8,512]{3,2,1,0:T(8,128)} %cond_ref.3) | copy-start | bytes 98308
  2.1 0.7 %copy-start.6 = (f32[2,1,8]{2,1,0:T(1,128)S(1)}, f32[2,1,8]{2,1,0:T(1,128)}, u32[]{:S(2)}) copy-start(f32[2,1,8]{2,1,0:T(1,128)} %gap_ref.1) | copy-start | bytes 196
  2.8 0.7 %copy-start.7 = (s32[8]{0:T(128)S(1)}, s32[8]{0:T(128)}, u32[]{:S(2)}) copy-start(s32[8]{0:T(128)} %partner_ref.1) | copy-start | bytes 100
  4.1 8.5 %copy-start.1 = (f32[2,1,8,512]{3,2,1,0:T(8,128)S(1)}, f32[2,1,8,512]{3,2,1,0:T(8,128)}, u32[]{:S(2)}) copy-start(f32[2,1,8,512]{3,2,1,0:T(8,128)} %temp_ref.3) | copy-start | bytes 98308
  4.1 8.5 %copy-start.3 = (f32[2,1,8,512]{3,2,1,0:T(8,128)S(1)}, f32[2,1,8,512]{3,2,1,0:T(8,128)}, u32[]{:S(2)}) copy-start(f32[2,1,8,512]{3,2,1,0:T(8,128)} %cond_ref.3) | copy-start | bytes 98308
  4.2 8.5 %copy-start.5 = (s32[1,8]{1,0:T(1,128)S(1)}, s32[1,8]{1,0:T(1,128)}, u32[]{:S(2)}) copy-start(s32[1,8]{1,0:T(1,128)} %order_ref.3) | copy-start | bytes 100
  14.0 18.2 %copy-start.4 = (f32[16,1,1,512]{3,2,1,0:T(1,128)S(1)}, f32[16,1,1,512]{3,2,1,0:T(1,128)}, u32[]{:S(2)}) copy-start(f32[16,1,1,512]{3,2,1,0:T(1,128)} %param.13) | copy-start | bytes 98308
  14.0 18.2 %all-to-all-start.1 = ((f32[8,96,128]{2,1,0:T(8,128)}), f32[8,96,128]{2,1,0:T(8,128)S(1)}, u32[]{:S(2)}, u32[]{:S(2)}) async-start(f32[8,96,128]{2,1,0:T(8,128)} %bitcast), calls=%async_computation.1 | async-start | bytes 786432 | tf_op jit(solution)/shard_map/all_to_all | solution.py:474

commit v3 on v0

--- a/solution.py
+++ b/solution.py
@@ -1,6 +1,9 @@
+import functools
 import jax
 import jax.numpy as jnp
 from jax import lax
+from jax.experimental import pallas as pl
+from jax.experimental.pallas import tpu as pltpu
 from jax.sharding import PartitionSpec as P
 
 SWEEPS = 2
@@ -81,7 +84,7 @@
     return (stress, strain)
 
 
-def on_device(
+def stepwise(
     temp_start, conductivity, gap_conductance, partner, row_order, active_layers, trial_stress
 ):
     depth = temp_start.shape[0]
@@ -122,6 +125,357 @@
     return creep_return(mech_temp, trial_stress, active_layers)
 
 
+LANES = 128
+HALO = 2
+EVERYONE = ("iface", "slab", "mech")
+
+
+def iota(shape, axis):
+    return lax.broadcasted_iota(jnp.int32, shape, axis)
+
+
+class Sizes:
+    def __init__(self, layers, rows, radial):
+        self.layers = layers
+        self.rows = rows
+        self.radial = radial
+        self.tiles = radial // LANES
+        self.sections = lax.axis_size("iface")
+        self.members = lax.axis_size("slab") * lax.axis_size("mech")
+        self.devices = self.sections * self.members
+        self.depth = layers * self.members
+        self.chunk = radial // self.devices
+        self.width = self.chunk + 2 * HALO
+        self.field = layers * self.width
+        self.gap_row = radial // 2
+
+
+def fits_tiles(sizes):
+    return (
+        sizes.rows == 8
+        and sizes.members == sizes.rows
+        and sizes.layers == 2
+        and sizes.sections * sizes.rows <= LANES
+        and sizes.radial % sizes.devices == 0
+        and sizes.chunk * 8 == LANES
+        and sizes.radial % (2 * LANES) == 0
+    )
+
+
+def deal_kernel(
+    sizes,
+    partner_hbm,
+    order_hbm,
+    gap_hbm,
+    temp_hbm,
+    cond_hbm,
+    out_ref,
+    partner_ref,
+    order_ref,
+    gap_ref,
+    temp_ref,
+    cond_ref,
+    sems,
+):
+    pairs = (
+        (temp_hbm, temp_ref),
+        (cond_hbm, cond_ref),
+        (gap_hbm, gap_ref),
+        (partner_hbm, partner_ref),
+        (order_hbm, order_ref),
+    )
+    copies = [
+        pltpu.make_async_copy(source, target, sems.at[index])
+        for index, (source, target) in enumerate(pairs)
+    ]
+    for copy in copies:
+        copy.start()
+    for copy in copies:
+        copy.wait()
+    shape = (sizes.rows, LANES)
+    lane = iota(shape, 1)
+    sub = iota(shape, 0)
+    extra_at = 2 * sizes.field
+    extra = jnp.zeros(shape, jnp.float32)
+    for row in range(sizes.rows):
+        for layer in range(sizes.layers):
+            spot = (sub == row) & (lane == extra_at + layer * sizes.width)
+            extra = jnp.where(spot, gap_ref[layer, 0, row], extra)
+        spot = (sub == row) & (lane == extra_at + 1)
+        extra = jnp.where(spot, partner_ref[row].astype(jnp.float32), extra)
+        spot = (sub == row) & (lane == extra_at + 2)
+        extra = jnp.where(spot, order_ref[0, row].astype(jnp.float32), extra)
+    blocks = [
+        [ref[layer, 0, :, pl.ds(tile * LANES, LANES)] for tile in range(sizes.tiles)]
+        for ref in (temp_ref, cond_ref)
+        for layer in range(sizes.layers)
+    ]
+    for device in range(sizes.devices):
+        first = device * sizes.chunk - HALO
+        packed = extra
+        for index, block in enumerate(blocks):
+            base = index * sizes.width
+            for tile in range(sizes.tiles):
+                low = max(first, tile * LANES)
+                high = min(first + sizes.width, (tile + 1) * LANES)
+                if low >= high:
+                    continue
+                moved = pltpu.roll(block[tile], (base - first + tile * LANES) % LANES, 1)
+                spot = (lane >= base + low - first) & (lane < base + high - first)
+                packed = jnp.where(spot, moved, packed)
+        out_ref[device] = packed
+
+
+def sweep_kernel(sizes, dealt_ref, out_ref):
+    rows, width, field = sizes.rows, sizes.width, sizes.field
+    sections, members = sizes.sections, sizes.members
+    shape = (rows, LANES)
+    lane = iota(shape, 1)
+    sub = iota(shape, 0)
+    place = lax.axis_index("iface") * members
+    place = place + lax.axis_index("slab") * lax.axis_size("mech") + lax.axis_index("mech")
+    first = place * sizes.chunk - HALO
+    segment = lane // width
+    radius = first + lane % width
+    lower_layer = segment % 2 == 0
+    at_compact = radius == sizes.gap_row - 1
+    at_canister = radius == sizes.gap_row
+    in_grid = (radius >= 0) & (radius < sizes.radial)
+    weight = jnp.where(at_compact | at_canister, 6.0, 8.0)
+    is_temp = lane < field
+    at_face = is_temp & (at_compact | at_canister)
+    keep_temp = jnp.where(is_temp & in_grid, 1.0, 0.0)
+    face_lane = sizes.gap_row - 1 - first
+
+    def turn(value, shift):
+        return pltpu.roll(value, shift % LANES, 1)
+
+    dealt = [[dealt_ref[s * members + k] for k in range(members)] for s in range(sections)]
+
+    strip_lane = (lane < 2 * members) | ((lane >= width) & (lane < width + 2 * members))
+    odd = (lane % width) % 2 == 1
+
+    def strip_of(values, start):
+        strips = []
+        for s in range(sections):
+            strip = jnp.zeros(shape, jnp.float32)
+            for k in range(members):
+                moved = pltpu.roll(values[s][k], (start + 2 * k + LANES) % LANES, 1)
+                spot = ((lane % width) // 2 == k) & (lane < 2 * width)
+                strip = jnp.where(spot, moved, strip)
+            strips.append(strip)
+        return jnp.concatenate(strips, axis=0)
+
+    total = sections * rows
+    meets = jnp.concatenate(
+        [
+            jnp.where(
+                lane == dealt[s][0][:, 2 * field + 1 : 2 * field + 2].astype(jnp.int32), 1.0, 0.0
+            )
+            for s in range(sections)
+        ]
+        + [jnp.zeros((LANES - total, LANES), jnp.float32)],
+        axis=0,
+    )
+    met_by = meets.T[:total, :total]
+    meets = meets[:total, :total]
+    both = jnp.concatenate([meets, met_by], axis=0)
+
+    def pick(table, strip):
+        return jnp.dot(
+            table, strip, precision=lax.Precision.HIGHEST, preferred_element_type=jnp.float32
+        )
+
+    wide_odd = jnp.concatenate([odd] * sections, axis=0)
+    gap = strip_of(dealt, 1 - 2 * field)
+    gap = jnp.where(wide_odd, gap, turn(pick(met_by, gap), -1))
+
+    def gains(values):
+        strip = strip_of(values, LANES - face_lane)
+        met = pick(both, strip)
+        met = jnp.where(wide_odd, turn(met[:total], 1), turn(met[total:], -1))
+        gain = FLUX_STEP * gap * (met - strip)
+        return [gain[s * rows : (s + 1) * rows] for s in range(sections)]
+
+    def with_product(value):
+        conds = turn(value, -field)
+        return jnp.where(lane < 2 * field, value, turn(value * conds, 2 * field))
+
+    def box_sum(values):
+        summed = []
+        for s in range(sections):
+            less = [turn(value, -width) for value in values[s]]
+            more = [turn(value, width) for value in values[s]]
+            line = []
+            for k in range(members):
+                low = less[k] + (less[k - 1] if k else 0.0)
+                high = more[k] + (more[k + 1] if k < members - 1 else 0.0)
+                line.append(values[s][k] + 0.5 * jnp.where(lower_layer, low, high))
+            summed.append(line)
+        result = []
+        up = [[pltpu.roll(value, 1, 0) for value in line] for line in summed]
+        down = [[pltpu.roll(value, rows - 1, 0) for value in line] for line in summed]
+        for s in range(sections):
+            line = []
+            for k in range(members):
+                before = jnp.where(sub == 0, up[s - 1][k] if s else 0.0, up[s][k])
+                after = jnp.where(
+                    sub == rows - 1, down[s + 1][k] if s < sections - 1 else 0.0, down[s][k]
+                )
+                value = summed[s][k] + 0.5 * (before + after)
+                inward = jnp.where(at_canister, 0.0, turn(value, 1))
+                outward = jnp.where(at_compact, 0.0, turn(value, -1))
+                line.append(value + 0.5 * (inward + outward))
+            result.append(line)
+        return result
+
+    values = dealt
+    for sweep in range(SWEEPS):
+        gain = gains(values)
+        packed = [[with_product(value) for value in line] for line in values]
+        sums = box_sum(packed)
+        fresh = []
+        for s in range(sections):
+            line = []
+            for k in range(members):
+                value = values[s][k]
+                total_sum = sums[s][k]
+                conds = turn(value, -field)
+                change = conds * (total_sum - weight * value)
+                change = change + turn(total_sum, -2 * field) - value * turn(total_sum, -field)
+                back = pltpu.roll(gain[s], (face_lane - 2 * k + LANES) % LANES, 1)
+                temp = value + FLUX_STEP * change + jnp.where(at_face, back, 0.0)
+                line.append(jnp.where(is_temp, keep_temp * temp, value))
+            fresh.append(line)
+        values = fresh
+
+    per_row = 8 // sizes.layers
+    for s in range(sections):
+        order = dealt[s][0][:, 2 * field + 2 : 2 * field + 3].astype(jnp.int32)
+        order = jnp.broadcast_to(order, shape)
+        for half in range(sizes.depth // 8):
+            merged = jnp.zeros(shape, jnp.float32)
+            for k in range(per_row):
+                for layer in range(sizes.layers):
+                    spot = (k * sizes.layers + layer) * sizes.chunk
+                    moved = turn(values[s][half * per_row + k], spot - layer * width - HALO)
+                    merged = jnp.where(lane // sizes.chunk == spot // sizes.chunk, moved, merged)
+            chosen = jnp.take_along_axis(merged, order, axis=0)
+            start = s * rows * (sizes.depth // 8) + half
+            out_ref[pl.ds(start, rows, stride=sizes.depth // 8), :] = chosen
+
+
+def swap_blocks(tile, block):
+    sub = iota(tile.shape, 0)
+    spot = iota(tile.shape, 1) // block
+    for bit in (4, 2, 1):
+        up = pltpu.roll(pltpu.roll(tile, 8 - bit, 0), bit * block, 1)
+        down = pltpu.roll(pltpu.roll(tile, bit, 0), LANES - bit * block, 1)
+        moved = jnp.where(sub & bit == 0, up, down)
+        tile = jnp.where((sub & bit) == (spot & bit), tile, moved)
+    return tile
+
+
+def creep_kernel(sizes, active_ref, temps_ref, trial_ref, stress_ref, strain_ref):
+    tiles = sizes.tiles
+    halves = sizes.depth // 8
+    active = active_ref[0, 0]
+    for tile in range(tiles):
+        for element in range(halves):
+            source = pl.ds(tile * 8 * halves + element, 8, stride=halves)
+            mech_temp = swap_blocks(temps_ref[source, :], sizes.chunk)
+            spot = pl.ds(element * 8 * tiles + tile, 8, stride=tiles)
+            trial = trial_ref[spot, :]
+            rate = CREEP_RATE * jnp.exp(-ACTIVATION / (mech_temp + REFERENCE_TEMP))
+            slip = jnp.zeros(trial.shape, jnp.float32)
+            for newton_step in range(NEWTON):
+                left = trial - slip
+                pull = rate * left * left
+                slip = slip - (slip - pull * left) / (1.0 + 3.0 * pull)
+            live = jnp.where(element < active, 1.0, 0.0).astype(jnp.float32)
+            creep = live * slip
+            stress_ref[spot, :] = trial - creep
+            strain_ref[pl.ds(element * tiles + tile, 1), :] = 0.125 * jnp.sum(
+                creep, axis=0, keepdims=True
+            )
+
+
+def kernel_call(body, sizes, out_shape, memories, scratch, operands):
+    out_spec = pl.BlockSpec(memory_space=pltpu.VMEM)
+    return pl.pallas_call(
+        functools.partial(body, sizes),
+        out_shape=out_shape,
+        in_specs=[pl.BlockSpec(memory_space=memory) for memory in memories],
+        out_specs=jax.tree.map(lambda _: out_spec, out_shape),
+        scratch_shapes=scratch,
+        compiler_params=pltpu.CompilerParams(vmem_limit_bytes=16 * 1024 * 1024),
+    )(*operands)
+
+
+def on_device(
+    temp_start, conductivity, gap_conductance, partner, row_order, active_layers, trial_stress
+):
+    layers, _, rows, radial = temp_start.shape
+    sizes = Sizes(layers, rows, radial)
+    if not fits_tiles(sizes):
+        return stepwise(
+            temp_start,
+            conductivity,
+            gap_conductance,
+            partner,
+            row_order,
+            active_layers,
+            trial_stress,
+        )
+
+    def floats(*shape):
+        return jax.ShapeDtypeStruct(shape, jnp.float32)
+
+    dealt = kernel_call(
+        deal_kernel,
+        sizes,
+        floats(sizes.devices, rows, LANES),
+        [pltpu.HBM] * 5,
+        [
+            pltpu.SMEM(partner.shape, jnp.int32),
+            pltpu.SMEM(row_order.shape, jnp.int32),
+            pltpu.SMEM(gap_conductance.shape, jnp.float32),
+            pltpu.VMEM(temp_start.shape, jnp.float32),
+            pltpu.VMEM(conductivity.shape, jnp.float32),
+            pltpu.SemaphoreType.DMA((5,)),
+        ],
+        (partner, row_order, gap_conductance, temp_start, conductivity),
+    )
+    dealt = lax.all_to_all(dealt, EVERYONE, split_axis=0, concat_axis=0, tiled=True)
+    halves = sizes.depth // 8
+    temps = kernel_call(
+        sweep_kernel,
+        sizes,
+        floats(sizes.devices * halves, LANES),
+        [pltpu.VMEM],
+        [],
+        (dealt,),
+    )
+    temps = temps.reshape(sizes.devices, halves, LANES)
+    temps = lax.all_to_all(temps, EVERYONE, split_axis=0, concat_axis=0, tiled=True)
+    stress, strain = kernel_call(
+        creep_kernel,
+        sizes,
+        (floats(sizes.depth * sizes.tiles, LANES), floats(halves * sizes.tiles, LANES)),
+        [pltpu.SMEM, pltpu.VMEM, pltpu.VMEM],
+        [],
+        (
+            active_layers,
+            temps.reshape(sizes.devices * halves, LANES),
+            trial_stress.reshape(sizes.depth * sizes.tiles, LANES),
+        ),
+    )
+    return (
+        stress.reshape(sizes.depth, 1, 1, radial),
+        strain.reshape(halves, 1, 1, radial),
+    )
+
+
 def solution(mesh):
     placed = (
         P(("slab", "mech"), "iface", None, None),

time: 92 us -> 33 us (0.36)
  starting transfers between devices: 39.7 us -> 2.7 us
  blocking collectives: 25.3 us -> 14.9 us
  waiting for transfers between devices: 12 us -> 6.54 us
  local copies, waits for them, and re-layouts: 8.64 us -> 3.5 us
  Pallas kernels: 0 us -> 3.67 us
  other arithmetic: 2.41 us -> 0 us
  between operations: 2.34 us -> 1.31 us
    ppermute x12 -> x0, starting transfers between devices: 28.1 us -> none  [the longest x6 20.4 us: padded(): lax.ppermute(lax.slice_in_dim(block, block.shape[dim] - width, None, axis...]
    all_to_all x0 -> x1, blocking collectives: none -> 14.9 us  [on_device(): lax.all_to_all(dealt, EVERYONE, split_axis=0, concat_axis=0, tiled=True)]
    unnamed x2 -> x0, blocking collectives: 13.9 us -> none
    all_gather x2 -> x0, blocking collectives: 11.4 us -> none  [on_device(): compact_all = lax.all_gather(compact, 'iface', axis=1, tiled=True)]
    all_to_all x1, starting transfers between devices: 11.5 us -> 2.7 us  [on_device(): lax.all_to_all(temps, EVERYONE, split_axis=0, concat_axis=0, tiled=True)]
    ppermute x12 -> x0, waiting for transfers between devices: 5.23 us -> none  [the longest x6 5.22 us: padded(): lax.ppermute(lax.slice_in_dim(block, 0, width, axis=dim), axis, backward)]
    pallas_call x0 -> x3, Pallas kernels: none -> 3.67 us  [kernel_call(): pl.pallas_call(functools.partial(body, sizes), out_shape=out_shape, in_sp...]
    gather x3 -> x0, local copies, waits for them, and re-layouts: 1.7 us -> none  [the longest x2 1.11 us: on_device(): facing = jnp.take(compact_all, partner, axis=1)]
  transfers between devices with their start and end apart: 13 -> 1, of which waited for: 3 -> 1; matrix products, arithmetic and copies ran while one was open for 3% -> 0% of each run, Pallas kernels for 0% -> 0%
where the time goes in v3:
time: 33 us; the launch traced here: 32.6 us
  blocking collectives  14.9 us (45%)
  waiting for transfers between devices  6.54 us (20%)
  Pallas kernels  3.67 us (11%)
  local copies, waits for them, and re-layouts  3.5 us (11%)
  starting transfers between devices  2.7 us (8%)
  between operations  1.31 us (4%)
    all_to_all x1, blocking collectives, on_device(): lax.all_to_all(dealt, EVERYONE, split_axis=0, concat_axis=0, tiled=True)  14.9 us
    all_to_all x1, waiting for transfers between devices, on_device(): lax.all_to_all(temps, EVERYONE, split_axis=0, concat_axis=0, tiled=True)  6.54 us
    pallas_call x3, Pallas kernels, kernel_call(): pl.pallas_call(functools.partial(body, sizes), out_shape=out_shape, in_sp...  3.67 us
    unnamed x12, local copies, waits for them, and re-layouts  3.5 us
    all_to_all x1, starting transfers between devices, on_device(): lax.all_to_all(temps, EVERYONE, split_axis=0, concat_axis=0, tiled=True)  2.7 us
  transfers between devices with their start and end apart: 1, of which 1 were waited for; matrix products, arithmetic and copies ran while one was open for 0% of the time, Pallas kernels for 0%

profile of v3, /device:TPU:0, one launch (start us, length us, event | category | flops | bytes accessed | tf_op | source)
XLA Modules:
  0.0 32.6 jit_solution(10378517536669781697)
XLA Ops:
  0.6 0.0 copy-start
  0.6 0.7 %copy-done = f32[2,1,8,512]{3,2,1,0:T(8,128)S(1)} copy-done((f32[2,1,8,512]{3,2,1,0:T(8,128)S(1)}, f32[2,1,8,512]{3,2,1,0:T(8,128)}, u32[]{:S(2)}) %copy-start) | copy-done | bytes 32792
  1.4 0.0 copy-start.1
  1.4 0.8 %copy-done.1 = f32[2,1,8,512]{3,2,1,0:T(8,128)S(1)} copy-done((f32[2,1,8,512]{3,2,1,0:T(8,128)S(1)}, f32[2,1,8,512]{3,2,1,0:T(8,128)}, u32[]{:S(2)}) %copy-start.1) | copy-done | bytes 32792
  2.1 0.0 copy-start.3
  2.2 0.7 %copy-done.3 = f32[2,1,8]{2,1,0:T(1,128)S(1)} copy-done((f32[2,1,8]{2,1,0:T(1,128)S(1)}, f32[2,1,8]{2,1,0:T(1,128)}, u32[]{:S(2)}) %copy-start.3) | copy-done | bytes 88
  2.8 0.0 copy-start.4
  2.8 0.7 %copy-done.4 = s32[8]{0:T(128)S(1)} copy-done((s32[8]{0:T(128)S(1)}, s32[8]{0:T(128)}, u32[]{:S(2)}) %copy-start.4) | copy-done | bytes 56
  3.5 0.0 copy-start.5
  3.5 0.7 %copy-done.5 = s32[1,8]{1,0:T(1,128)S(1)} copy-done((s32[1,8]{1,0:T(1,128)S(1)}, s32[1,8]{1,0:T(1,128)}, u32[]{:S(2)}) %copy-start.5) | copy-done | bytes 56
  4.1 0.9 %shard_map.86 = f32[32,8,128]{2,1,0:T(8,128)S(1)} custom-call(s32[8]{0:T(128)S(1)} %copy-done.4, s32[1,8]{1,0:T(1,128)S(1)} %copy-done.5, f32[2,1,8]{2,1,0:T(1,128)S(1)} %copy-done.3, f32[2,1,8,512]{3,2,1,0:T(8,128)S(1)} %copy-done, f32[2,1,8,512]{3,2,1,0:T(8,128)S(1)} %copy-done.1), custom_call_target="tpu_custom_call" | custom-call | tf_op jit(solution)/shard_map/pallas_call | solution.py:405
  5.0 14.9 %all_to_all.10.dealt_ref = f32[32,8,128]{2,1,0:T(8,128)S(1)} all-to-all(f32[32,8,128]{2,1,0:T(8,128)S(1)} %shard_map.86), channel_id=1, replica_groups=mesh['slab'=2,'iface'=4,'mech'=4] {'iface','slab','mech'}, dimensions={0} | all-to-all | bytes 262144 | tf_op jit(solution)/shard_map/all_to_all | solution.py:449
  19.9 1.9 %shard_map.87 = f32[64,128]{1,0:T(8,128)} custom-call(f32[32,8,128]{2,1,0:T(8,128)S(1)} %all_to_all.10.dealt_ref), custom_call_target="tpu_custom_call" | custom-call | tf_op jit(solution)/shard_map/pallas_call | solution.py:405
  21.8 0.0 copy-start.2
  21.8 2.7 %all-to-all-start.1 = ((f32[32,2,128]{2,1,0:T(2,128)}), f32[32,2,128]{2,1,0:T(2,128)S(1)}, u32[]{:S(2)}, u32[]{:S(2)}) async-start(f32[32,2,128]{2,1,0:T(2,128)} %bitcast), calls=%async_computation.1 | async-start | bytes 65536 | tf_op jit(solution)/shard_map/all_to_all | solution.py:460
  25.1 6.5 %all-to-all-done.1 = f32[32,2,128]{2,1,0:T(2,128)S(1)} async-done(((f32[32,2,128]{2,1,0:T(2,128)}), f32[32,2,128]{2,1,0:T(2,128)S(1)}, u32[]{:S(2)}, u32[]{:S(2)}) %all-to-all-start.1) | async-done | bytes 32800 | tf_op jit(solution)/shard_map/all_to_all | solution.py:460
  31.6 0.0 copy-done.2
  31.7 0.9 %shard_map.88 = (f32[64,128]{1,0:T(8,128)}, f32[8,128]{1,0:T(8,128)}) custom-call(s32[1,1]{1,0:T(1,128)S(6)} %copy.11.active_ref, f32[64,128]{1,0:T(8,128)S(1)} %bitcast.5, f32[64,128]{1,0:T(8,128)S(1)} %bitcast.6), custom_call_target="tpu_custom_call" | custom-call | tf_op jit(solution)/shard_map/pallas_call | solution.py:405
Async XLA Ops:
  0.6 0.8 %copy-start = (f32[2,1,8,512]{3,2,1,0:T(8,128)S(1)}, f32[2,1,8,512]{3,2,1,0:T(8,128)}, u32[]{:S(2)}) copy-start(f32[2,1,8,512]{3,2,1,0:T(8,128)} %temp_hbm.1) | copy-start | bytes 98308
  1.4 0.8 %copy-start.1 = (f32[2,1,8,512]{3,2,1,0:T(8,128)S(1)}, f32[2,1,8,512]{3,2,1,0:T(8,128)}, u32[]{:S(2)}) copy-start(f32[2,1,8,512]{3,2,1,0:T(8,128)} %cond_hbm.1) | copy-start | bytes 98308
  2.1 0.7 %copy-start.3 = (f32[2,1,8]{2,1,0:T(1,128)S(1)}, f32[2,1,8]{2,1,0:T(1,128)}, u32[]{:S(2)}) copy-start(f32[2,1,8]{2,1,0:T(1,128)} %gap_hbm.1) | copy-start | bytes 196
  2.8 0.7 %copy-start.4 = (s32[8]{0:T(128)S(1)}, s32[8]{0:T(128)}, u32[]{:S(2)}) copy-start(s32[8]{0:T(128)} %partner_hbm.1) | copy-start | bytes 100
  3.5 0.7 %copy-start.5 = (s32[1,8]{1,0:T(1,128)S(1)}, s32[1,8]{1,0:T(1,128)}, u32[]{:S(2)}) copy-start(s32[1,8]{1,0:T(1,128)} %order_hbm.1) | copy-start | bytes 100
  21.8 9.9 %copy-start.2 = (f32[16,1,1,512]{3,2,1,0:T(1,128)S(1)}, f32[16,1,1,512]{3,2,1,0:T(1,128)}, u32[]{:S(2)}) copy-start(f32[16,1,1,512]{3,2,1,0:T(1,128)} %param.13) | copy-start | bytes 98308
  21.8 9.9 %all-to-all-start.1 = ((f32[32,2,128]{2,1,0:T(2,128)}), f32[32,2,128]{2,1,0:T(2,128)S(1)}, u32[]{:S(2)}, u32[]{:S(2)}) async-start(f32[32,2,128]{2,1,0:T(2,128)} %bitcast), calls=%async_computation.1 | async-start | bytes 65536 | tf_op jit(solution)/shard_map/all_to_all | solution.py:460

commit v4 on v3

--- a/solution.py
+++ b/solution.py
@@ -400,7 +400,7 @@
             )
 
 
-def kernel_call(body, sizes, out_shape, memories, scratch, operands):
+def kernel_call(body, sizes, out_shape, memories, scratch, operands, grant=16 * 1024 * 1024):
     out_spec = pl.BlockSpec(memory_space=pltpu.VMEM)
     return pl.pallas_call(
         functools.partial(body, sizes),
@@ -408,7 +408,7 @@
         in_specs=[pl.BlockSpec(memory_space=memory) for memory in memories],
         out_specs=jax.tree.map(lambda _: out_spec, out_shape),
         scratch_shapes=scratch,
-        compiler_params=pltpu.CompilerParams(vmem_limit_bytes=16 * 1024 * 1024),
+        compiler_params=pltpu.CompilerParams(vmem_limit_bytes=grant),
     )(*operands)
 
 
@@ -445,6 +445,7 @@
             pltpu.SemaphoreType.DMA((5,)),
         ],
         (partner, row_order, gap_conductance, temp_start, conductivity),
+        grant=60 * 1024 * 1024,
     )
     dealt = lax.all_to_all(dealt, EVERYONE, split_axis=0, concat_axis=0, tiled=True)
     halves = sizes.depth // 8

time: 33 us -> 30.5 us (0.924)
  local copies, waits for them, and re-layouts: 3.5 us -> 0.01 us
  Pallas kernels: 3.67 us -> 4.53 us
    unnamed x12 -> x2, local copies, waits for them, and re-layouts: 3.5 us -> 0.01 us
    pallas_call x3, Pallas kernels: 3.67 us -> 4.53 us  [kernel_call(): pl.pallas_call(functools.partial(body, sizes), out_shape=out_shape, in_sp...]
where the time goes in v4:
time: 30.5 us; the launch traced here: 30.1 us
  blocking collectives  15.1 us (50%)
  waiting for transfers between devices  6.54 us (21%)
  Pallas kernels  4.53 us (15%)
  starting transfers between devices  2.7 us (9%)
  between operations  1.3 us (4%)
    all_to_all x1, blocking collectives, on_device(): lax.all_to_all(dealt, EVERYONE, split_axis=0, concat_axis=0, tiled=True)  15.1 us
    all_to_all x1, waiting for transfers between devices, on_device(): lax.all_to_all(temps, EVERYONE, split_axis=0, concat_axis=0, tiled=True)  6.54 us
    pallas_call x3, Pallas kernels, kernel_call(): pl.pallas_call(functools.partial(body, sizes), out_shape=out_shape, in_sp...  4.53 us
    all_to_all x1, starting transfers between devices, on_device(): lax.all_to_all(temps, EVERYONE, split_axis=0, concat_axis=0, tiled=True)  2.7 us
  transfers between devices with their start and end apart: 1, of which 1 were waited for; matrix products, arithmetic and copies ran while one was open for 0% of the time, Pallas kernels for 0%

profile of v4, /device:TPU:0, one launch (start us, length us, event | category | flops | bytes accessed | tf_op | source)
XLA Modules:
  0.0 30.1 jit_solution(16817808257601182756)
XLA Ops:
  0.6 1.7 %shard_map.86 = f32[32,8,128]{2,1,0:T(8,128)} custom-call(s32[8]{0:T(128)} %partner_hbm.1, s32[1,8]{1,0:T(1,128)} %order_hbm.1, f32[2,1,8]{2,1,0:T(1,128)} %gap_hbm.1, f32[2,1,8,512]{3,2,1,0:T(8,128)} %temp_hbm.1, f32[2,1,8,512]{3,2,1,0:T(8,128)} %cond_hbm.1), custom_call_target="tpu_custom_call" | custom-call | tf_op jit(solution)/shard_map/pallas_call | solution.py:405
  2.4 15.1 %all_to_all.10.dealt_ref = f32[32,8,128]{2,1,0:T(8,128)S(1)} all-to-all(f32[32,8,128]{2,1,0:T(8,128)} %shard_map.86), channel_id=1, replica_groups=mesh['slab'=2,'iface'=4,'mech'=4] {'iface','slab','mech'}, dimensions={0} | all-to-all | bytes 262144 | tf_op jit(solution)/shard_map/all_to_all | solution.py:450
  17.4 1.9 %shard_map.87 = f32[64,128]{1,0:T(8,128)} custom-call(f32[32,8,128]{2,1,0:T(8,128)S(1)} %all_to_all.10.dealt_ref), custom_call_target="tpu_custom_call" | custom-call | tf_op jit(solution)/shard_map/pallas_call | solution.py:405
  19.3 0.0 copy-start
  19.3 2.7 %all-to-all-start.1 = ((f32[32,2,128]{2,1,0:T(2,128)}), f32[32,2,128]{2,1,0:T(2,128)S(1)}, u32[]{:S(2)}, u32[]{:S(2)}) async-start(f32[32,2,128]{2,1,0:T(2,128)} %bitcast), calls=%async_computation.1 | async-start | bytes 65536 | tf_op jit(solution)/shard_map/all_to_all | solution.py:461
  22.7 6.5 %all-to-all-done.1 = f32[32,2,128]{2,1,0:T(2,128)S(1)} async-done(((f32[32,2,128]{2,1,0:T(2,128)}), f32[32,2,128]{2,1,0:T(2,128)S(1)}, u32[]{:S(2)}, u32[]{:S(2)}) %all-to-all-start.1) | async-done | bytes 32800 | tf_op jit(solution)/shard_map/all_to_all | solution.py:461
  29.2 0.0 copy-done
  29.2 0.9 %shard_map.88 = (f32[64,128]{1,0:T(8,128)}, f32[8,128]{1,0:T(8,128)}) custom-call(s32[1,1]{1,0:T(1,128)S(6)} %copy.11.active_ref, f32[64,128]{1,0:T(8,128)S(1)} %bitcast.5, f32[64,128]{1,0:T(8,128)S(1)} %bitcast.6), custom_call_target="tpu_custom_call" | custom-call | tf_op jit(solution)/shard_map/pallas_call | solution.py:405
Async XLA Ops:
  19.3 9.9 %copy-start = (f32[16,1,1,512]{3,2,1,0:T(1,128)S(1)}, f32[16,1,1,512]{3,2,1,0:T(1,128)}, u32[]{:S(2)}) copy-start(f32[16,1,1,512]{3,2,1,0:T(1,128)} %param.13) | copy-start | bytes 98308
  19.3 9.9 %all-to-all-start.1 = ((f32[32,2,128]{2,1,0:T(2,128)}), f32[32,2,128]{2,1,0:T(2,128)S(1)}, u32[]{:S(2)}, u32[]{:S(2)}) async-start(f32[32,2,128]{2,1,0:T(2,128)} %bitcast), calls=%async_computation.1 | async-start | bytes 65536 | tf_op jit(solution)/shard_map/all_to_all | solution.py:461

commit v5 on v3

--- a/solution.py
+++ b/solution.py
@@ -178,11 +178,11 @@
     sems,
 ):
     pairs = (
-        (temp_hbm, temp_ref),
-        (cond_hbm, cond_ref),
         (gap_hbm, gap_ref),
         (partner_hbm, partner_ref),
         (order_hbm, order_ref),
+        (temp_hbm, temp_ref),
+        (cond_hbm, cond_ref),
     )
     copies = [
         pltpu.make_async_copy(source, target, sems.at[index])
@@ -190,7 +190,7 @@
     ]
     for copy in copies:
         copy.start()
-    for copy in copies:
+    for copy in copies[:3]:
         copy.wait()
     shape = (sizes.rows, LANES)
     lane = iota(shape, 1)
@@ -205,6 +205,8 @@
         extra = jnp.where(spot, partner_ref[row].astype(jnp.float32), extra)
         spot = (sub == row) & (lane == extra_at + 2)
         extra = jnp.where(spot, order_ref[0, row].astype(jnp.float32), extra)
+    for copy in copies[3:]:
+        copy.wait()
     blocks = [
         [ref[layer, 0, :, pl.ds(tile * LANES, LANES)] for tile in range(sizes.tiles)]
         for ref in (temp_ref, cond_ref)
@@ -297,9 +299,10 @@
         gain = FLUX_STEP * gap * (met - strip)
         return [gain[s * rows : (s + 1) * rows] for s in range(sections)]
 
-    def with_product(value):
-        conds = turn(value, -field)
-        return jnp.where(lane < 2 * field, value, turn(value * conds, 2 * field))
+    conds = [[turn(value, -field) for value in line] for line in dealt]
+
+    def with_product(value, cond):
+        return jnp.where(lane < 2 * field, value, turn(value * cond, 2 * field))
 
     def box_sum(values):
         summed = []
@@ -330,19 +333,24 @@
         return result
 
     values = dealt
+    cond_sums = None
     for sweep in range(SWEEPS):
         gain = gains(values)
-        packed = [[with_product(value) for value in line] for line in values]
+        packed = [
+            [with_product(value, cond) for value, cond in zip(*lines)]
+            for lines in zip(values, conds)
+        ]
         sums = box_sum(packed)
+        if cond_sums is None:
+            cond_sums = [[turn(total_sum, -field) for total_sum in line] for line in sums]
         fresh = []
         for s in range(sections):
             line = []
             for k in range(members):
                 value = values[s][k]
                 total_sum = sums[s][k]
-                conds = turn(value, -field)
-                change = conds * (total_sum - weight * value)
-                change = change + turn(total_sum, -2 * field) - value * turn(total_sum, -field)
+                change = conds[s][k] * (total_sum - weight * value)
+                change = change + turn(total_sum, -2 * field) - value * cond_sums[s][k]
                 back = pltpu.roll(gain[s], (face_lane - 2 * k + LANES) % LANES, 1)
                 temp = value + FLUX_STEP * change + jnp.where(at_face, back, 0.0)
                 line.append(jnp.where(is_temp, keep_temp * temp, value))
@@ -392,8 +400,7 @@
                 left = trial - slip
                 pull = rate * left * left
                 slip = slip - (slip - pull * left) / (1.0 + 3.0 * pull)
-            live = jnp.where(element < active, 1.0, 0.0).astype(jnp.float32)
-            creep = live * slip
+            creep = jnp.where(element < active, slip, 0.0)
             stress_ref[spot, :] = trial - creep
             strain_ref[pl.ds(element * tiles + tile, 1), :] = 0.125 * jnp.sum(
                 creep, axis=0, keepdims=True
@@ -402,14 +409,18 @@
 
 def kernel_call(body, sizes, out_shape, memories, scratch, operands):
     out_spec = pl.BlockSpec(memory_space=pltpu.VMEM)
+    pinned = [
+        pltpu.with_memory_space_constraint(operand, memory) if memory is pltpu.HBM else operand
+        for operand, memory in zip(operands, memories)
+    ]
     return pl.pallas_call(
         functools.partial(body, sizes),
         out_shape=out_shape,
         in_specs=[pl.BlockSpec(memory_space=memory) for memory in memories],
-        out_specs=jax.tree.map(lambda _: out_spec, out_shape),
+        out_specs=[out_spec] * len(out_shape),
         scratch_shapes=scratch,
         compiler_params=pltpu.CompilerParams(vmem_limit_bytes=16 * 1024 * 1024),
-    )(*operands)
+    )(*pinned)
 
 
 def on_device(
@@ -431,10 +442,13 @@
     def floats(*shape):
         return jax.ShapeDtypeStruct(shape, jnp.float32)
 
-    dealt = kernel_call(
+    def near(*shape):
+        return pltpu.VMEM(shape, jnp.float32)
+
+    (dealt,) = kernel_call(
         deal_kernel,
         sizes,
-        floats(sizes.devices, rows, LANES),
+        (near(sizes.devices, rows, LANES),),
         [pltpu.HBM] * 5,
         [
             pltpu.SMEM(partner.shape, jnp.int32),
@@ -448,10 +462,10 @@
     )
     dealt = lax.all_to_all(dealt, EVERYONE, split_axis=0, concat_axis=0, tiled=True)
     halves = sizes.depth // 8
-    temps = kernel_call(
+    (temps,) = kernel_call(
         sweep_kernel,
         sizes,
-        floats(sizes.devices * halves, LANES),
+        (near(sizes.devices * halves, LANES),),
         [pltpu.VMEM],
         [],
         (dealt,),

time: 33 us -> 29.4 us (0.89)
  local copies, waits for them, and re-layouts: 3.5 us -> 0.01 us
    unnamed x12 -> x2, local copies, waits for them, and re-layouts: 3.5 us -> 0.01 us
where the time goes in v5:
time: 29.4 us; the launch traced here: 29.1 us
  blocking collectives  14.9 us (51%)
  waiting for transfers between devices  6.54 us (22%)
  Pallas kernels  3.75 us (13%)
  starting transfers between devices  2.7 us (9%)
  between operations  1.3 us (4%)
    all_to_all x1, blocking collectives, on_device(): lax.all_to_all(dealt, EVERYONE, split_axis=0, concat_axis=0, tiled=True)  14.9 us
    all_to_all x1, waiting for transfers between devices, on_device(): lax.all_to_all(temps, EVERYONE, split_axis=0, concat_axis=0, tiled=True)  6.54 us
    pallas_call x3, Pallas kernels, kernel_call(): pl.pallas_call(functools.partial(body, sizes), out_shape=out_shape, in_sp...  3.75 us
    all_to_all x1, starting transfers between devices, on_device(): lax.all_to_all(temps, EVERYONE, split_axis=0, concat_axis=0, tiled=True)  2.7 us
  transfers between devices with their start and end apart: 1, of which 1 were waited for; matrix products, arithmetic and copies ran while one was open for 0% of the time, Pallas kernels for 0%

profile of v5, /device:TPU:0, one launch (start us, length us, event | category | flops | bytes accessed | tf_op | source)
XLA Modules:
  0.0 29.1 jit_solution(5230403554757364852)
XLA Ops:
  0.6 1.0 %shard_map.86 = f32[32,8,128]{2,1,0:T(8,128)S(1)} custom-call(s32[8]{0:T(128)} %partner_hbm.1, s32[1,8]{1,0:T(1,128)} %order_hbm.1, f32[2,1,8]{2,1,0:T(1,128)} %gap_hbm.1, f32[2,1,8,512]{3,2,1,0:T(8,128)} %temp_hbm.1, f32[2,1,8,512]{3,2,1,0:T(8,128)} %cond_hbm.1), custom_call_target="tpu_custom_call" | custom-call | tf_op jit(solution)/shard_map/pallas_call | solution.py:416
  1.7 14.9 %all_to_all.10.dealt_ref = f32[32,8,128]{2,1,0:T(8,128)S(1)} all-to-all(f32[32,8,128]{2,1,0:T(8,128)S(1)} %shard_map.86), channel_id=1, replica_groups=mesh['slab'=2,'iface'=4,'mech'=4] {'iface','slab','mech'}, dimensions={0} | all-to-all | bytes 262144 | tf_op jit(solution)/shard_map/all_to_all | solution.py:463
  16.5 1.8 %shard_map.87 = f32[64,128]{1,0:T(8,128)} custom-call(f32[32,8,128]{2,1,0:T(8,128)S(1)} %all_to_all.10.dealt_ref), custom_call_target="tpu_custom_call" | custom-call | tf_op jit(solution)/shard_map/pallas_call | solution.py:416
  18.3 0.0 copy-start
  18.3 2.7 %all-to-all-start.1 = ((f32[32,2,128]{2,1,0:T(2,128)}), f32[32,2,128]{2,1,0:T(2,128)S(1)}, u32[]{:S(2)}, u32[]{:S(2)}) async-start(f32[32,2,128]{2,1,0:T(2,128)} %bitcast), calls=%async_computation.1 | async-start | bytes 65536 | tf_op jit(solution)/shard_map/all_to_all | solution.py:474
  21.7 6.5 %all-to-all-done.1 = f32[32,2,128]{2,1,0:T(2,128)S(1)} async-done(((f32[32,2,128]{2,1,0:T(2,128)}), f32[32,2,128]{2,1,0:T(2,128)S(1)}, u32[]{:S(2)}, u32[]{:S(2)}) %all-to-all-start.1) | async-done | bytes 32800 | tf_op jit(solution)/shard_map/all_to_all | solution.py:474
  28.2 0.0 copy-done
  28.2 0.9 %shard_map.88 = (f32[64,128]{1,0:T(8,128)}, f32[8,128]{1,0:T(8,128)}) custom-call(s32[1,1]{1,0:T(1,128)S(6)} %copy.11.active_ref, f32[64,128]{1,0:T(8,128)S(1)} %bitcast.5, f32[64,128]{1,0:T(8,128)S(1)} %bitcast.6), custom_call_target="tpu_custom_call" | custom-call | tf_op jit(solution)/shard_map/pallas_call | solution.py:416
Async XLA Ops:
  18.3 9.9 %copy-start = (f32[16,1,1,512]{3,2,1,0:T(1,128)S(1)}, f32[16,1,1,512]{3,2,1,0:T(1,128)}, u32[]{:S(2)}) copy-start(f32[16,1,1,512]{3,2,1,0:T(1,128)} %param.13) | copy-start | bytes 98308
  18.3 9.9 %all-to-all-start.1 = ((f32[32,2,128]{2,1,0:T(2,128)}), f32[32,2,128]{2,1,0:T(2,128)S(1)}, u32[]{:S(2)}, u32[]{:S(2)}) async-start(f32[32,2,128]{2,1,0:T(2,128)} %bitcast), calls=%async_computation.1 | async-start | bytes 65536 | tf_op jit(solution)/shard_map/all_to_all | solution.py:474

commit v6 on v5

--- a/solution.py
+++ b/solution.py
@@ -203,6 +203,9 @@
             extra = jnp.where(spot, gap_ref[layer, 0, row], extra)
         spot = (sub == row) & (lane == extra_at + 1)
         extra = jnp.where(spot, partner_ref[row].astype(jnp.float32), extra)
+        extra = jnp.where(
+            lane == extra_at + sizes.rows + row, partner_ref[row].astype(jnp.float32), extra
+        )
         spot = (sub == row) & (lane == extra_at + 2)
         extra = jnp.where(spot, order_ref[0, row].astype(jnp.float32), extra)
     for copy in copies[3:]:
@@ -254,7 +257,6 @@
 
     dealt = [[dealt_ref[s * members + k] for k in range(members)] for s in range(sections)]
 
-    strip_lane = (lane < 2 * members) | ((lane >= width) & (lane < width + 2 * members))
     odd = (lane % width) % 2 == 1
 
     def strip_of(values, start):
@@ -262,42 +264,48 @@
         for s in range(sections):
             strip = jnp.zeros(shape, jnp.float32)
             for k in range(members):
-                moved = pltpu.roll(values[s][k], (start + 2 * k + LANES) % LANES, 1)
+                moved = pltpu.roll(values[s][k], (start + 2 * k) % LANES, 1)
                 spot = ((lane % width) // 2 == k) & (lane < 2 * width)
                 strip = jnp.where(spot, moved, strip)
             strips.append(strip)
-        return jnp.concatenate(strips, axis=0)
-
-    total = sections * rows
-    meets = jnp.concatenate(
-        [
-            jnp.where(
-                lane == dealt[s][0][:, 2 * field + 1 : 2 * field + 2].astype(jnp.int32), 1.0, 0.0
-            )
-            for s in range(sections)
-        ]
-        + [jnp.zeros((LANES - total, LANES), jnp.float32)],
-        axis=0,
-    )
-    met_by = meets.T[:total, :total]
-    meets = meets[:total, :total]
-    both = jnp.concatenate([meets, met_by], axis=0)
-
-    def pick(table, strip):
-        return jnp.dot(
-            table, strip, precision=lax.Precision.HIGHEST, preferred_element_type=jnp.float32
-        )
-
-    wide_odd = jnp.concatenate([odd] * sections, axis=0)
-    gap = strip_of(dealt, 1 - 2 * field)
-    gap = jnp.where(wide_odd, gap, turn(pick(met_by, gap), -1))
+        return strips
+
+    name_at = 2 * field + rows
+    named = (lane >= name_at) & (lane < name_at + rows)
+    blocks = []
+    places = []
+    for s in range(sections):
+        partner = dealt[s][0][:, 2 * field + 1 : 2 * field + 2]
+        names = jnp.zeros(shape, jnp.float32)
+        target = (s * rows + sub).astype(jnp.float32)
+        for t in range(sections):
+            hit = named & (dealt[t][0] == target)
+            names = jnp.where(hit, (t * rows + lane - name_at).astype(jnp.float32), names)
+        inverse = jnp.sum(names, axis=1, keepdims=True)
+        index = jnp.where(
+            odd, jnp.broadcast_to(partner, shape), jnp.broadcast_to(inverse, shape)
+        ).astype(jnp.int32)
+        blocks.append(index // rows)
+        places.append(index % rows)
+
+    def met_by(strips):
+        swapped = [jnp.where(odd, turn(strip, 1), turn(strip, -1)) for strip in strips]
+        result = []
+        for s in range(sections):
+            met = jnp.take_along_axis(swapped[0], places[s], axis=0)
+            for t in range(1, sections):
+                other = jnp.take_along_axis(swapped[t], places[s], axis=0)
+                met = jnp.where(blocks[s] == t, other, met)
+            result.append(met)
+        return result
+
+    gap = strip_of(dealt, LANES + 1 - 2 * field)
+    gap = [jnp.where(odd, own, met) for own, met in zip(gap, met_by(gap))]
 
     def gains(values):
-        strip = strip_of(values, LANES - face_lane)
-        met = pick(both, strip)
-        met = jnp.where(wide_odd, turn(met[:total], 1), turn(met[total:], -1))
-        gain = FLUX_STEP * gap * (met - strip)
-        return [gain[s * rows : (s + 1) * rows] for s in range(sections)]
+        strips = strip_of(values, LANES - face_lane)
+        met = met_by(strips)
+        return [FLUX_STEP * g * (m - own) for g, m, own in zip(gap, met, strips)]
 
     conds = [[turn(value, -field) for value in line] for line in dealt]
 

time: 29.4 us -> 29.5 us (level)
  no operation moved by 1% of the time
where the time goes in v6:
time: 29.5 us; the launch traced here: 29.2 us
  blocking collectives  14.9 us (51%)
  waiting for transfers between devices  6.54 us (22%)
  Pallas kernels  3.84 us (13%)
  starting transfers between devices  2.7 us (9%)
  between operations  1.3 us (4%)
    all_to_all x1, blocking collectives, on_device(): lax.all_to_all(dealt, EVERYONE, split_axis=0, concat_axis=0, tiled=True)  14.9 us
    all_to_all x1, waiting for transfers between devices, on_device(): lax.all_to_all(temps, EVERYONE, split_axis=0, concat_axis=0, tiled=True)  6.54 us
    pallas_call x3, Pallas kernels, kernel_call(): pl.pallas_call(functools.partial(body, sizes), out_shape=out_shape, in_sp...  3.84 us
    all_to_all x1, starting transfers between devices, on_device(): lax.all_to_all(temps, EVERYONE, split_axis=0, concat_axis=0, tiled=True)  2.7 us
  transfers between devices with their start and end apart: 1, of which 1 were waited for; matrix products, arithmetic and copies ran while one was open for 0% of the time, Pallas kernels for 0%

profile of v6, /device:TPU:0, one launch (start us, length us, event | category | flops | bytes accessed | tf_op | source)
XLA Modules:
  0.0 29.2 jit_solution(5565694175017142424)
XLA Ops:
  0.6 1.0 %shard_map.86 = f32[32,8,128]{2,1,0:T(8,128)S(1)} custom-call(s32[8]{0:T(128)} %partner_hbm.1, s32[1,8]{1,0:T(1,128)} %order_hbm.1, f32[2,1,8]{2,1,0:T(1,128)} %gap_hbm.1, f32[2,1,8,512]{3,2,1,0:T(8,128)} %temp_hbm.1, f32[2,1,8,512]{3,2,1,0:T(8,128)} %cond_hbm.1), custom_call_target="tpu_custom_call" | custom-call | tf_op jit(solution)/shard_map/pallas_call | solution.py:424
  1.7 14.9 %all_to_all.10.dealt_ref = f32[32,8,128]{2,1,0:T(8,128)S(1)} all-to-all(f32[32,8,128]{2,1,0:T(8,128)S(1)} %shard_map.86), channel_id=1, replica_groups=mesh['slab'=2,'iface'=4,'mech'=4] {'iface','slab','mech'}, dimensions={0} | all-to-all | bytes 262144 | tf_op jit(solution)/shard_map/all_to_all | solution.py:471
  16.5 1.9 %shard_map.87 = f32[64,128]{1,0:T(8,128)} custom-call(f32[32,8,128]{2,1,0:T(8,128)S(1)} %all_to_all.10.dealt_ref), custom_call_target="tpu_custom_call" | custom-call | tf_op jit(solution)/shard_map/pallas_call | solution.py:424
  18.4 0.0 copy-start
  18.4 2.7 %all-to-all-start.1 = ((f32[32,2,128]{2,1,0:T(2,128)}), f32[32,2,128]{2,1,0:T(2,128)S(1)}, u32[]{:S(2)}, u32[]{:S(2)}) async-start(f32[32,2,128]{2,1,0:T(2,128)} %bitcast), calls=%async_computation.1 | async-start | bytes 65536 | tf_op jit(solution)/shard_map/all_to_all | solution.py:482
  21.8 6.5 %all-to-all-done.1 = f32[32,2,128]{2,1,0:T(2,128)S(1)} async-done(((f32[32,2,128]{2,1,0:T(2,128)}), f32[32,2,128]{2,1,0:T(2,128)S(1)}, u32[]{:S(2)}, u32[]{:S(2)}) %all-to-all-start.1) | async-done | bytes 32800 | tf_op jit(solution)/shard_map/all_to_all | solution.py:482
  28.3 0.0 copy-done
  28.3 0.9 %shard_map.88 = (f32[64,128]{1,0:T(8,128)}, f32[8,128]{1,0:T(8,128)}) custom-call(s32[1,1]{1,0:T(1,128)S(6)} %copy.11.active_ref, f32[64,128]{1,0:T(8,128)S(1)} %bitcast.5, f32[64,128]{1,0:T(8,128)S(1)} %bitcast.6), custom_call_target="tpu_custom_call" | custom-call | tf_op jit(solution)/shard_map/pallas_call | solution.py:424
Async XLA Ops:
  18.4 9.9 %copy-start = (f32[16,1,1,512]{3,2,1,0:T(1,128)S(1)}, f32[16,1,1,512]{3,2,1,0:T(1,128)}, u32[]{:S(2)}) copy-start(f32[16,1,1,512]{3,2,1,0:T(1,128)} %param.13) | copy-start | bytes 98308
  18.4 9.9 %all-to-all-start.1 = ((f32[32,2,128]{2,1,0:T(2,128)}), f32[32,2,128]{2,1,0:T(2,128)S(1)}, u32[]{:S(2)}, u32[]{:S(2)}) async-start(f32[32,2,128]{2,1,0:T(2,128)} %bitcast), calls=%async_computation.1 | async-start | bytes 65536 | tf_op jit(solution)/shard_map/all_to_all | solution.py:482

commit v7 on v5

--- a/solution.py
+++ b/solution.py
@@ -146,7 +146,8 @@
         self.depth = layers * self.members
         self.chunk = radial // self.devices
         self.width = self.chunk + 2 * HALO
-        self.field = layers * self.width
+        self.layer_lanes = LANES // layers
+        self.extra_at = 3 * self.width
         self.gap_row = radial // 2
 
 
@@ -159,6 +160,7 @@
         and sizes.radial % sizes.devices == 0
         and sizes.chunk * 8 == LANES
         and sizes.radial % (2 * LANES) == 0
+        and sizes.extra_at + 3 <= sizes.layer_lanes
     )
 
 
@@ -195,11 +197,11 @@
     shape = (sizes.rows, LANES)
     lane = iota(shape, 1)
     sub = iota(shape, 0)
-    extra_at = 2 * sizes.field
+    extra_at = sizes.extra_at
     extra = jnp.zeros(shape, jnp.float32)
     for row in range(sizes.rows):
         for layer in range(sizes.layers):
-            spot = (sub == row) & (lane == extra_at + layer * sizes.width)
+            spot = (sub == row) & (lane == extra_at + layer * sizes.layer_lanes)
             extra = jnp.where(spot, gap_ref[layer, 0, row], extra)
         spot = (sub == row) & (lane == extra_at + 1)
         extra = jnp.where(spot, partner_ref[row].astype(jnp.float32), extra)
@@ -208,15 +210,17 @@
     for copy in copies[3:]:
         copy.wait()
     blocks = [
-        [ref[layer, 0, :, pl.ds(tile * LANES, LANES)] for tile in range(sizes.tiles)]
-        for ref in (temp_ref, cond_ref)
+        (
+            layer * sizes.layer_lanes + field * sizes.width,
+            [ref[layer, 0, :, pl.ds(tile * LANES, LANES)] for tile in range(sizes.tiles)],
+        )
+        for field, ref in enumerate((temp_ref, cond_ref))
         for layer in range(sizes.layers)
     ]
     for device in range(sizes.devices):
         first = device * sizes.chunk - HALO
         packed = extra
-        for index, block in enumerate(blocks):
-            base = index * sizes.width
+        for base, block in blocks:
             for tile in range(sizes.tiles):
                 low = max(first, tile * LANES)
                 high = min(first + sizes.width, (tile + 1) * LANES)
@@ -228,8 +232,8 @@
         out_ref[device] = packed
 
 
-def sweep_kernel(sizes, dealt_ref, out_ref):
-    rows, width, field = sizes.rows, sizes.width, sizes.field
+def sweep_kernel(sizes, dealt_ref, out_ref, line_ref):
+    rows, width, half_lanes = sizes.rows, sizes.width, sizes.layer_lanes
     sections, members = sizes.sections, sizes.members
     shape = (rows, LANES)
     lane = iota(shape, 1)
@@ -237,14 +241,14 @@
     place = lax.axis_index("iface") * members
     place = place + lax.axis_index("slab") * lax.axis_size("mech") + lax.axis_index("mech")
     first = place * sizes.chunk - HALO
-    segment = lane // width
-    radius = first + lane % width
-    lower_layer = segment % 2 == 0
+    spot_in_layer = lane % half_lanes
+    radius = first + spot_in_layer % width
+    lower_layer = lane < half_lanes
     at_compact = radius == sizes.gap_row - 1
     at_canister = radius == sizes.gap_row
     in_grid = (radius >= 0) & (radius < sizes.radial)
     weight = jnp.where(at_compact | at_canister, 6.0, 8.0)
-    is_temp = lane < field
+    is_temp = spot_in_layer < width
     at_face = is_temp & (at_compact | at_canister)
     keep_temp = jnp.where(is_temp & in_grid, 1.0, 0.0)
     face_lane = sizes.gap_row - 1 - first
@@ -254,16 +258,15 @@
 
     dealt = [[dealt_ref[s * members + k] for k in range(members)] for s in range(sections)]
 
-    strip_lane = (lane < 2 * members) | ((lane >= width) & (lane < width + 2 * members))
-    odd = (lane % width) % 2 == 1
+    odd = lane % 2 == 1
 
     def strip_of(values, start):
         strips = []
         for s in range(sections):
             strip = jnp.zeros(shape, jnp.float32)
             for k in range(members):
-                moved = pltpu.roll(values[s][k], (start + 2 * k + LANES) % LANES, 1)
-                spot = ((lane % width) // 2 == k) & (lane < 2 * width)
+                moved = pltpu.roll(values[s][k], (start + 2 * k) % LANES, 1)
+                spot = spot_in_layer // 2 == k
                 strip = jnp.where(spot, moved, strip)
             strips.append(strip)
         return jnp.concatenate(strips, axis=0)
@@ -272,7 +275,7 @@
     meets = jnp.concatenate(
         [
             jnp.where(
-                lane == dealt[s][0][:, 2 * field + 1 : 2 * field + 2].astype(jnp.int32), 1.0, 0.0
+                lane == dealt[s][0][:, sizes.extra_at + 1 : sizes.extra_at + 2].astype(jnp.int32), 1.0, 0.0
             )
             for s in range(sections)
         ]
@@ -289,7 +292,7 @@
         )
 
     wide_odd = jnp.concatenate([odd] * sections, axis=0)
-    gap = strip_of(dealt, 1 - 2 * field)
+    gap = strip_of(dealt, LANES + 1 - sizes.extra_at)
     gap = jnp.where(wide_odd, gap, turn(pick(met_by, gap), -1))
 
     def gains(values):
@@ -299,33 +302,30 @@
         gain = FLUX_STEP * gap * (met - strip)
         return [gain[s * rows : (s + 1) * rows] for s in range(sections)]
 
-    conds = [[turn(value, -field) for value in line] for line in dealt]
+    conds = [[turn(value, -width) for value in line] for line in dealt]
+    edge = jnp.zeros(shape, jnp.float32)
+    for k in range(members):
+        line_ref[k, pl.ds(0, rows), :] = edge
+        line_ref[k, pl.ds(rows + total, rows), :] = edge
 
     def with_product(value, cond):
-        return jnp.where(lane < 2 * field, value, turn(value * cond, 2 * field))
+        return jnp.where(spot_in_layer < 2 * width, value, turn(value * cond, 2 * width))
 
     def box_sum(values):
-        summed = []
         for s in range(sections):
-            less = [turn(value, -width) for value in values[s]]
-            more = [turn(value, width) for value in values[s]]
-            line = []
+            other = [turn(value, half_lanes) for value in values[s]]
             for k in range(members):
-                low = less[k] + (less[k - 1] if k else 0.0)
-                high = more[k] + (more[k + 1] if k < members - 1 else 0.0)
-                line.append(values[s][k] + 0.5 * jnp.where(lower_layer, low, high))
-            summed.append(line)
+                before = other[k - 1] if k else 0.0
+                after = other[k + 1] if k < members - 1 else 0.0
+                near = other[k] + jnp.where(lower_layer, before, after)
+                line_ref[k, pl.ds(rows + s * rows, rows), :] = values[s][k] + 0.5 * near
         result = []
-        up = [[pltpu.roll(value, 1, 0) for value in line] for line in summed]
-        down = [[pltpu.roll(value, rows - 1, 0) for value in line] for line in summed]
         for s in range(sections):
             line = []
             for k in range(members):
-                before = jnp.where(sub == 0, up[s - 1][k] if s else 0.0, up[s][k])
-                after = jnp.where(
-                    sub == rows - 1, down[s + 1][k] if s < sections - 1 else 0.0, down[s][k]
-                )
-                value = summed[s][k] + 0.5 * (before + after)
+                start = rows + s * rows
+                near = line_ref[k, pl.ds(start - 1, rows), :] + line_ref[k, pl.ds(start + 1, rows), :]
+                value = line_ref[k, pl.ds(start, rows), :] + 0.5 * near
                 inward = jnp.where(at_canister, 0.0, turn(value, 1))
                 outward = jnp.where(at_compact, 0.0, turn(value, -1))
                 line.append(value + 0.5 * (inward + outward))
@@ -342,7 +342,7 @@
         ]
         sums = box_sum(packed)
         if cond_sums is None:
-            cond_sums = [[turn(total_sum, -field) for total_sum in line] for line in sums]
+            cond_sums = [[turn(total_sum, -width) for total_sum in line] for line in sums]
         fresh = []
         for s in range(sections):
             line = []
@@ -350,7 +350,7 @@
                 value = values[s][k]
                 total_sum = sums[s][k]
                 change = conds[s][k] * (total_sum - weight * value)
-                change = change + turn(total_sum, -2 * field) - value * cond_sums[s][k]
+                change = change + turn(total_sum, -2 * width) - value * cond_sums[s][k]
                 back = pltpu.roll(gain[s], (face_lane - 2 * k + LANES) % LANES, 1)
                 temp = value + FLUX_STEP * change + jnp.where(at_face, back, 0.0)
                 line.append(jnp.where(is_temp, keep_temp * temp, value))
@@ -359,15 +359,13 @@
 
     per_row = 8 // sizes.layers
     for s in range(sections):
-        order = dealt[s][0][:, 2 * field + 2 : 2 * field + 3].astype(jnp.int32)
+        order = dealt[s][0][:, sizes.extra_at + 2 : sizes.extra_at + 3].astype(jnp.int32)
         order = jnp.broadcast_to(order, shape)
         for half in range(sizes.depth // 8):
             merged = jnp.zeros(shape, jnp.float32)
             for k in range(per_row):
-                for layer in range(sizes.layers):
-                    spot = (k * sizes.layers + layer) * sizes.chunk
-                    moved = turn(values[s][half * per_row + k], spot - layer * width - HALO)
-                    merged = jnp.where(lane // sizes.chunk == spot // sizes.chunk, moved, merged)
+                moved = turn(values[s][half * per_row + k], k * sizes.chunk - HALO)
+                merged = jnp.where(spot_in_layer // sizes.chunk == k, moved, merged)
             chosen = jnp.take_along_axis(merged, order, axis=0)
             start = s * rows * (sizes.depth // 8) + half
             out_ref[pl.ds(start, rows, stride=sizes.depth // 8), :] = chosen
@@ -388,10 +386,13 @@
     tiles = sizes.tiles
     halves = sizes.depth // 8
     active = active_ref[0, 0]
+    sub = iota((8, LANES), 0)
+    natural = sub % sizes.layers * (8 // sizes.layers) + sub // sizes.layers
     for tile in range(tiles):
         for element in range(halves):
             source = pl.ds(tile * 8 * halves + element, 8, stride=halves)
             mech_temp = swap_blocks(temps_ref[source, :], sizes.chunk)
+            mech_temp = jnp.take_along_axis(mech_temp, natural, axis=0)
             spot = pl.ds(element * 8 * tiles + tile, 8, stride=tiles)
             trial = trial_ref[spot, :]
             rate = CREEP_RATE * jnp.exp(-ACTIVATION / (mech_temp + REFERENCE_TEMP))
@@ -467,7 +468,7 @@
         sizes,
         (near(sizes.devices * halves, LANES),),
         [pltpu.VMEM],
-        [],
+        [pltpu.VMEM((sizes.members, rows * (sizes.sections + 2), LANES), jnp.float32)],
         (dealt,),
     )
     temps = temps.reshape(sizes.devices, halves, LANES)

time: 29.4 us -> 29.4 us (level)
  no operation moved by 1% of the time
where the time goes in v7:
time: 29.4 us; the launch traced here: 29.1 us
  blocking collectives  14.9 us (51%)
  waiting for transfers between devices  6.54 us (22%)
  Pallas kernels  3.74 us (13%)
  starting transfers between devices  2.7 us (9%)
  between operations  1.3 us (4%)
    all_to_all x1, blocking collectives, on_device(): lax.all_to_all(dealt, EVERYONE, split_axis=0, concat_axis=0, tiled=True)  14.9 us
    all_to_all x1, waiting for transfers between devices, on_device(): lax.all_to_all(temps, EVERYONE, split_axis=0, concat_axis=0, tiled=True)  6.54 us
    pallas_call x3, Pallas kernels, kernel_call(): pl.pallas_call(functools.partial(body, sizes), out_shape=out_shape, in_sp...  3.74 us
    all_to_all x1, starting transfers between devices, on_device(): lax.all_to_all(temps, EVERYONE, split_axis=0, concat_axis=0, tiled=True)  2.7 us
  transfers between devices with their start and end apart: 1, of which 1 were waited for; matrix products, arithmetic and copies ran while one was open for 0% of the time, Pallas kernels for 0%

profile of v7, /device:TPU:0, one launch (start us, length us, event | category | flops | bytes accessed | tf_op | source)
XLA Modules:
  0.0 29.1 jit_solution(3351920026641369524)
XLA Ops:
  0.6 1.0 %shard_map.86 = f32[32,8,128]{2,1,0:T(8,128)S(1)} custom-call(s32[8]{0:T(128)} %partner_hbm.1, s32[1,8]{1,0:T(1,128)} %order_hbm.1, f32[2,1,8]{2,1,0:T(1,128)} %gap_hbm.1, f32[2,1,8,512]{3,2,1,0:T(8,128)} %temp_hbm.1, f32[2,1,8,512]{3,2,1,0:T(8,128)} %cond_hbm.1), custom_call_target="tpu_custom_call" | custom-call | tf_op jit(solution)/shard_map/pallas_call | solution.py:417
  1.7 14.9 %all_to_all.10.dealt_ref = f32[32,8,128]{2,1,0:T(8,128)S(1)} all-to-all(f32[32,8,128]{2,1,0:T(8,128)S(1)} %shard_map.86), channel_id=1, replica_groups=mesh['slab'=2,'iface'=4,'mech'=4] {'iface','slab','mech'}, dimensions={0} | all-to-all | bytes 262144 | tf_op jit(solution)/shard_map/all_to_all | solution.py:464
  16.5 1.8 %shard_map.87 = f32[64,128]{1,0:T(8,128)} custom-call(f32[32,8,128]{2,1,0:T(8,128)S(1)} %all_to_all.10.dealt_ref), custom_call_target="tpu_custom_call" | custom-call | tf_op jit(solution)/shard_map/pallas_call | solution.py:417
  18.3 0.0 copy-start
  18.3 2.7 %all-to-all-start.1 = ((f32[32,2,128]{2,1,0:T(2,128)}), f32[32,2,128]{2,1,0:T(2,128)S(1)}, u32[]{:S(2)}, u32[]{:S(2)}) async-start(f32[32,2,128]{2,1,0:T(2,128)} %bitcast), calls=%async_computation.1 | async-start | bytes 65536 | tf_op jit(solution)/shard_map/all_to_all | solution.py:475
  21.7 6.5 %all-to-all-done.1 = f32[32,2,128]{2,1,0:T(2,128)S(1)} async-done(((f32[32,2,128]{2,1,0:T(2,128)}), f32[32,2,128]{2,1,0:T(2,128)S(1)}, u32[]{:S(2)}, u32[]{:S(2)}) %all-to-all-start.1) | async-done | bytes 32800 | tf_op jit(solution)/shard_map/all_to_all | solution.py:475
  28.2 0.0 copy-done
  28.2 0.9 %shard_map.88 = (f32[64,128]{1,0:T(8,128)}, f32[8,128]{1,0:T(8,128)}) custom-call(s32[1,1]{1,0:T(1,128)S(6)} %copy.11.active_ref, f32[64,128]{1,0:T(8,128)S(1)} %bitcast.5, f32[64,128]{1,0:T(8,128)S(1)} %bitcast.6), custom_call_target="tpu_custom_call" | custom-call | tf_op jit(solution)/shard_map/pallas_call | solution.py:417
Async XLA Ops:
  18.3 9.9 %copy-start = (f32[16,1,1,512]{3,2,1,0:T(1,128)S(1)}, f32[16,1,1,512]{3,2,1,0:T(1,128)}, u32[]{:S(2)}) copy-start(f32[16,1,1,512]{3,2,1,0:T(1,128)} %param.13) | copy-start | bytes 98308
  18.3 9.9 %all-to-all-start.1 = ((f32[32,2,128]{2,1,0:T(2,128)}), f32[32,2,128]{2,1,0:T(2,128)S(1)}, u32[]{:S(2)}, u32[]{:S(2)}) async-start(f32[32,2,128]{2,1,0:T(2,128)} %bitcast), calls=%async_computation.1 | async-start | bytes 65536 | tf_op jit(solution)/shard_map/all_to_all | solution.py:475

commit v8 on v7

--- a/solution.py
+++ b/solution.py
@@ -212,9 +212,9 @@
     blocks = [
         (
             layer * sizes.layer_lanes + field * sizes.width,
-            [ref[layer, 0, :, pl.ds(tile * LANES, LANES)] for tile in range(sizes.tiles)],
+            [scale * ref[layer, 0, :, pl.ds(tile * LANES, LANES)] for tile in range(sizes.tiles)],
         )
-        for field, ref in enumerate((temp_ref, cond_ref))
+        for field, (ref, scale) in enumerate(((temp_ref, 1.0), (cond_ref, FLUX_STEP)))
         for layer in range(sizes.layers)
     ]
     for device in range(sizes.devices):
@@ -246,11 +246,11 @@
     lower_layer = lane < half_lanes
     at_compact = radius == sizes.gap_row - 1
     at_canister = radius == sizes.gap_row
-    in_grid = (radius >= 0) & (radius < sizes.radial)
     weight = jnp.where(at_compact | at_canister, 6.0, 8.0)
     is_temp = spot_in_layer < width
-    at_face = is_temp & (at_compact | at_canister)
-    keep_temp = jnp.where(is_temp & in_grid, 1.0, 0.0)
+    at_face = jnp.where(is_temp & (at_compact | at_canister), 1.0, 0.0)
+    from_inward = jnp.where(at_canister | (radius == 0), 0.0, 0.5)
+    from_outward = jnp.where(at_compact | (radius == sizes.radial - 1), 0.0, 0.5)
     face_lane = sizes.gap_row - 1 - first
 
     def turn(value, shift):
@@ -284,22 +284,30 @@
     )
     met_by = meets.T[:total, :total]
     meets = meets[:total, :total]
-    both = jnp.concatenate([meets, met_by], axis=0)
+    both = jnp.concatenate([meets, met_by], axis=0).astype(jnp.bfloat16)
+    third = 2 * members
 
     def pick(table, strip):
-        return jnp.dot(
-            table, strip, precision=lax.Precision.HIGHEST, preferred_element_type=jnp.float32
+        rest = strip
+        parts = jnp.zeros(strip.shape, jnp.float32)
+        for index in range(3):
+            part = rest.astype(jnp.bfloat16).astype(jnp.float32)
+            rest = rest - part
+            parts = parts + (turn(part, index * third) if index else part)
+        picked = jnp.dot(
+            table, parts.astype(jnp.bfloat16), preferred_element_type=jnp.float32
         )
+        return picked + turn(picked, -third) + turn(picked, -2 * third)
 
     wide_odd = jnp.concatenate([odd] * sections, axis=0)
     gap = strip_of(dealt, LANES + 1 - sizes.extra_at)
-    gap = jnp.where(wide_odd, gap, turn(pick(met_by, gap), -1))
+    gap = FLUX_STEP * jnp.where(wide_odd, gap, turn(pick(both[total:], gap), -1))
 
     def gains(values):
         strip = strip_of(values, LANES - face_lane)
         met = pick(both, strip)
         met = jnp.where(wide_odd, turn(met[:total], 1), turn(met[total:], -1))
-        gain = FLUX_STEP * gap * (met - strip)
+        gain = gap * (met - strip)
         return [gain[s * rows : (s + 1) * rows] for s in range(sections)]
 
     conds = [[turn(value, -width) for value in line] for line in dealt]
@@ -326,14 +334,12 @@
                 start = rows + s * rows
                 near = line_ref[k, pl.ds(start - 1, rows), :] + line_ref[k, pl.ds(start + 1, rows), :]
                 value = line_ref[k, pl.ds(start, rows), :] + 0.5 * near
-                inward = jnp.where(at_canister, 0.0, turn(value, 1))
-                outward = jnp.where(at_compact, 0.0, turn(value, -1))
-                line.append(value + 0.5 * (inward + outward))
+                line.append(value + from_inward * turn(value, 1) + from_outward * turn(value, -1))
             result.append(line)
         return result
 
     values = dealt
-    cond_sums = None
+    keeps = None
     for sweep in range(SWEEPS):
         gain = gains(values)
         packed = [
@@ -341,19 +347,19 @@
             for lines in zip(values, conds)
         ]
         sums = box_sum(packed)
-        if cond_sums is None:
-            cond_sums = [[turn(total_sum, -width) for total_sum in line] for line in sums]
+        if keeps is None:
+            keeps = [
+                [1.0 - weight * cond - turn(total_sum, -width) for cond, total_sum in zip(*lines)]
+                for lines in zip(conds, sums)
+            ]
         fresh = []
         for s in range(sections):
             line = []
             for k in range(members):
-                value = values[s][k]
-                total_sum = sums[s][k]
-                change = conds[s][k] * (total_sum - weight * value)
-                change = change + turn(total_sum, -2 * width) - value * cond_sums[s][k]
+                temp = values[s][k] * keeps[s][k] + conds[s][k] * sums[s][k]
+                temp = temp + turn(sums[s][k], -2 * width)
                 back = pltpu.roll(gain[s], (face_lane - 2 * k + LANES) % LANES, 1)
-                temp = value + FLUX_STEP * change + jnp.where(at_face, back, 0.0)
-                line.append(jnp.where(is_temp, keep_temp * temp, value))
+                line.append(temp + at_face * back)
             fresh.append(line)
         values = fresh
 

time: 29.4 us -> 29.8 us (1.014)
  Pallas kernels: 3.74 us -> 4.08 us
    pallas_call x3, Pallas kernels: 3.74 us -> 4.08 us  [kernel_call(): pl.pallas_call(functools.partial(body, sizes), out_shape=out_shape, in_sp...]
where the time goes in v8:
time: 29.8 us; the launch traced here: 29.5 us
  blocking collectives  14.9 us (50%)
  waiting for transfers between devices  6.54 us (22%)
  Pallas kernels  4.08 us (14%)
  starting transfers between devices  2.7 us (9%)
  between operations  1.3 us (4%)
    all_to_all x1, blocking collectives, on_device(): lax.all_to_all(dealt, EVERYONE, split_axis=0, concat_axis=0, tiled=True)  14.9 us
    all_to_all x1, waiting for transfers between devices, on_device(): lax.all_to_all(temps, EVERYONE, split_axis=0, concat_axis=0, tiled=True)  6.54 us
    pallas_call x3, Pallas kernels, kernel_call(): pl.pallas_call(functools.partial(body, sizes), out_shape=out_shape, in_sp...  4.08 us
    all_to_all x1, starting transfers between devices, on_device(): lax.all_to_all(temps, EVERYONE, split_axis=0, concat_axis=0, tiled=True)  2.7 us
  transfers between devices with their start and end apart: 1, of which 1 were waited for; matrix products, arithmetic and copies ran while one was open for 0% of the time, Pallas kernels for 0%

profile of v8, /device:TPU:0, one launch (start us, length us, event | category | flops | bytes accessed | tf_op | source)
XLA Modules:
  0.0 29.5 jit_solution(10757357150264637767)
XLA Ops:
  0.6 1.0 %shard_map.86 = f32[32,8,128]{2,1,0:T(8,128)S(1)} custom-call(s32[8]{0:T(128)} %partner_hbm.1, s32[1,8]{1,0:T(1,128)} %order_hbm.1, f32[2,1,8]{2,1,0:T(1,128)} %gap_hbm.1, f32[2,1,8,512]{3,2,1,0:T(8,128)} %temp_hbm.1, f32[2,1,8,512]{3,2,1,0:T(8,128)} %cond_hbm.1), custom_call_target="tpu_custom_call" | custom-call | tf_op jit(solution)/shard_map/pallas_call | solution.py:423
  1.7 14.9 %all_to_all.10.dealt_ref = f32[32,8,128]{2,1,0:T(8,128)S(1)} all-to-all(f32[32,8,128]{2,1,0:T(8,128)S(1)} %shard_map.86), channel_id=1, replica_groups=mesh['slab'=2,'iface'=4,'mech'=4] {'iface','slab','mech'}, dimensions={0} | all-to-all | bytes 262144 | tf_op jit(solution)/shard_map/all_to_all | solution.py:470
  16.5 2.1 %shard_map.87 = f32[64,128]{1,0:T(8,128)} custom-call(f32[32,8,128]{2,1,0:T(8,128)S(1)} %all_to_all.10.dealt_ref), custom_call_target="tpu_custom_call" | custom-call | tf_op jit(solution)/shard_map/pallas_call | solution.py:423
  18.7 0.0 copy-start
  18.7 2.7 %all-to-all-start.1 = ((f32[32,2,128]{2,1,0:T(2,128)}), f32[32,2,128]{2,1,0:T(2,128)S(1)}, u32[]{:S(2)}, u32[]{:S(2)}) async-start(f32[32,2,128]{2,1,0:T(2,128)} %bitcast), calls=%async_computation.1 | async-start | bytes 65536 | tf_op jit(solution)/shard_map/all_to_all | solution.py:481
  22.0 6.5 %all-to-all-done.1 = f32[32,2,128]{2,1,0:T(2,128)S(1)} async-done(((f32[32,2,128]{2,1,0:T(2,128)}), f32[32,2,128]{2,1,0:T(2,128)S(1)}, u32[]{:S(2)}, u32[]{:S(2)}) %all-to-all-start.1) | async-done | bytes 32800 | tf_op jit(solution)/shard_map/all_to_all | solution.py:481
  28.6 0.0 copy-done
  28.6 0.9 %shard_map.88 = (f32[64,128]{1,0:T(8,128)}, f32[8,128]{1,0:T(8,128)}) custom-call(s32[1,1]{1,0:T(1,128)S(6)} %copy.11.active_ref, f32[64,128]{1,0:T(8,128)S(1)} %bitcast.5, f32[64,128]{1,0:T(8,128)S(1)} %bitcast.6), custom_call_target="tpu_custom_call" | custom-call | tf_op jit(solution)/shard_map/pallas_call | solution.py:423
Async XLA Ops:
  18.7 9.9 %copy-start = (f32[16,1,1,512]{3,2,1,0:T(1,128)S(1)}, f32[16,1,1,512]{3,2,1,0:T(1,128)}, u32[]{:S(2)}) copy-start(f32[16,1,1,512]{3,2,1,0:T(1,128)} %param.13) | copy-start | bytes 98308
  18.7 9.9 %all-to-all-start.1 = ((f32[32,2,128]{2,1,0:T(2,128)}), f32[32,2,128]{2,1,0:T(2,128)S(1)}, u32[]{:S(2)}, u32[]{:S(2)}) async-start(f32[32,2,128]{2,1,0:T(2,128)} %bitcast), calls=%async_computation.1 | async-start | bytes 65536 | tf_op jit(solution)/shard_map/all_to_all | solution.py:481

commit v9 on v5

--- a/solution.py
+++ b/solution.py
@@ -127,7 +127,7 @@
 
 LANES = 128
 HALO = 2
-EVERYONE = ("iface", "slab", "mech")
+EVERYONE = ("slab", "mech", "iface")
 
 
 def iota(shape, axis):
@@ -234,8 +234,8 @@
     shape = (rows, LANES)
     lane = iota(shape, 1)
     sub = iota(shape, 0)
-    place = lax.axis_index("iface") * members
-    place = place + lax.axis_index("slab") * lax.axis_size("mech") + lax.axis_index("mech")
+    place = lax.axis_index("slab") * lax.axis_size("mech") + lax.axis_index("mech")
+    place = place * sections + lax.axis_index("iface")
     first = place * sizes.chunk - HALO
     segment = lane // width
     radius = first + lane % width
@@ -252,7 +252,7 @@
     def turn(value, shift):
         return pltpu.roll(value, shift % LANES, 1)
 
-    dealt = [[dealt_ref[s * members + k] for k in range(members)] for s in range(sections)]
+    dealt = [[dealt_ref[k * sections + s] for k in range(members)] for s in range(sections)]
 
     strip_lane = (lane < 2 * members) | ((lane >= width) & (lane < width + 2 * members))
     odd = (lane % width) % 2 == 1
@@ -369,8 +369,8 @@
                     moved = turn(values[s][half * per_row + k], spot - layer * width - HALO)
                     merged = jnp.where(lane // sizes.chunk == spot // sizes.chunk, moved, merged)
             chosen = jnp.take_along_axis(merged, order, axis=0)
-            start = s * rows * (sizes.depth // 8) + half
-            out_ref[pl.ds(start, rows, stride=sizes.depth // 8), :] = chosen
+            start = s * (sizes.depth // 8) + half
+            out_ref[pl.ds(start, rows, stride=sections * (sizes.depth // 8)), :] = chosen
 
 
 def swap_blocks(tile, block):

time: 29.4 us -> 30 us (1.020)
  blocking collectives: 14.9 us -> 15.3 us
    all_to_all x1, blocking collectives: 14.9 us -> 15.3 us  [on_device(): lax.all_to_all(dealt, EVERYONE, split_axis=0, concat_axis=0, tiled=True)]
where the time goes in v9:
time: 30 us; the launch traced here: 29.7 us
  blocking collectives  15.3 us (51%)
  waiting for transfers between devices  6.6 us (22%)
  Pallas kernels  3.75 us (12%)
  starting transfers between devices  2.7 us (9%)
  between operations  1.3 us (4%)
    all_to_all x1, blocking collectives, on_device(): lax.all_to_all(dealt, EVERYONE, split_axis=0, concat_axis=0, tiled=True)  15.3 us
    all_to_all x1, waiting for transfers between devices, on_device(): lax.all_to_all(temps, EVERYONE, split_axis=0, concat_axis=0, tiled=True)  6.6 us
    pallas_call x3, Pallas kernels, kernel_call(): pl.pallas_call(functools.partial(body, sizes), out_shape=out_shape, in_sp...  3.75 us
    all_to_all x1, starting transfers between devices, on_device(): lax.all_to_all(temps, EVERYONE, split_axis=0, concat_axis=0, tiled=True)  2.7 us
  transfers between devices with their start and end apart: 1, of which 1 were waited for; matrix products, arithmetic and copies ran while one was open for 0% of the time, Pallas kernels for 0%

profile of v9, /device:TPU:0, one launch (start us, length us, event | category | flops | bytes accessed | tf_op | source)
XLA Modules:
  0.0 29.7 jit_solution(15112413880842520835)
XLA Ops:
  0.6 1.0 %shard_map.86 = f32[32,8,128]{2,1,0:T(8,128)S(1)} custom-call(s32[8]{0:T(128)} %partner_hbm.1, s32[1,8]{1,0:T(1,128)} %order_hbm.1, f32[2,1,8]{2,1,0:T(1,128)} %gap_hbm.1, f32[2,1,8,512]{3,2,1,0:T(8,128)} %temp_hbm.1, f32[2,1,8,512]{3,2,1,0:T(8,128)} %cond_hbm.1), custom_call_target="tpu_custom_call" | custom-call | tf_op jit(solution)/shard_map/pallas_call | solution.py:416
  1.7 15.3 %all_to_all.10.dealt_ref = f32[32,8,128]{2,1,0:T(8,128)S(1)} all-to-all(f32[32,8,128]{2,1,0:T(8,128)S(1)} %shard_map.86), channel_id=1, replica_groups=mesh['slab'=2,'iface'=4,'mech'=4] {'slab','mech','iface'}, dimensions={0} | all-to-all | bytes 262144 | tf_op jit(solution)/shard_map/all_to_all | solution.py:463
  17.0 1.8 %shard_map.87 = f32[64,128]{1,0:T(8,128)} custom-call(f32[32,8,128]{2,1,0:T(8,128)S(1)} %all_to_all.10.dealt_ref), custom_call_target="tpu_custom_call" | custom-call | tf_op jit(solution)/shard_map/pallas_call | solution.py:416
  18.8 0.0 copy-start
  18.8 2.7 %all-to-all-start.1 = ((f32[32,2,128]{2,1,0:T(2,128)}), f32[32,2,128]{2,1,0:T(2,128)S(1)}, u32[]{:S(2)}, u32[]{:S(2)}) async-start(f32[32,2,128]{2,1,0:T(2,128)} %bitcast), calls=%async_computation.1 | async-start | bytes 65536 | tf_op jit(solution)/shard_map/all_to_all | solution.py:474
  22.2 6.6 %all-to-all-done.1 = f32[32,2,128]{2,1,0:T(2,128)S(1)} async-done(((f32[32,2,128]{2,1,0:T(2,128)}), f32[32,2,128]{2,1,0:T(2,128)S(1)}, u32[]{:S(2)}, u32[]{:S(2)}) %all-to-all-start.1) | async-done | bytes 32800 | tf_op jit(solution)/shard_map/all_to_all | solution.py:474
  28.8 0.0 copy-done
  28.8 0.9 %shard_map.88 = (f32[64,128]{1,0:T(8,128)}, f32[8,128]{1,0:T(8,128)}) custom-call(s32[1,1]{1,0:T(1,128)S(6)} %copy.11.active_ref, f32[64,128]{1,0:T(8,128)S(1)} %bitcast.5, f32[64,128]{1,0:T(8,128)S(1)} %bitcast.6), custom_call_target="tpu_custom_call" | custom-call | tf_op jit(solution)/shard_map/pallas_call | solution.py:416
Async XLA Ops:
  18.8 10.0 %copy-start = (f32[16,1,1,512]{3,2,1,0:T(1,128)S(1)}, f32[16,1,1,512]{3,2,1,0:T(1,128)}, u32[]{:S(2)}) copy-start(f32[16,1,1,512]{3,2,1,0:T(1,128)} %param.13) | copy-start | bytes 98308
  18.8 10.0 %all-to-all-start.1 = ((f32[32,2,128]{2,1,0:T(2,128)}), f32[32,2,128]{2,1,0:T(2,128)S(1)}, u32[]{:S(2)}, u32[]{:S(2)}) async-start(f32[32,2,128]{2,1,0:T(2,128)} %bitcast), calls=%async_computation.1 | async-start | bytes 65536 | tf_op jit(solution)/shard_map/all_to_all | solution.py:474

commit v10 on v9

--- a/solution.py
+++ b/solution.py
@@ -127,7 +127,7 @@
 
 LANES = 128
 HALO = 2
-EVERYONE = ("slab", "mech", "iface")
+EVERYONE = ("slab", "iface", "mech")
 
 
 def iota(shape, axis):
@@ -234,8 +234,13 @@
     shape = (rows, LANES)
     lane = iota(shape, 1)
     sub = iota(shape, 0)
-    place = lax.axis_index("slab") * lax.axis_size("mech") + lax.axis_index("mech")
-    place = place * sections + lax.axis_index("iface")
+    per_slab = lax.axis_size("mech")
+
+    def number(section, member):
+        return (member // per_slab * sections + section) * per_slab + member % per_slab
+
+    place = lax.axis_index("slab") * sections + lax.axis_index("iface")
+    place = place * per_slab + lax.axis_index("mech")
     first = place * sizes.chunk - HALO
     segment = lane // width
     radius = first + lane % width
@@ -252,7 +257,7 @@
     def turn(value, shift):
         return pltpu.roll(value, shift % LANES, 1)
 
-    dealt = [[dealt_ref[k * sections + s] for k in range(members)] for s in range(sections)]
+    dealt = [[dealt_ref[number(s, k)] for k in range(members)] for s in range(sections)]
 
     strip_lane = (lane < 2 * members) | ((lane >= width) & (lane < width + 2 * members))
     odd = (lane % width) % 2 == 1
@@ -369,8 +374,10 @@
                     moved = turn(values[s][half * per_row + k], spot - layer * width - HALO)
                     merged = jnp.where(lane // sizes.chunk == spot // sizes.chunk, moved, merged)
             chosen = jnp.take_along_axis(merged, order, axis=0)
-            start = s * (sizes.depth // 8) + half
-            out_ref[pl.ds(start, rows, stride=sections * (sizes.depth // 8)), :] = chosen
+            halves = sizes.depth // 8
+            for row in range(0, rows, per_slab):
+                start = number(s, row) * halves + half
+                out_ref[pl.ds(start, per_slab, stride=halves), :] = chosen[row : row + per_slab]
 
 
 def swap_blocks(tile, block):

time: 30 us -> 30.2 us (level)
  no operation moved by 1% of the time
where the time goes in v10:
time: 30.2 us; the launch traced here: 29.9 us
  blocking collectives  15.5 us (51%)
  waiting for transfers between devices  6.65 us (22%)
  Pallas kernels  3.75 us (12%)
  starting transfers between devices  2.7 us (9%)
  between operations  1.3 us (4%)
    all_to_all x1, blocking collectives, on_device(): lax.all_to_all(dealt, EVERYONE, split_axis=0, concat_axis=0, tiled=True)  15.5 us
    all_to_all x1, waiting for transfers between devices, on_device(): lax.all_to_all(temps, EVERYONE, split_axis=0, concat_axis=0, tiled=True)  6.65 us
    pallas_call x3, Pallas kernels, kernel_call(): pl.pallas_call(functools.partial(body, sizes), out_shape=out_shape, in_sp...  3.75 us
    all_to_all x1, starting transfers between devices, on_device(): lax.all_to_all(temps, EVERYONE, split_axis=0, concat_axis=0, tiled=True)  2.7 us
  transfers between devices with their start and end apart: 1, of which 1 were waited for; matrix products, arithmetic and copies ran while one was open for 0% of the time, Pallas kernels for 0%

profile of v10, /device:TPU:0, one launch (start us, length us, event | category | flops | bytes accessed | tf_op | source)
XLA Modules:
  0.0 29.9 jit_solution(3365982383206278583)
XLA Ops:
  0.6 1.0 %shard_map.86 = f32[32,8,128]{2,1,0:T(8,128)S(1)} custom-call(s32[8]{0:T(128)} %partner_hbm.1, s32[1,8]{1,0:T(1,128)} %order_hbm.1, f32[2,1,8]{2,1,0:T(1,128)} %gap_hbm.1, f32[2,1,8,512]{3,2,1,0:T(8,128)} %temp_hbm.1, f32[2,1,8,512]{3,2,1,0:T(8,128)} %cond_hbm.1), custom_call_target="tpu_custom_call" | custom-call | tf_op jit(solution)/shard_map/pallas_call | solution.py:423
  1.7 15.5 %all_to_all.10.dealt_ref = f32[32,8,128]{2,1,0:T(8,128)S(1)} all-to-all(f32[32,8,128]{2,1,0:T(8,128)S(1)} %shard_map.86), channel_id=1, replica_groups=mesh['slab'=2,'iface'=4,'mech'=4] {'slab','iface','mech'}, dimensions={0} | all-to-all | bytes 262144 | tf_op jit(solution)/shard_map/all_to_all | solution.py:470
  17.2 1.8 %shard_map.87 = f32[64,128]{1,0:T(8,128)} custom-call(f32[32,8,128]{2,1,0:T(8,128)S(1)} %all_to_all.10.dealt_ref), custom_call_target="tpu_custom_call" | custom-call | tf_op jit(solution)/shard_map/pallas_call | solution.py:423
  19.0 0.0 copy-start
  19.0 2.7 %all-to-all-start.1 = ((f32[32,2,128]{2,1,0:T(2,128)}), f32[32,2,128]{2,1,0:T(2,128)S(1)}, u32[]{:S(2)}, u32[]{:S(2)}) async-start(f32[32,2,128]{2,1,0:T(2,128)} %bitcast), calls=%async_computation.1 | async-start | bytes 65536 | tf_op jit(solution)/shard_map/all_to_all | solution.py:481
  22.3 6.6 %all-to-all-done.1 = f32[32,2,128]{2,1,0:T(2,128)S(1)} async-done(((f32[32,2,128]{2,1,0:T(2,128)}), f32[32,2,128]{2,1,0:T(2,128)S(1)}, u32[]{:S(2)}, u32[]{:S(2)}) %all-to-all-start.1) | async-done | bytes 32800 | tf_op jit(solution)/shard_map/all_to_all | solution.py:481
  29.0 0.0 copy-done
  29.0 0.9 %shard_map.88 = (f32[64,128]{1,0:T(8,128)}, f32[8,128]{1,0:T(8,128)}) custom-call(s32[1,1]{1,0:T(1,128)S(6)} %copy.11.active_ref, f32[64,128]{1,0:T(8,128)S(1)} %bitcast.5, f32[64,128]{1,0:T(8,128)S(1)} %bitcast.6), custom_call_target="tpu_custom_call" | custom-call | tf_op jit(solution)/shard_map/pallas_call | solution.py:423
Async XLA Ops:
  19.0 10.0 %copy-start = (f32[16,1,1,512]{3,2,1,0:T(1,128)S(1)}, f32[16,1,1,512]{3,2,1,0:T(1,128)}, u32[]{:S(2)}) copy-start(f32[16,1,1,512]{3,2,1,0:T(1,128)} %param.13) | copy-start | bytes 98308
  19.0 10.0 %all-to-all-start.1 = ((f32[32,2,128]{2,1,0:T(2,128)}), f32[32,2,128]{2,1,0:T(2,128)S(1)}, u32[]{:S(2)}, u32[]{:S(2)}) async-start(f32[32,2,128]{2,1,0:T(2,128)} %bitcast), calls=%async_computation.1 | async-start | bytes 65536 | tf_op jit(solution)/shard_map/all_to_all | solution.py:481

commit v11 on v5

--- a/solution.py
+++ b/solution.py
@@ -204,7 +204,7 @@
         spot = (sub == row) & (lane == extra_at + 1)
         extra = jnp.where(spot, partner_ref[row].astype(jnp.float32), extra)
         spot = (sub == row) & (lane == extra_at + 2)
-        extra = jnp.where(spot, order_ref[0, row].astype(jnp.float32), extra)
+        extra = jnp.where(spot, order_ref[0, sizes.rows - 1 - row].astype(jnp.float32), extra)
     for copy in copies[3:]:
         copy.wait()
     blocks = [
@@ -236,6 +236,7 @@
     sub = iota(shape, 0)
     place = lax.axis_index("iface") * members
     place = place + lax.axis_index("slab") * lax.axis_size("mech") + lax.axis_index("mech")
+    place = sizes.devices - 1 - place
     first = place * sizes.chunk - HALO
     segment = lane // width
     radius = first + lane % width
@@ -252,7 +253,7 @@
     def turn(value, shift):
         return pltpu.roll(value, shift % LANES, 1)
 
-    dealt = [[dealt_ref[s * members + k] for k in range(members)] for s in range(sections)]
+    dealt = [[dealt_ref[sizes.devices - 1 - s * members - k] for k in range(members)] for s in range(sections)]
 
     strip_lane = (lane < 2 * members) | ((lane >= width) & (lane < width + 2 * members))
     odd = (lane % width) % 2 == 1
@@ -369,7 +370,7 @@
                     moved = turn(values[s][half * per_row + k], spot - layer * width - HALO)
                     merged = jnp.where(lane // sizes.chunk == spot // sizes.chunk, moved, merged)
             chosen = jnp.take_along_axis(merged, order, axis=0)
-            start = s * rows * (sizes.depth // 8) + half
+            start = (sizes.devices - (s + 1) * rows) * (sizes.depth // 8) + half
             out_ref[pl.ds(start, rows, stride=sizes.depth // 8), :] = chosen
 
 
@@ -423,6 +424,17 @@
     )(*pinned)
 
 
+def exchanged(parts, sizes):
+    return lax.all_to_all(
+        parts,
+        EVERYONE,
+        split_axis=0,
+        concat_axis=0,
+        tiled=True,
+        axis_index_groups=[list(range(sizes.devices - 1, -1, -1))],
+    )
+
+
 def on_device(
     temp_start, conductivity, gap_conductance, partner, row_order, active_layers, trial_stress
 ):
@@ -460,7 +472,7 @@
         ],
         (partner, row_order, gap_conductance, temp_start, conductivity),
     )
-    dealt = lax.all_to_all(dealt, EVERYONE, split_axis=0, concat_axis=0, tiled=True)
+    dealt = exchanged(dealt, sizes)
     halves = sizes.depth // 8
     (temps,) = kernel_call(
         sweep_kernel,
@@ -471,7 +483,7 @@
         (dealt,),
     )
     temps = temps.reshape(sizes.devices, halves, LANES)
-    temps = lax.all_to_all(temps, EVERYONE, split_axis=0, concat_axis=0, tiled=True)
+    temps = exchanged(temps, sizes)
     stress, strain = kernel_call(
         creep_kernel,
         sizes,

time: 29.4 us -> 30.2 us (1.027)
  blocking collectives: 14.9 us -> 15.5 us
    all_to_all x1, blocking collectives: 14.9 us -> 15.5 us  [exchanged(): lax.all_to_all(parts, EVERYONE, split_axis=0, concat_axis=0, tiled=True,...]
where the time goes in v11:
time: 30.2 us; the launch traced here: 29.8 us
  blocking collectives  15.5 us (51%)
  waiting for transfers between devices  6.64 us (22%)
  Pallas kernels  3.75 us (12%)
  starting transfers between devices  2.7 us (9%)
  between operations  1.3 us (4%)
    all_to_all x1, blocking collectives, exchanged(): lax.all_to_all(parts, EVERYONE, split_axis=0, concat_axis=0, tiled=True,...  15.5 us
    all_to_all x1, waiting for transfers between devices, exchanged(): lax.all_to_all(parts, EVERYONE, split_axis=0, concat_axis=0, tiled=True,...  6.64 us
    pallas_call x3, Pallas kernels, kernel_call(): pl.pallas_call(functools.partial(body, sizes), out_shape=out_shape, in_sp...  3.75 us
    all_to_all x1, starting transfers between devices, exchanged(): lax.all_to_all(parts, EVERYONE, split_axis=0, concat_axis=0, tiled=True,...  2.7 us
  transfers between devices with their start and end apart: 1, of which 1 were waited for; matrix products, arithmetic and copies ran while one was open for 0% of the time, Pallas kernels for 0%

profile of v11, /device:TPU:0, one launch (start us, length us, event | category | flops | bytes accessed | tf_op | source)
XLA Modules:
  0.0 29.8 jit_solution(16094192642629877230)
XLA Ops:
  0.6 1.0 %shard_map.86 = f32[32,8,128]{2,1,0:T(8,128)S(1)} custom-call(s32[8]{0:T(128)} %partner_hbm.1, s32[1,8]{1,0:T(1,128)} %order_hbm.1, f32[2,1,8]{2,1,0:T(1,128)} %gap_hbm.1, f32[2,1,8,512]{3,2,1,0:T(8,128)} %temp_hbm.1, f32[2,1,8,512]{3,2,1,0:T(8,128)} %cond_hbm.1), custom_call_target="tpu_custom_call" | custom-call | tf_op jit(solution)/shard_map/pallas_call | solution.py:417
  1.7 15.5 %all_to_all.10.dealt_ref = f32[32,8,128]{2,1,0:T(8,128)S(1)} all-to-all(f32[32,8,128]{2,1,0:T(8,128)S(1)} %shard_map.86), channel_id=1, replica_groups={{31,30,29,28,15,14,13,12,27,26,25,24,11,10,9,8,23,22,21,20,7,6,5,4,19,1..., dimensions={0} | all-to-all | bytes 262144 | tf_op jit(solution)/shard_map/all_to_all | solution.py:428
  17.1 1.8 %shard_map.87 = f32[64,128]{1,0:T(8,128)} custom-call(f32[32,8,128]{2,1,0:T(8,128)S(1)} %all_to_all.10.dealt_ref), custom_call_target="tpu_custom_call" | custom-call | tf_op jit(solution)/shard_map/pallas_call | solution.py:417
  18.9 0.0 copy-start
  18.9 2.7 %all-to-all-start.1 = ((f32[32,2,128]{2,1,0:T(2,128)}), f32[32,2,128]{2,1,0:T(2,128)S(1)}, u32[]{:S(2)}, u32[]{:S(2)}) async-start(f32[32,2,128]{2,1,0:T(2,128)} %bitcast), calls=%async_computation.1 | async-start | bytes 65536 | tf_op jit(solution)/shard_map/all_to_all | solution.py:428
  22.3 6.6 %all-to-all-done.1 = f32[32,2,128]{2,1,0:T(2,128)S(1)} async-done(((f32[32,2,128]{2,1,0:T(2,128)}), f32[32,2,128]{2,1,0:T(2,128)S(1)}, u32[]{:S(2)}, u32[]{:S(2)}) %all-to-all-start.1) | async-done | bytes 32800 | tf_op jit(solution)/shard_map/all_to_all | solution.py:428
  28.9 0.0 copy-done
  28.9 0.9 %shard_map.88 = (f32[64,128]{1,0:T(8,128)}, f32[8,128]{1,0:T(8,128)}) custom-call(s32[1,1]{1,0:T(1,128)S(6)} %copy.11.active_ref, f32[64,128]{1,0:T(8,128)S(1)} %bitcast.5, f32[64,128]{1,0:T(8,128)S(1)} %bitcast.6), custom_call_target="tpu_custom_call" | custom-call | tf_op jit(solution)/shard_map/pallas_call | solution.py:417
Async XLA Ops:
  18.9 10.0 %copy-start = (f32[16,1,1,512]{3,2,1,0:T(1,128)S(1)}, f32[16,1,1,512]{3,2,1,0:T(1,128)}, u32[]{:S(2)}) copy-start(f32[16,1,1,512]{3,2,1,0:T(1,128)} %param.13) | copy-start | bytes 98308
  18.9 10.0 %all-to-all-start.1 = ((f32[32,2,128]{2,1,0:T(2,128)}), f32[32,2,128]{2,1,0:T(2,128)S(1)}, u32[]{:S(2)}, u32[]{:S(2)}) async-start(f32[32,2,128]{2,1,0:T(2,128)} %bitcast), calls=%async_computation.1 | async-start | bytes 65536 | tf_op jit(solution)/shard_map/all_to_all | solution.py:428

commit v12 on v10

--- a/solution.py
+++ b/solution.py
@@ -127,7 +127,7 @@
 
 LANES = 128
 HALO = 2
-EVERYONE = ("slab", "iface", "mech")
+EVERYONE = ("mech", "slab", "iface")
 
 
 def iota(shape, axis):
@@ -234,13 +234,13 @@
     shape = (rows, LANES)
     lane = iota(shape, 1)
     sub = iota(shape, 0)
-    per_slab = lax.axis_size("mech")
+    slabs, per_slab = lax.axis_size("slab"), lax.axis_size("mech")
 
     def number(section, member):
-        return (member // per_slab * sections + section) * per_slab + member % per_slab
-
-    place = lax.axis_index("slab") * sections + lax.axis_index("iface")
-    place = place * per_slab + lax.axis_index("mech")
+        return (member % per_slab * slabs + member // per_slab) * sections + section
+
+    place = lax.axis_index("mech") * slabs + lax.axis_index("slab")
+    place = place * sections + lax.axis_index("iface")
     first = place * sizes.chunk - HALO
     segment = lane // width
     radius = first + lane % width
@@ -375,9 +375,10 @@
                     merged = jnp.where(lane // sizes.chunk == spot // sizes.chunk, moved, merged)
             chosen = jnp.take_along_axis(merged, order, axis=0)
             halves = sizes.depth // 8
+            stride = halves * slabs * sections
             for row in range(0, rows, per_slab):
                 start = number(s, row) * halves + half
-                out_ref[pl.ds(start, per_slab, stride=halves), :] = chosen[row : row + per_slab]
+                out_ref[pl.ds(start, per_slab, stride=stride), :] = chosen[row : row + per_slab]
 
 
 def swap_blocks(tile, block):

time: 30.2 us -> 30 us (level)
  no operation moved by 1% of the time
where the time goes in v12:
time: 30 us; the launch traced here: 29.7 us
  blocking collectives  15.3 us (51%)
  waiting for transfers between devices  6.6 us (22%)
  Pallas kernels  3.75 us (12%)
  starting transfers between devices  2.7 us (9%)
  between operations  1.3 us (4%)
    all_to_all x1, blocking collectives, on_device(): lax.all_to_all(dealt, EVERYONE, split_axis=0, concat_axis=0, tiled=True)  15.3 us
    all_to_all x1, waiting for transfers between devices, on_device(): lax.all_to_all(temps, EVERYONE, split_axis=0, concat_axis=0, tiled=True)  6.6 us
    pallas_call x3, Pallas kernels, kernel_call(): pl.pallas_call(functools.partial(body, sizes), out_shape=out_shape, in_sp...  3.75 us
    all_to_all x1, starting transfers between devices, on_device(): lax.all_to_all(temps, EVERYONE, split_axis=0, concat_axis=0, tiled=True)  2.7 us
  transfers between devices with their start and end apart: 1, of which 1 were waited for; matrix products, arithmetic and copies ran while one was open for 0% of the time, Pallas kernels for 0%

profile of v12, /device:TPU:0, one launch (start us, length us, event | category | flops | bytes accessed | tf_op | source)
XLA Modules:
  0.0 29.7 jit_solution(2899482616744539746)
XLA Ops:
  0.6 1.0 %shard_map.86 = f32[32,8,128]{2,1,0:T(8,128)S(1)} custom-call(s32[8]{0:T(128)} %partner_hbm.1, s32[1,8]{1,0:T(1,128)} %order_hbm.1, f32[2,1,8]{2,1,0:T(1,128)} %gap_hbm.1, f32[2,1,8,512]{3,2,1,0:T(8,128)} %temp_hbm.1, f32[2,1,8,512]{3,2,1,0:T(8,128)} %cond_hbm.1), custom_call_target="tpu_custom_call" | custom-call | tf_op jit(solution)/shard_map/pallas_call | solution.py:424
  1.7 15.3 %all_to_all.10.dealt_ref = f32[32,8,128]{2,1,0:T(8,128)S(1)} all-to-all(f32[32,8,128]{2,1,0:T(8,128)S(1)} %shard_map.86), channel_id=1, replica_groups=mesh['slab'=2,'iface'=4,'mech'=4] {'mech','slab','iface'}, dimensions={0} | all-to-all | bytes 262144 | tf_op jit(solution)/shard_map/all_to_all | solution.py:471
  17.0 1.8 %shard_map.87 = f32[64,128]{1,0:T(8,128)} custom-call(f32[32,8,128]{2,1,0:T(8,128)S(1)} %all_to_all.10.dealt_ref), custom_call_target="tpu_custom_call" | custom-call | tf_op jit(solution)/shard_map/pallas_call | solution.py:424
  18.8 0.0 copy-start
  18.8 2.7 %all-to-all-start.1 = ((f32[32,2,128]{2,1,0:T(2,128)}), f32[32,2,128]{2,1,0:T(2,128)S(1)}, u32[]{:S(2)}, u32[]{:S(2)}) async-start(f32[32,2,128]{2,1,0:T(2,128)} %bitcast), calls=%async_computation.1 | async-start | bytes 65536 | tf_op jit(solution)/shard_map/all_to_all | solution.py:482
  22.2 6.6 %all-to-all-done.1 = f32[32,2,128]{2,1,0:T(2,128)S(1)} async-done(((f32[32,2,128]{2,1,0:T(2,128)}), f32[32,2,128]{2,1,0:T(2,128)S(1)}, u32[]{:S(2)}, u32[]{:S(2)}) %all-to-all-start.1) | async-done | bytes 32800 | tf_op jit(solution)/shard_map/all_to_all | solution.py:482
  28.8 0.0 copy-done
  28.8 0.9 %shard_map.88 = (f32[64,128]{1,0:T(8,128)}, f32[8,128]{1,0:T(8,128)}) custom-call(s32[1,1]{1,0:T(1,128)S(6)} %copy.11.active_ref, f32[64,128]{1,0:T(8,128)S(1)} %bitcast.5, f32[64,128]{1,0:T(8,128)S(1)} %bitcast.6), custom_call_target="tpu_custom_call" | custom-call | tf_op jit(solution)/shard_map/pallas_call | solution.py:424
Async XLA Ops:
  18.8 10.0 %copy-start = (f32[16,1,1,512]{3,2,1,0:T(1,128)S(1)}, f32[16,1,1,512]{3,2,1,0:T(1,128)}, u32[]{:S(2)}) copy-start(f32[16,1,1,512]{3,2,1,0:T(1,128)} %param.13) | copy-start | bytes 98308
  18.8 10.0 %all-to-all-start.1 = ((f32[32,2,128]{2,1,0:T(2,128)}), f32[32,2,128]{2,1,0:T(2,128)S(1)}, u32[]{:S(2)}, u32[]{:S(2)}) async-start(f32[32,2,128]{2,1,0:T(2,128)} %bitcast), calls=%async_computation.1 | async-start | bytes 65536 | tf_op jit(solution)/shard_map/all_to_all | solution.py:482

commit v13 on v7

--- a/solution.py
+++ b/solution.py
@@ -358,41 +358,43 @@
         values = fresh
 
     per_row = 8 // sizes.layers
+    skew = place % 8 * sizes.chunk
+    unskewed = (lane - skew + LANES) % half_lanes
     for s in range(sections):
         order = dealt[s][0][:, sizes.extra_at + 2 : sizes.extra_at + 3].astype(jnp.int32)
         order = jnp.broadcast_to(order, shape)
         for half in range(sizes.depth // 8):
             merged = jnp.zeros(shape, jnp.float32)
             for k in range(per_row):
-                moved = turn(values[s][half * per_row + k], k * sizes.chunk - HALO)
-                merged = jnp.where(spot_in_layer // sizes.chunk == k, moved, merged)
+                moved = pltpu.roll(
+                    values[s][half * per_row + k], (k * sizes.chunk - HALO + skew) % LANES, 1
+                )
+                merged = jnp.where(unskewed // sizes.chunk == k, moved, merged)
             chosen = jnp.take_along_axis(merged, order, axis=0)
             start = s * rows * (sizes.depth // 8) + half
             out_ref[pl.ds(start, rows, stride=sizes.depth // 8), :] = chosen
 
 
-def swap_blocks(tile, block):
+def swap_blocks(tile, block, layers):
     sub = iota(tile.shape, 0)
     spot = iota(tile.shape, 1) // block
-    for bit in (4, 2, 1):
-        up = pltpu.roll(pltpu.roll(tile, 8 - bit, 0), bit * block, 1)
-        down = pltpu.roll(pltpu.roll(tile, bit, 0), LANES - bit * block, 1)
-        moved = jnp.where(sub & bit == 0, up, down)
-        tile = jnp.where((sub & bit) == (spot & bit), tile, moved)
-    return tile
+    held = sub % layers * (8 // layers) + sub // layers
+    gathered = jnp.take_along_axis(tile, (spot - held + 8) % 8, axis=0)
+    rolled = [pltpu.roll(gathered, (8 - row) % 8 * block, 1) if row else gathered for row in range(8)]
+    result = rolled[0]
+    for row in range(1, 8):
+        result = jnp.where(held == row, rolled[row], result)
+    return result
 
 
 def creep_kernel(sizes, active_ref, temps_ref, trial_ref, stress_ref, strain_ref):
     tiles = sizes.tiles
     halves = sizes.depth // 8
     active = active_ref[0, 0]
-    sub = iota((8, LANES), 0)
-    natural = sub % sizes.layers * (8 // sizes.layers) + sub // sizes.layers
     for tile in range(tiles):
         for element in range(halves):
             source = pl.ds(tile * 8 * halves + element, 8, stride=halves)
-            mech_temp = swap_blocks(temps_ref[source, :], sizes.chunk)
-            mech_temp = jnp.take_along_axis(mech_temp, natural, axis=0)
+            mech_temp = swap_blocks(temps_ref[source, :], sizes.chunk, sizes.layers)
             spot = pl.ds(element * 8 * tiles + tile, 8, stride=tiles)
             trial = trial_ref[spot, :]
             rate = CREEP_RATE * jnp.exp(-ACTIVATION / (mech_temp + REFERENCE_TEMP))

time: 29.4 us -> 29.4 us (level)
  no operation moved by 1% of the time
where the time goes in v13:
time: 29.4 us; the launch traced here: 29 us
  blocking collectives  14.9 us (51%)
  waiting for transfers between devices  6.54 us (22%)
  Pallas kernels  3.66 us (12%)
  starting transfers between devices  2.7 us (9%)
  between operations  1.3 us (4%)
    all_to_all x1, blocking collectives, on_device(): lax.all_to_all(dealt, EVERYONE, split_axis=0, concat_axis=0, tiled=True)  14.9 us
    all_to_all x1, waiting for transfers between devices, on_device(): lax.all_to_all(temps, EVERYONE, split_axis=0, concat_axis=0, tiled=True)  6.54 us
    pallas_call x3, Pallas kernels, kernel_call(): pl.pallas_call(functools.partial(body, sizes), out_shape=out_shape, in_sp...  3.66 us
    all_to_all x1, starting transfers between devices, on_device(): lax.all_to_all(temps, EVERYONE, split_axis=0, concat_axis=0, tiled=True)  2.7 us
  transfers between devices with their start and end apart: 1, of which 1 were waited for; matrix products, arithmetic and copies ran while one was open for 0% of the time, Pallas kernels for 0%

profile of v13, /device:TPU:0, one launch (start us, length us, event | category | flops | bytes accessed | tf_op | source)
XLA Modules:
  0.0 29.0 jit_solution(4651340343648977838)
XLA Ops:
  0.6 1.0 %shard_map.86 = f32[32,8,128]{2,1,0:T(8,128)S(1)} custom-call(s32[8]{0:T(128)} %partner_hbm.1, s32[1,8]{1,0:T(1,128)} %order_hbm.1, f32[2,1,8]{2,1,0:T(1,128)} %gap_hbm.1, f32[2,1,8,512]{3,2,1,0:T(8,128)} %temp_hbm.1, f32[2,1,8,512]{3,2,1,0:T(8,128)} %cond_hbm.1), custom_call_target="tpu_custom_call" | custom-call | tf_op jit(solution)/shard_map/pallas_call | solution.py:419
  1.7 14.9 %all_to_all.10.dealt_ref = f32[32,8,128]{2,1,0:T(8,128)S(1)} all-to-all(f32[32,8,128]{2,1,0:T(8,128)S(1)} %shard_map.86), channel_id=1, replica_groups=mesh['slab'=2,'iface'=4,'mech'=4] {'iface','slab','mech'}, dimensions={0} | all-to-all | bytes 262144 | tf_op jit(solution)/shard_map/all_to_all | solution.py:466
  16.5 1.8 %shard_map.87 = f32[64,128]{1,0:T(8,128)} custom-call(f32[32,8,128]{2,1,0:T(8,128)S(1)} %all_to_all.10.dealt_ref), custom_call_target="tpu_custom_call" | custom-call | tf_op jit(solution)/shard_map/pallas_call | solution.py:419
  18.3 0.0 copy-start
  18.3 2.7 %all-to-all-start.1 = ((f32[32,2,128]{2,1,0:T(2,128)}), f32[32,2,128]{2,1,0:T(2,128)S(1)}, u32[]{:S(2)}, u32[]{:S(2)}) async-start(f32[32,2,128]{2,1,0:T(2,128)} %bitcast), calls=%async_computation.1 | async-start | bytes 65536 | tf_op jit(solution)/shard_map/all_to_all | solution.py:477
  21.7 6.5 %all-to-all-done.1 = f32[32,2,128]{2,1,0:T(2,128)S(1)} async-done(((f32[32,2,128]{2,1,0:T(2,128)}), f32[32,2,128]{2,1,0:T(2,128)S(1)}, u32[]{:S(2)}, u32[]{:S(2)}) %all-to-all-start.1) | async-done | bytes 32800 | tf_op jit(solution)/shard_map/all_to_all | solution.py:477
  28.2 0.0 copy-done
  28.2 0.8 %shard_map.88 = (f32[64,128]{1,0:T(8,128)}, f32[8,128]{1,0:T(8,128)}) custom-call(s32[1,1]{1,0:T(1,128)S(6)} %copy.11.active_ref, f32[64,128]{1,0:T(8,128)S(1)} %bitcast.5, f32[64,128]{1,0:T(8,128)S(1)} %bitcast.6), custom_call_target="tpu_custom_call" | custom-call | tf_op jit(solution)/shard_map/pallas_call | solution.py:419
Async XLA Ops:
  18.3 9.9 %copy-start = (f32[16,1,1,512]{3,2,1,0:T(1,128)S(1)}, f32[16,1,1,512]{3,2,1,0:T(1,128)}, u32[]{:S(2)}) copy-start(f32[16,1,1,512]{3,2,1,0:T(1,128)} %param.13) | copy-start | bytes 98308
  18.3 9.9 %all-to-all-start.1 = ((f32[32,2,128]{2,1,0:T(2,128)}), f32[32,2,128]{2,1,0:T(2,128)S(1)}, u32[]{:S(2)}, u32[]{:S(2)}) async-start(f32[32,2,128]{2,1,0:T(2,128)} %bitcast), calls=%async_computation.1 | async-start | bytes 65536 | tf_op jit(solution)/shard_map/all_to_all | solution.py:477

commit v14 on v13

--- a/solution.py
+++ b/solution.py
@@ -212,9 +212,9 @@
     blocks = [
         (
             layer * sizes.layer_lanes + field * sizes.width,
-            [ref[layer, 0, :, pl.ds(tile * LANES, LANES)] for tile in range(sizes.tiles)],
-        )
-        for field, ref in enumerate((temp_ref, cond_ref))
+            [scale * ref[layer, 0, :, pl.ds(tile * LANES, LANES)] for tile in range(sizes.tiles)],
+        )
+        for field, (ref, scale) in enumerate(((temp_ref, 1.0), (cond_ref, FLUX_STEP)))
         for layer in range(sizes.layers)
     ]
     for device in range(sizes.devices):
@@ -232,7 +232,7 @@
         out_ref[device] = packed
 
 
-def sweep_kernel(sizes, dealt_ref, out_ref, line_ref):
+def sweep_kernel(sizes, dealt_ref, out_ref, temp_ref, keep_ref):
     rows, width, half_lanes = sizes.rows, sizes.width, sizes.layer_lanes
     sections, members = sizes.sections, sizes.members
     shape = (rows, LANES)
@@ -246,133 +246,140 @@
     lower_layer = lane < half_lanes
     at_compact = radius == sizes.gap_row - 1
     at_canister = radius == sizes.gap_row
-    in_grid = (radius >= 0) & (radius < sizes.radial)
     weight = jnp.where(at_compact | at_canister, 6.0, 8.0)
     is_temp = spot_in_layer < width
-    at_face = is_temp & (at_compact | at_canister)
-    keep_temp = jnp.where(is_temp & in_grid, 1.0, 0.0)
+    at_face = jnp.where(is_temp & (at_compact | at_canister), 1.0, 0.0)
+    from_inward = jnp.where(at_canister | (radius == 0), 0.0, 0.5)
+    from_outward = jnp.where(at_compact | (radius == sizes.radial - 1), 0.0, 0.5)
     face_lane = sizes.gap_row - 1 - first
+    is_given = spot_in_layer < 2 * width
+    top = sub == 0
+    bottom = sub == rows - 1
+    odd = lane % 2 == 1
+    total = sections * rows
 
     def turn(value, shift):
         return pltpu.roll(value, shift % LANES, 1)
 
-    dealt = [[dealt_ref[s * members + k] for k in range(members)] for s in range(sections)]
-
-    odd = lane % 2 == 1
-
-    def strip_of(values, start):
-        strips = []
-        for s in range(sections):
-            strip = jnp.zeros(shape, jnp.float32)
-            for k in range(members):
-                moved = pltpu.roll(values[s][k], (start + 2 * k) % LANES, 1)
-                spot = spot_in_layer // 2 == k
-                strip = jnp.where(spot, moved, strip)
-            strips.append(strip)
-        return jnp.concatenate(strips, axis=0)
-
-    total = sections * rows
+    def dealt(s, k):
+        return dealt_ref[s * members + k]
+
+    def add_to_strip(strip, value, start, k):
+        moved = pltpu.roll(value, (start + 2 * k) % LANES, 1)
+        return jnp.where(spot_in_layer // 2 == k, moved, strip)
+
+    def strips_of_dealt(start):
+        strips = [jnp.zeros(shape, jnp.float32)] * sections
+        for k in range(members):
+            strips = [add_to_strip(strips[s], dealt(s, k), start, k) for s in range(sections)]
+        return strips
+
+    meets = [
+        jnp.where(
+            lane == dealt(s, 0)[:, sizes.extra_at + 1 : sizes.extra_at + 2].astype(jnp.int32),
+            1.0,
+            0.0,
+        )
+        for s in range(sections)
+    ]
     meets = jnp.concatenate(
-        [
-            jnp.where(
-                lane == dealt[s][0][:, sizes.extra_at + 1 : sizes.extra_at + 2].astype(jnp.int32), 1.0, 0.0
-            )
-            for s in range(sections)
-        ]
-        + [jnp.zeros((LANES - total, LANES), jnp.float32)],
-        axis=0,
+        meets + [jnp.zeros((LANES - total, LANES), jnp.float32)], axis=0
     )
     met_by = meets.T[:total, :total]
-    meets = meets[:total, :total]
-    both = jnp.concatenate([meets, met_by], axis=0)
+    both = jnp.concatenate([meets[:total, :total], met_by], axis=0)
+    wide_odd = jnp.concatenate([odd] * sections, axis=0)
 
     def pick(table, strip):
         return jnp.dot(
             table, strip, precision=lax.Precision.HIGHEST, preferred_element_type=jnp.float32
         )
 
-    wide_odd = jnp.concatenate([odd] * sections, axis=0)
-    gap = strip_of(dealt, LANES + 1 - sizes.extra_at)
-    gap = jnp.where(wide_odd, gap, turn(pick(met_by, gap), -1))
-
-    def gains(values):
-        strip = strip_of(values, LANES - face_lane)
+    gap = jnp.concatenate(strips_of_dealt(LANES + 1 - sizes.extra_at), axis=0)
+    gap = FLUX_STEP * jnp.where(wide_odd, gap, turn(pick(met_by, gap), -1))
+
+    def gains(strips):
+        strip = jnp.concatenate(strips, axis=0)
         met = pick(both, strip)
         met = jnp.where(wide_odd, turn(met[:total], 1), turn(met[total:], -1))
-        gain = FLUX_STEP * gap * (met - strip)
+        gain = gap * (met - strip)
         return [gain[s * rows : (s + 1) * rows] for s in range(sections)]
 
-    conds = [[turn(value, -width) for value in line] for line in dealt]
-    edge = jnp.zeros(shape, jnp.float32)
-    for k in range(members):
-        line_ref[k, pl.ds(0, rows), :] = edge
-        line_ref[k, pl.ds(rows + total, rows), :] = edge
-
-    def with_product(value, cond):
-        return jnp.where(spot_in_layer < 2 * width, value, turn(value * cond, 2 * width))
-
-    def box_sum(values):
+    def sweep(sweep_index, gain, take):
+        def prepared(k):
+            temps = [dealt(s, k) if sweep_index == 0 else temp_ref[s, k] for s in range(sections)]
+            conds = [turn(dealt(s, k), -width) for s in range(sections)]
+            packed = [
+                jnp.where(is_given, temp, turn(temp * cond, 2 * width))
+                for temp, cond in zip(temps, conds)
+            ]
+            other = [turn(value, half_lanes) for value in packed]
+            return temps, conds, packed, other
+
+        nothing = [jnp.zeros(shape, jnp.float32)] * sections
+        below = nothing
+        current = prepared(0)
+        for k in range(members):
+            following = prepared(k + 1) if k < members - 1 else None
+            above = following[3] if following else nothing
+            temps, conds, packed, other = current
+            line = []
+            for s in range(sections):
+                near = other[s] + jnp.where(lower_layer, below[s], above[s])
+                line.append(packed[s] + 0.5 * near)
+            up = [pltpu.roll(value, 1, 0) for value in line]
+            down = [pltpu.roll(value, rows - 1, 0) for value in line]
+            fresh = []
+            for s in range(sections):
+                before = jnp.where(top, up[s - 1] if s else 0.0, up[s])
+                after = jnp.where(bottom, down[s + 1] if s < sections - 1 else 0.0, down[s])
+                value = line[s] + 0.5 * (before + after)
+                value = value + from_inward * turn(value, 1) + from_outward * turn(value, -1)
+                if sweep_index == 0:
+                    keep = 1.0 - weight * conds[s] - turn(value, -width)
+                    keep_ref[s, k] = keep
+                else:
+                    keep = keep_ref[s, k]
+                temp = temps[s] * keep + conds[s] * value + turn(value, -2 * width)
+                back = pltpu.roll(gain[s], (face_lane - 2 * k + LANES) % LANES, 1)
+                fresh.append(temp + at_face * back)
+            take(k, fresh)
+            below = other
+            current = following
+
+    strips = [jnp.zeros(shape, jnp.float32)] * sections
+
+    def keep_first(k, tiles):
         for s in range(sections):
-            other = [turn(value, half_lanes) for value in values[s]]
-            for k in range(members):
-                before = other[k - 1] if k else 0.0
-                after = other[k + 1] if k < members - 1 else 0.0
-                near = other[k] + jnp.where(lower_layer, before, after)
-                line_ref[k, pl.ds(rows + s * rows, rows), :] = values[s][k] + 0.5 * near
-        result = []
-        for s in range(sections):
-            line = []
-            for k in range(members):
-                start = rows + s * rows
-                near = line_ref[k, pl.ds(start - 1, rows), :] + line_ref[k, pl.ds(start + 1, rows), :]
-                value = line_ref[k, pl.ds(start, rows), :] + 0.5 * near
-                inward = jnp.where(at_canister, 0.0, turn(value, 1))
-                outward = jnp.where(at_compact, 0.0, turn(value, -1))
-                line.append(value + 0.5 * (inward + outward))
-            result.append(line)
-        return result
-
-    values = dealt
-    cond_sums = None
-    for sweep in range(SWEEPS):
-        gain = gains(values)
-        packed = [
-            [with_product(value, cond) for value, cond in zip(*lines)]
-            for lines in zip(values, conds)
-        ]
-        sums = box_sum(packed)
-        if cond_sums is None:
-            cond_sums = [[turn(total_sum, -width) for total_sum in line] for line in sums]
-        fresh = []
-        for s in range(sections):
-            line = []
-            for k in range(members):
-                value = values[s][k]
-                total_sum = sums[s][k]
-                change = conds[s][k] * (total_sum - weight * value)
-                change = change + turn(total_sum, -2 * width) - value * cond_sums[s][k]
-                back = pltpu.roll(gain[s], (face_lane - 2 * k + LANES) % LANES, 1)
-                temp = value + FLUX_STEP * change + jnp.where(at_face, back, 0.0)
-                line.append(jnp.where(is_temp, keep_temp * temp, value))
-            fresh.append(line)
-        values = fresh
+            temp_ref[s, k] = tiles[s]
+            strips[s] = add_to_strip(strips[s], tiles[s], LANES - face_lane, k)
+
+    for sweep_index in range(SWEEPS - 1):
+        if sweep_index == 0:
+            met_strips = strips_of_dealt(LANES - face_lane)
+        else:
+            met_strips = list(strips)
+        sweep(sweep_index, gains(met_strips), keep_first)
 
     per_row = 8 // sizes.layers
+    halves = sizes.depth // 8
     skew = place % 8 * sizes.chunk
     unskewed = (lane - skew + LANES) % half_lanes
-    for s in range(sections):
-        order = dealt[s][0][:, sizes.extra_at + 2 : sizes.extra_at + 3].astype(jnp.int32)
-        order = jnp.broadcast_to(order, shape)
-        for half in range(sizes.depth // 8):
-            merged = jnp.zeros(shape, jnp.float32)
-            for k in range(per_row):
-                moved = pltpu.roll(
-                    values[s][half * per_row + k], (k * sizes.chunk - HALO + skew) % LANES, 1
+    merged = [jnp.zeros(shape, jnp.float32)] * sections
+
+    def pack_last(k, tiles):
+        for s in range(sections):
+            shift = (k % per_row * sizes.chunk - HALO + skew) % LANES
+            moved = pltpu.roll(tiles[s], shift, 1)
+            merged[s] = jnp.where(unskewed // sizes.chunk == k % per_row, moved, merged[s])
+            if k % per_row == per_row - 1:
+                order = dealt(s, 0)[:, sizes.extra_at + 2 : sizes.extra_at + 3]
+                order = jnp.broadcast_to(order.astype(jnp.int32), shape)
+                start = s * rows * halves + k // per_row
+                out_ref[pl.ds(start, rows, stride=halves), :] = jnp.take_along_axis(
+                    merged[s], order, axis=0
                 )
-                merged = jnp.where(unskewed // sizes.chunk == k, moved, merged)
-            chosen = jnp.take_along_axis(merged, order, axis=0)
-            start = s * rows * (sizes.depth // 8) + half
-            out_ref[pl.ds(start, rows, stride=sizes.depth // 8), :] = chosen
+
+    sweep(SWEEPS - 1, gains(list(strips)), pack_last)
 
 
 def swap_blocks(tile, block, layers):
@@ -470,7 +477,7 @@
         sizes,
         (near(sizes.devices * halves, LANES),),
         [pltpu.VMEM],
-        [pltpu.VMEM((sizes.members, rows * (sizes.sections + 2), LANES), jnp.float32)],
+        [pltpu.VMEM((sizes.sections, sizes.members, rows, LANES), jnp.float32)] * 2,
         (dealt,),
     )
     temps = temps.reshape(sizes.devices, halves, LANES)

time: 29.4 us -> 29.9 us (1.017)
  Pallas kernels: 3.66 us -> 4.2 us
    pallas_call x3, Pallas kernels: 3.66 us -> 4.2 us  [kernel_call(): pl.pallas_call(functools.partial(body, sizes), out_shape=out_shape, in_sp...]
where the time goes in v14:
time: 29.9 us; the launch traced here: 29.6 us
  blocking collectives  14.9 us (50%)
  waiting for transfers between devices  6.54 us (22%)
  Pallas kernels  4.2 us (14%)
  starting transfers between devices  2.7 us (9%)
  between operations  1.3 us (4%)
    all_to_all x1, blocking collectives, on_device(): lax.all_to_all(dealt, EVERYONE, split_axis=0, concat_axis=0, tiled=True)  14.9 us
    all_to_all x1, waiting for transfers between devices, on_device(): lax.all_to_all(temps, EVERYONE, split_axis=0, concat_axis=0, tiled=True)  6.54 us
    pallas_call x3, Pallas kernels, kernel_call(): pl.pallas_call(functools.partial(body, sizes), out_shape=out_shape, in_sp...  4.2 us
    all_to_all x1, starting transfers between devices, on_device(): lax.all_to_all(temps, EVERYONE, split_axis=0, concat_axis=0, tiled=True)  2.7 us
  transfers between devices with their start and end apart: 1, of which 1 were waited for; matrix products, arithmetic and copies ran while one was open for 0% of the time, Pallas kernels for 0%

profile of v14, /device:TPU:0, one launch (start us, length us, event | category | flops | bytes accessed | tf_op | source)
XLA Modules:
  0.0 29.6 jit_solution(17436432257878930948)
XLA Ops:
  0.6 1.0 %shard_map.86 = f32[32,8,128]{2,1,0:T(8,128)S(1)} custom-call(s32[8]{0:T(128)} %partner_hbm.1, s32[1,8]{1,0:T(1,128)} %order_hbm.1, f32[2,1,8]{2,1,0:T(1,128)} %gap_hbm.1, f32[2,1,8,512]{3,2,1,0:T(8,128)} %temp_hbm.1, f32[2,1,8,512]{3,2,1,0:T(8,128)} %cond_hbm.1), custom_call_target="tpu_custom_call" | custom-call | tf_op jit(solution)/shard_map/pallas_call | solution.py:426
  1.7 14.9 %all_to_all.10.dealt_ref = f32[32,8,128]{2,1,0:T(8,128)S(1)} all-to-all(f32[32,8,128]{2,1,0:T(8,128)S(1)} %shard_map.86), channel_id=1, replica_groups=mesh['slab'=2,'iface'=4,'mech'=4] {'iface','slab','mech'}, dimensions={0} | all-to-all | bytes 262144 | tf_op jit(solution)/shard_map/all_to_all | solution.py:473
  16.5 2.3 %shard_map.87 = f32[64,128]{1,0:T(8,128)} custom-call(f32[32,8,128]{2,1,0:T(8,128)S(1)} %all_to_all.10.dealt_ref), custom_call_target="tpu_custom_call" | custom-call | tf_op jit(solution)/shard_map/pallas_call | solution.py:426
  18.9 0.0 copy-start
  18.9 2.7 %all-to-all-start.1 = ((f32[32,2,128]{2,1,0:T(2,128)}), f32[32,2,128]{2,1,0:T(2,128)S(1)}, u32[]{:S(2)}, u32[]{:S(2)}) async-start(f32[32,2,128]{2,1,0:T(2,128)} %bitcast), calls=%async_computation.1 | async-start | bytes 65536 | tf_op jit(solution)/shard_map/all_to_all | solution.py:484
  22.2 6.5 %all-to-all-done.1 = f32[32,2,128]{2,1,0:T(2,128)S(1)} async-done(((f32[32,2,128]{2,1,0:T(2,128)}), f32[32,2,128]{2,1,0:T(2,128)S(1)}, u32[]{:S(2)}, u32[]{:S(2)}) %all-to-all-start.1) | async-done | bytes 32800 | tf_op jit(solution)/shard_map/all_to_all | solution.py:484
  28.7 0.0 copy-done
  28.7 0.8 %shard_map.88 = (f32[64,128]{1,0:T(8,128)}, f32[8,128]{1,0:T(8,128)}) custom-call(s32[1,1]{1,0:T(1,128)S(6)} %copy.11.active_ref, f32[64,128]{1,0:T(8,128)S(1)} %bitcast.5, f32[64,128]{1,0:T(8,128)S(1)} %bitcast.6), custom_call_target="tpu_custom_call" | custom-call | tf_op jit(solution)/shard_map/pallas_call | solution.py:426
Async XLA Ops:
  18.9 9.9 %copy-start = (f32[16,1,1,512]{3,2,1,0:T(1,128)S(1)}, f32[16,1,1,512]{3,2,1,0:T(1,128)}, u32[]{:S(2)}) copy-start(f32[16,1,1,512]{3,2,1,0:T(1,128)} %param.13) | copy-start | bytes 98308
  18.9 9.9 %all-to-all-start.1 = ((f32[32,2,128]{2,1,0:T(2,128)}), f32[32,2,128]{2,1,0:T(2,128)S(1)}, u32[]{:S(2)}, u32[]{:S(2)}) async-start(f32[32,2,128]{2,1,0:T(2,128)} %bitcast), calls=%async_computation.1 | async-start | bytes 65536 | tf_op jit(solution)/shard_map/all_to_all | solution.py:484

commit v15 on v13

--- a/solution.py
+++ b/solution.py
@@ -212,9 +212,9 @@
     blocks = [
         (
             layer * sizes.layer_lanes + field * sizes.width,
-            [ref[layer, 0, :, pl.ds(tile * LANES, LANES)] for tile in range(sizes.tiles)],
+            [scale * ref[layer, 0, :, pl.ds(tile * LANES, LANES)] for tile in range(sizes.tiles)],
         )
-        for field, ref in enumerate((temp_ref, cond_ref))
+        for field, (ref, scale) in enumerate(((temp_ref, 1.0), (cond_ref, FLUX_STEP)))
         for layer in range(sizes.layers)
     ]
     for device in range(sizes.devices):
@@ -246,11 +246,11 @@
     lower_layer = lane < half_lanes
     at_compact = radius == sizes.gap_row - 1
     at_canister = radius == sizes.gap_row
-    in_grid = (radius >= 0) & (radius < sizes.radial)
     weight = jnp.where(at_compact | at_canister, 6.0, 8.0)
     is_temp = spot_in_layer < width
-    at_face = is_temp & (at_compact | at_canister)
-    keep_temp = jnp.where(is_temp & in_grid, 1.0, 0.0)
+    at_face = jnp.where(is_temp & (at_compact | at_canister), 1.0, 0.0)
+    from_inward = jnp.where(at_canister | (radius == 0), 0.0, 0.5)
+    from_outward = jnp.where(at_compact | (radius == sizes.radial - 1), 0.0, 0.5)
     face_lane = sizes.gap_row - 1 - first
 
     def turn(value, shift):
@@ -293,13 +293,13 @@
 
     wide_odd = jnp.concatenate([odd] * sections, axis=0)
     gap = strip_of(dealt, LANES + 1 - sizes.extra_at)
-    gap = jnp.where(wide_odd, gap, turn(pick(met_by, gap), -1))
+    gap = FLUX_STEP * jnp.where(wide_odd, gap, turn(pick(met_by, gap), -1))
 
     def gains(values):
         strip = strip_of(values, LANES - face_lane)
         met = pick(both, strip)
         met = jnp.where(wide_odd, turn(met[:total], 1), turn(met[total:], -1))
-        gain = FLUX_STEP * gap * (met - strip)
+        gain = gap * (met - strip)
         return [gain[s * rows : (s + 1) * rows] for s in range(sections)]
 
     conds = [[turn(value, -width) for value in line] for line in dealt]
@@ -326,14 +326,12 @@
                 start = rows + s * rows
                 near = line_ref[k, pl.ds(start - 1, rows), :] + line_ref[k, pl.ds(start + 1, rows), :]
                 value = line_ref[k, pl.ds(start, rows), :] + 0.5 * near
-                inward = jnp.where(at_canister, 0.0, turn(value, 1))
-                outward = jnp.where(at_compact, 0.0, turn(value, -1))
-                line.append(value + 0.5 * (inward + outward))
+                line.append(value + from_inward * turn(value, 1) + from_outward * turn(value, -1))
             result.append(line)
         return result
 
     values = dealt
-    cond_sums = None
+    keeps = None
     for sweep in range(SWEEPS):
         gain = gains(values)
         packed = [
@@ -341,19 +339,19 @@
             for lines in zip(values, conds)
         ]
         sums = box_sum(packed)
-        if cond_sums is None:
-            cond_sums = [[turn(total_sum, -width) for total_sum in line] for line in sums]
+        if keeps is None:
+            keeps = [
+                [1.0 - weight * cond - turn(total_sum, -width) for cond, total_sum in zip(*lines)]
+                for lines in zip(conds, sums)
+            ]
         fresh = []
         for s in range(sections):
             line = []
             for k in range(members):
-                value = values[s][k]
-                total_sum = sums[s][k]
-                change = conds[s][k] * (total_sum - weight * value)
-                change = change + turn(total_sum, -2 * width) - value * cond_sums[s][k]
+                temp = values[s][k] * keeps[s][k] + conds[s][k] * sums[s][k]
+                temp = temp + turn(sums[s][k], -2 * width)
                 back = pltpu.roll(gain[s], (face_lane - 2 * k + LANES) % LANES, 1)
-                temp = value + FLUX_STEP * change + jnp.where(at_face, back, 0.0)
-                line.append(jnp.where(is_temp, keep_temp * temp, value))
+                line.append(temp + at_face * back)
             fresh.append(line)
         values = fresh
 

time: 29.4 us -> 29.4 us (level)
  no operation moved by 1% of the time
where the time goes in v15:
time: 29.4 us; the launch traced here: 29 us
  blocking collectives  14.9 us (51%)
  waiting for transfers between devices  6.54 us (22%)
  Pallas kernels  3.66 us (12%)
  starting transfers between devices  2.7 us (9%)
  between operations  1.3 us (4%)
    all_to_all x1, blocking collectives, on_device(): lax.all_to_all(dealt, EVERYONE, split_axis=0, concat_axis=0, tiled=True)  14.9 us
    all_to_all x1, waiting for transfers between devices, on_device(): lax.all_to_all(temps, EVERYONE, split_axis=0, concat_axis=0, tiled=True)  6.54 us
    pallas_call x3, Pallas kernels, kernel_call(): pl.pallas_call(functools.partial(body, sizes), out_shape=out_shape, in_sp...  3.66 us
    all_to_all x1, starting transfers between devices, on_device(): lax.all_to_all(temps, EVERYONE, split_axis=0, concat_axis=0, tiled=True)  2.7 us
  transfers between devices with their start and end apart: 1, of which 1 were waited for; matrix products, arithmetic and copies ran while one was open for 0% of the time, Pallas kernels for 0%

profile of v15, /device:TPU:0, one launch (start us, length us, event | category | flops | bytes accessed | tf_op | source)
XLA Modules:
  0.0 29.0 jit_solution(10848631007028269806)
XLA Ops:
  0.6 1.0 %shard_map.86 = f32[32,8,128]{2,1,0:T(8,128)S(1)} custom-call(s32[8]{0:T(128)} %partner_hbm.1, s32[1,8]{1,0:T(1,128)} %order_hbm.1, f32[2,1,8]{2,1,0:T(1,128)} %gap_hbm.1, f32[2,1,8,512]{3,2,1,0:T(8,128)} %temp_hbm.1, f32[2,1,8,512]{3,2,1,0:T(8,128)} %cond_hbm.1), custom_call_target="tpu_custom_call" | custom-call | tf_op jit(solution)/shard_map/pallas_call | solution.py:417
  1.7 14.9 %all_to_all.10.dealt_ref = f32[32,8,128]{2,1,0:T(8,128)S(1)} all-to-all(f32[32,8,128]{2,1,0:T(8,128)S(1)} %shard_map.86), channel_id=1, replica_groups=mesh['slab'=2,'iface'=4,'mech'=4] {'iface','slab','mech'}, dimensions={0} | all-to-all | bytes 262144 | tf_op jit(solution)/shard_map/all_to_all | solution.py:464
  16.5 1.8 %shard_map.87 = f32[64,128]{1,0:T(8,128)} custom-call(f32[32,8,128]{2,1,0:T(8,128)S(1)} %all_to_all.10.dealt_ref), custom_call_target="tpu_custom_call" | custom-call | tf_op jit(solution)/shard_map/pallas_call | solution.py:417
  18.3 0.0 copy-start
  18.3 2.7 %all-to-all-start.1 = ((f32[32,2,128]{2,1,0:T(2,128)}), f32[32,2,128]{2,1,0:T(2,128)S(1)}, u32[]{:S(2)}, u32[]{:S(2)}) async-start(f32[32,2,128]{2,1,0:T(2,128)} %bitcast), calls=%async_computation.1 | async-start | bytes 65536 | tf_op jit(solution)/shard_map/all_to_all | solution.py:475
  21.7 6.5 %all-to-all-done.1 = f32[32,2,128]{2,1,0:T(2,128)S(1)} async-done(((f32[32,2,128]{2,1,0:T(2,128)}), f32[32,2,128]{2,1,0:T(2,128)S(1)}, u32[]{:S(2)}, u32[]{:S(2)}) %all-to-all-start.1) | async-done | bytes 32800 | tf_op jit(solution)/shard_map/all_to_all | solution.py:475
  28.2 0.0 copy-done
  28.2 0.8 %shard_map.88 = (f32[64,128]{1,0:T(8,128)}, f32[8,128]{1,0:T(8,128)}) custom-call(s32[1,1]{1,0:T(1,128)S(6)} %copy.11.active_ref, f32[64,128]{1,0:T(8,128)S(1)} %bitcast.5, f32[64,128]{1,0:T(8,128)S(1)} %bitcast.6), custom_call_target="tpu_custom_call" | custom-call | tf_op jit(solution)/shard_map/pallas_call | solution.py:417
Async XLA Ops:
  18.3 9.9 %copy-start = (f32[16,1,1,512]{3,2,1,0:T(1,128)S(1)}, f32[16,1,1,512]{3,2,1,0:T(1,128)}, u32[]{:S(2)}) copy-start(f32[16,1,1,512]{3,2,1,0:T(1,128)} %param.13) | copy-start | bytes 98308
  18.3 9.9 %all-to-all-start.1 = ((f32[32,2,128]{2,1,0:T(2,128)}), f32[32,2,128]{2,1,0:T(2,128)S(1)}, u32[]{:S(2)}, u32[]{:S(2)}) async-start(f32[32,2,128]{2,1,0:T(2,128)} %bitcast), calls=%async_computation.1 | async-start | bytes 65536 | tf_op jit(solution)/shard_map/all_to_all | solution.py:475

commit v16 on v15

--- a/solution.py
+++ b/solution.py
@@ -205,6 +205,9 @@
             extra = jnp.where(spot, gap_ref[layer, 0, row], extra)
         spot = (sub == row) & (lane == extra_at + 1)
         extra = jnp.where(spot, partner_ref[row].astype(jnp.float32), extra)
+        extra = jnp.where(
+            lane == 2 * sizes.width + row, partner_ref[row].astype(jnp.float32), extra
+        )
         spot = (sub == row) & (lane == extra_at + 2)
         extra = jnp.where(spot, order_ref[0, row].astype(jnp.float32), extra)
     for copy in copies[3:]:
@@ -272,28 +275,30 @@
         return jnp.concatenate(strips, axis=0)
 
     total = sections * rows
-    meets = jnp.concatenate(
-        [
-            jnp.where(
-                lane == dealt[s][0][:, sizes.extra_at + 1 : sizes.extra_at + 2].astype(jnp.int32), 1.0, 0.0
-            )
-            for s in range(sections)
-        ]
-        + [jnp.zeros((LANES - total, LANES), jnp.float32)],
-        axis=0,
-    )
-    met_by = meets.T[:total, :total]
-    meets = meets[:total, :total]
-    both = jnp.concatenate([meets, met_by], axis=0)
+    names = jnp.full(shape, -1.0, jnp.float32)
+    for s in range(sections):
+        names = jnp.where(lane // rows == s, turn(dealt[s][0], s * rows - 2 * width), names)
+    tables = []
+    for s in range(sections):
+        partner = dealt[s][0][:, sizes.extra_at + 1 : sizes.extra_at + 2].astype(jnp.int32)
+        tables.append(jnp.where(lane == partner, 1.0, 0.0))
+    for s in range(sections):
+        tables.append(jnp.where(names == (s * rows + sub).astype(jnp.float32), 1.0, 0.0))
+    both = jnp.concatenate(tables, axis=0)[:, :total].astype(jnp.bfloat16)
 
     def pick(table, strip):
-        return jnp.dot(
-            table, strip, precision=lax.Precision.HIGHEST, preferred_element_type=jnp.float32
-        )
+        rest = strip
+        picked = None
+        for _ in range(3):
+            part = rest.astype(jnp.bfloat16)
+            rest = rest - part.astype(jnp.float32)
+            share = jnp.dot(table, part, preferred_element_type=jnp.float32)
+            picked = share if picked is None else picked + share
+        return picked
 
     wide_odd = jnp.concatenate([odd] * sections, axis=0)
     gap = strip_of(dealt, LANES + 1 - sizes.extra_at)
-    gap = FLUX_STEP * jnp.where(wide_odd, gap, turn(pick(met_by, gap), -1))
+    gap = FLUX_STEP * jnp.where(wide_odd, gap, turn(pick(both[total:], gap), -1))
 
     def gains(values):
         strip = strip_of(values, LANES - face_lane)

time: 29.4 us -> 29.3 us (level)
  no operation moved by 1% of the time
where the time goes in v16:
time: 29.3 us; the launch traced here: 28.9 us
  blocking collectives  14.9 us (51%)
  waiting for transfers between devices  6.54 us (22%)
  Pallas kernels  3.56 us (12%)
  starting transfers between devices  2.7 us (9%)
  between operations  1.3 us (4%)
    all_to_all x1, blocking collectives, on_device(): lax.all_to_all(dealt, EVERYONE, split_axis=0, concat_axis=0, tiled=True)  14.9 us
    all_to_all x1, waiting for transfers between devices, on_device(): lax.all_to_all(temps, EVERYONE, split_axis=0, concat_axis=0, tiled=True)  6.54 us
    pallas_call x3, Pallas kernels, kernel_call(): pl.pallas_call(functools.partial(body, sizes), out_shape=out_shape, in_sp...  3.56 us
    all_to_all x1, starting transfers between devices, on_device(): lax.all_to_all(temps, EVERYONE, split_axis=0, concat_axis=0, tiled=True)  2.7 us
  transfers between devices with their start and end apart: 1, of which 1 were waited for; matrix products, arithmetic and copies ran while one was open for 0% of the time, Pallas kernels for 0%

profile of v16, /device:TPU:0, one launch (start us, length us, event | category | flops | bytes accessed | tf_op | source)
XLA Modules:
  0.0 28.9 jit_solution(13243635345338700601)
XLA Ops:
  0.6 1.0 %shard_map.86 = f32[32,8,128]{2,1,0:T(8,128)S(1)} custom-call(s32[8]{0:T(128)} %partner_hbm.1, s32[1,8]{1,0:T(1,128)} %order_hbm.1, f32[2,1,8]{2,1,0:T(1,128)} %gap_hbm.1, f32[2,1,8,512]{3,2,1,0:T(8,128)} %temp_hbm.1, f32[2,1,8,512]{3,2,1,0:T(8,128)} %cond_hbm.1), custom_call_target="tpu_custom_call" | custom-call | tf_op jit(solution)/shard_map/pallas_call | solution.py:422
  1.7 14.9 %all_to_all.10.dealt_ref = f32[32,8,128]{2,1,0:T(8,128)S(1)} all-to-all(f32[32,8,128]{2,1,0:T(8,128)S(1)} %shard_map.86), channel_id=1, replica_groups=mesh['slab'=2,'iface'=4,'mech'=4] {'iface','slab','mech'}, dimensions={0} | all-to-all | bytes 262144 | tf_op jit(solution)/shard_map/all_to_all | solution.py:469
  16.5 1.7 %shard_map.87 = f32[64,128]{1,0:T(8,128)} custom-call(f32[32,8,128]{2,1,0:T(8,128)S(1)} %all_to_all.10.dealt_ref), custom_call_target="tpu_custom_call" | custom-call | tf_op jit(solution)/shard_map/pallas_call | solution.py:422
  18.2 0.0 copy-start
  18.2 2.7 %all-to-all-start.1 = ((f32[32,2,128]{2,1,0:T(2,128)}), f32[32,2,128]{2,1,0:T(2,128)S(1)}, u32[]{:S(2)}, u32[]{:S(2)}) async-start(f32[32,2,128]{2,1,0:T(2,128)} %bitcast), calls=%async_computation.1 | async-start | bytes 65536 | tf_op jit(solution)/shard_map/all_to_all | solution.py:480
  21.6 6.5 %all-to-all-done.1 = f32[32,2,128]{2,1,0:T(2,128)S(1)} async-done(((f32[32,2,128]{2,1,0:T(2,128)}), f32[32,2,128]{2,1,0:T(2,128)S(1)}, u32[]{:S(2)}, u32[]{:S(2)}) %all-to-all-start.1) | async-done | bytes 32800 | tf_op jit(solution)/shard_map/all_to_all | solution.py:480
  28.1 0.0 copy-done
  28.1 0.8 %shard_map.88 = (f32[64,128]{1,0:T(8,128)}, f32[8,128]{1,0:T(8,128)}) custom-call(s32[1,1]{1,0:T(1,128)S(6)} %copy.11.active_ref, f32[64,128]{1,0:T(8,128)S(1)} %bitcast.5, f32[64,128]{1,0:T(8,128)S(1)} %bitcast.6), custom_call_target="tpu_custom_call" | custom-call | tf_op jit(solution)/shard_map/pallas_call | solution.py:422
Async XLA Ops:
  18.2 9.9 %copy-start = (f32[16,1,1,512]{3,2,1,0:T(1,128)S(1)}, f32[16,1,1,512]{3,2,1,0:T(1,128)}, u32[]{:S(2)}) copy-start(f32[16,1,1,512]{3,2,1,0:T(1,128)} %param.13) | copy-start | bytes 98308
  18.2 9.9 %all-to-all-start.1 = ((f32[32,2,128]{2,1,0:T(2,128)}), f32[32,2,128]{2,1,0:T(2,128)S(1)}, u32[]{:S(2)}, u32[]{:S(2)}) async-start(f32[32,2,128]{2,1,0:T(2,128)} %bitcast), calls=%async_computation.1 | async-start | bytes 65536 | tf_op jit(solution)/shard_map/all_to_all | solution.py:480

commit v17 on v16

--- a/solution.py
+++ b/solution.py
@@ -171,7 +171,9 @@
     gap_hbm,
     temp_hbm,
     cond_hbm,
+    active_ref,
     out_ref,
+    live_ref,
     partner_ref,
     order_ref,
     gap_ref,
@@ -197,6 +199,7 @@
     shape = (sizes.rows, LANES)
     lane = iota(shape, 1)
     sub = iota(shape, 0)
+    live_ref[...] = jnp.where(sub < active_ref[0, 0], 1.0, 0.0)
     extra_at = sizes.extra_at
     extra = jnp.zeros(shape, jnp.float32)
     for row in range(sizes.rows):
@@ -390,10 +393,9 @@
     return result
 
 
-def creep_kernel(sizes, active_ref, temps_ref, trial_ref, stress_ref, strain_ref):
+def creep_kernel(sizes, live_ref, temps_ref, trial_ref, stress_ref, strain_ref):
     tiles = sizes.tiles
     halves = sizes.depth // 8
-    active = active_ref[0, 0]
     for tile in range(tiles):
         for element in range(halves):
             source = pl.ds(tile * 8 * halves + element, 8, stride=halves)
@@ -406,7 +408,7 @@
                 left = trial - slip
                 pull = rate * left * left
                 slip = slip - (slip - pull * left) / (1.0 + 3.0 * pull)
-            creep = jnp.where(element < active, slip, 0.0)
+            creep = live_ref[pl.ds(element, 1), :] * slip
             stress_ref[spot, :] = trial - creep
             strain_ref[pl.ds(element * tiles + tile, 1), :] = 0.125 * jnp.sum(
                 creep, axis=0, keepdims=True
@@ -451,11 +453,11 @@
     def near(*shape):
         return pltpu.VMEM(shape, jnp.float32)
 
-    (dealt,) = kernel_call(
+    dealt, live = kernel_call(
         deal_kernel,
         sizes,
-        (near(sizes.devices, rows, LANES),),
-        [pltpu.HBM] * 5,
+        (near(sizes.devices, rows, LANES), near(8, LANES)),
+        [pltpu.HBM] * 5 + [pltpu.SMEM],
         [
             pltpu.SMEM(partner.shape, jnp.int32),
             pltpu.SMEM(row_order.shape, jnp.int32),
@@ -464,7 +466,7 @@
             pltpu.VMEM(conductivity.shape, jnp.float32),
             pltpu.SemaphoreType.DMA((5,)),
         ],
-        (partner, row_order, gap_conductance, temp_start, conductivity),
+        (partner, row_order, gap_conductance, temp_start, conductivity, active_layers),
     )
     dealt = lax.all_to_all(dealt, EVERYONE, split_axis=0, concat_axis=0, tiled=True)
     halves = sizes.depth // 8
@@ -482,10 +484,10 @@
         creep_kernel,
         sizes,
         (floats(sizes.depth * sizes.tiles, LANES), floats(halves * sizes.tiles, LANES)),
-        [pltpu.SMEM, pltpu.VMEM, pltpu.VMEM],
+        [pltpu.VMEM, pltpu.VMEM, pltpu.VMEM],
         [],
         (
-            active_layers,
+            live,
             temps.reshape(sizes.devices * halves, LANES),
             trial_stress.reshape(sizes.depth * sizes.tiles, LANES),
         ),

time: 29.3 us -> 28.7 us (0.980)
  blocking collectives: 14.9 us -> 24.2 us
  waiting for transfers between devices: 6.54 us -> 0 us
  starting transfers between devices: 2.7 us -> 0 us
  Pallas kernels: 3.56 us -> 2.94 us
    all_to_all x0 -> x1, blocking collectives: none -> 9.31 us  [on_device(): lax.all_to_all(temps, EVERYONE, split_axis=0, concat_axis=0, tiled=True)]
    all_to_all x1 -> x0, waiting for transfers between devices: 6.54 us -> none  [on_device(): lax.all_to_all(temps, EVERYONE, split_axis=0, concat_axis=0, tiled=True)]
    all_to_all x1 -> x0, starting transfers between devices: 2.7 us -> none  [on_device(): lax.all_to_all(temps, EVERYONE, split_axis=0, concat_axis=0, tiled=True)]
    pallas_call x3, Pallas kernels: 3.56 us -> 2.94 us  [kernel_call(): pl.pallas_call(functools.partial(body, sizes), out_shape=out_shape, in_sp...]
  transfers between devices with their start and end apart: 1 -> 0, of which waited for: 1 -> 0; matrix products, arithmetic and copies ran while one was open for 0% -> 0% of each run, Pallas kernels for 0% -> 0%
where the time goes in v17:
time: 28.7 us; the launch traced here: 28.4 us
  blocking collectives  24.2 us (84%)
  Pallas kernels  2.94 us (10%)
  between operations  1.3 us (5%)
    all_to_all x1, blocking collectives, on_device(): lax.all_to_all(dealt, EVERYONE, split_axis=0, concat_axis=0, tiled=True)  14.9 us
    all_to_all x1, blocking collectives, on_device(): lax.all_to_all(temps, EVERYONE, split_axis=0, concat_axis=0, tiled=True)  9.31 us
    pallas_call x3, Pallas kernels, kernel_call(): pl.pallas_call(functools.partial(body, sizes), out_shape=out_shape, in_sp...  2.94 us

profile of v17, /device:TPU:0, one launch (start us, length us, event | category | flops | bytes accessed | tf_op | source)
XLA Modules:
  0.0 28.4 jit_solution(8331907166142175970)
XLA Ops:
  1.3 1.0 %shard_map.86 = (f32[32,8,128]{2,1,0:T(8,128)S(1)}, f32[8,128]{1,0:T(8,128)S(1)}) custom-call(s32[8]{0:T(128)} %partner_hbm.1, s32[1,8]{1,0:T(1,128)} %order_hbm.1, f32[2,1,8]{2,1,0:T(1,128)} %gap_hbm.1, f32[2,1,8,512]{3,2,1,0:T(8,128)} %temp_hbm.1, f32[2,1,8,512]{3,2,1,0:T(8,128)} %cond_hbm.1, s32[1,1]{1,0:T(1,128)S(6)} %copy.11.active_ref), custom_call_target="tpu_custom_call" | custom-call | tf_op jit(solution)/shard_map/pallas_call | solution.py:424
  2.3 14.9 %all_to_all.10.dealt_ref = f32[32,8,128]{2,1,0:T(8,128)S(1)} all-to-all(f32[32,8,128]{2,1,0:T(8,128)S(1)} %get-tuple-element.7), channel_id=1, replica_groups=mesh['slab'=2,'iface'=4,'mech'=4] {'iface','slab','mech'}, dimensions={0} | all-to-all | bytes 262144 | tf_op jit(solution)/shard_map/all_to_all | solution.py:471
  17.2 1.1 %shard_map.87 = f32[64,128]{1,0:T(8,128)S(1)} custom-call(f32[32,8,128]{2,1,0:T(8,128)S(1)} %all_to_all.10.dealt_ref), custom_call_target="tpu_custom_call" | custom-call | tf_op jit(solution)/shard_map/pallas_call | solution.py:424
  18.3 0.0 copy-start
  18.3 9.3 %all_to_all.11 = f32[32,2,128]{2,1,0:T(2,128)S(1)} all-to-all(f32[32,2,128]{2,1,0:T(2,128)S(1)} %bitcast.5), channel_id=1, replica_groups=mesh['slab'=2,'iface'=4,'mech'=4] {'iface','slab','mech'}, dimensions={0} | all-to-all | bytes 65536 | tf_op jit(solution)/shard_map/all_to_all | solution.py:482
  27.6 0.0 copy-done
  27.6 0.8 %shard_map.88 = (f32[64,128]{1,0:T(8,128)}, f32[8,128]{1,0:T(8,128)}) custom-call(f32[8,128]{1,0:T(8,128)S(1)} %get-tuple-element.6.live_ref, f32[64,128]{1,0:T(8,128)S(1)} %bitcast.6, f32[64,128]{1,0:T(8,128)S(1)} %bitcast.7), custom_call_target="tpu_custom_call" | custom-call | tf_op jit(solution)/shard_map/pallas_call | solution.py:424
Async XLA Ops:
  18.3 9.3 %copy-start = (f32[16,1,1,512]{3,2,1,0:T(1,128)S(1)}, f32[16,1,1,512]{3,2,1,0:T(1,128)}, u32[]{:S(2)}) copy-start(f32[16,1,1,512]{3,2,1,0:T(1,128)} %param.13) | copy-start | bytes 98308

commit v18 on v17

--- a/solution.py
+++ b/solution.py
@@ -151,6 +151,15 @@
         self.gap_row = radial // 2
 
 
+def chunk_of(sizes, section, member):
+    mirrored = section < sizes.sections // 2
+    if isinstance(section, int):
+        place = sizes.members - 1 - member if mirrored else member
+    else:
+        place = jnp.where(mirrored, sizes.members - 1 - member, member)
+    return section * sizes.members + place
+
+
 def fits_tiles(sizes):
     return (
         sizes.rows == 8
@@ -224,7 +233,8 @@
         for layer in range(sizes.layers)
     ]
     for device in range(sizes.devices):
-        first = device * sizes.chunk - HALO
+        chunk = chunk_of(sizes, device // sizes.members, device % sizes.members)
+        first = chunk * sizes.chunk - HALO
         packed = extra
         for base, block in blocks:
             for tile in range(sizes.tiles):
@@ -238,14 +248,14 @@
         out_ref[device] = packed
 
 
-def sweep_kernel(sizes, dealt_ref, out_ref, line_ref):
+def sweep_kernel(sizes, dealt_ref, out_ref, line_ref, temp_ref, table_ref, gap_ref):
     rows, width, half_lanes = sizes.rows, sizes.width, sizes.layer_lanes
     sections, members = sizes.sections, sizes.members
     shape = (rows, LANES)
     lane = iota(shape, 1)
     sub = iota(shape, 0)
-    place = lax.axis_index("iface") * members
-    place = place + lax.axis_index("slab") * lax.axis_size("mech") + lax.axis_index("mech")
+    member = lax.axis_index("slab") * lax.axis_size("mech") + lax.axis_index("mech")
+    place = chunk_of(sizes, lax.axis_index("iface"), member)
     first = place * sizes.chunk - HALO
     spot_in_layer = lane % half_lanes
     radius = first + spot_in_layer % width
@@ -278,16 +288,8 @@
         return jnp.concatenate(strips, axis=0)
 
     total = sections * rows
-    names = jnp.full(shape, -1.0, jnp.float32)
-    for s in range(sections):
-        names = jnp.where(lane // rows == s, turn(dealt[s][0], s * rows - 2 * width), names)
-    tables = []
-    for s in range(sections):
-        partner = dealt[s][0][:, sizes.extra_at + 1 : sizes.extra_at + 2].astype(jnp.int32)
-        tables.append(jnp.where(lane == partner, 1.0, 0.0))
-    for s in range(sections):
-        tables.append(jnp.where(names == (s * rows + sub).astype(jnp.float32), 1.0, 0.0))
-    both = jnp.concatenate(tables, axis=0)[:, :total].astype(jnp.bfloat16)
+    has_face = (first < sizes.gap_row) & (first + width > sizes.gap_row)
+    wide_odd = jnp.concatenate([odd] * sections, axis=0)
 
     def pick(table, strip):
         rest = strip
@@ -299,16 +301,31 @@
             picked = share if picked is None else picked + share
         return picked
 
-    wide_odd = jnp.concatenate([odd] * sections, axis=0)
-    gap = strip_of(dealt, LANES + 1 - sizes.extra_at)
-    gap = FLUX_STEP * jnp.where(wide_odd, gap, turn(pick(both[total:], gap), -1))
-
-    def gains(values):
+    @pl.when(has_face)
+    def prepare_exchange():
+        names = jnp.full(shape, -1.0, jnp.float32)
+        for s in range(sections):
+            names = jnp.where(lane // rows == s, turn(dealt[s][0], s * rows - 2 * width), names)
+        for s in range(sections):
+            partner = dealt[s][0][:, sizes.extra_at + 1 : sizes.extra_at + 2].astype(jnp.int32)
+            table_ref[pl.ds(s * rows, rows), :] = jnp.where(lane == partner, 1.0, 0.0)
+        for s in range(sections):
+            target = (s * rows + sub).astype(jnp.float32)
+            table_ref[pl.ds(total + s * rows, rows), :] = jnp.where(names == target, 1.0, 0.0)
+        table = table_ref[pl.ds(total, total), :][:, :total].astype(jnp.bfloat16)
+        gap = strip_of(dealt, LANES + 1 - sizes.extra_at)
+        gap_ref[...] = FLUX_STEP * jnp.where(wide_odd, gap, turn(pick(table, gap), -1))
+
+    def exchange(values):
         strip = strip_of(values, LANES - face_lane)
-        met = pick(both, strip)
+        met = pick(table_ref[...][:, :total].astype(jnp.bfloat16), strip)
         met = jnp.where(wide_odd, turn(met[:total], 1), turn(met[total:], -1))
-        gain = gap * (met - strip)
-        return [gain[s * rows : (s + 1) * rows] for s in range(sections)]
+        gain = gap_ref[...] * (met - strip)
+        for s in range(sections):
+            own = gain[s * rows : (s + 1) * rows]
+            for k in range(members):
+                back = pltpu.roll(own, (face_lane - 2 * k + LANES) % LANES, 1)
+                temp_ref[s, k] = temp_ref[s, k] + at_face * back
 
     conds = [[turn(value, -width) for value in line] for line in dealt]
     edge = jnp.zeros(shape, jnp.float32)
@@ -341,7 +358,6 @@
     values = dealt
     keeps = None
     for sweep in range(SWEEPS):
-        gain = gains(values)
         packed = [
             [with_product(value, cond) for value, cond in zip(*lines)]
             for lines in zip(values, conds)
@@ -352,16 +368,12 @@
                 [1.0 - weight * cond - turn(total_sum, -width) for cond, total_sum in zip(*lines)]
                 for lines in zip(conds, sums)
             ]
-        fresh = []
-        for s in range(sections):
-            line = []
+        for s in range(sections):
             for k in range(members):
                 temp = values[s][k] * keeps[s][k] + conds[s][k] * sums[s][k]
-                temp = temp + turn(sums[s][k], -2 * width)
-                back = pltpu.roll(gain[s], (face_lane - 2 * k + LANES) % LANES, 1)
-                line.append(temp + at_face * back)
-            fresh.append(line)
-        values = fresh
+                temp_ref[s, k] = temp + turn(sums[s][k], -2 * width)
+        pl.when(has_face)(functools.partial(exchange, values))
+        values = [[temp_ref[s, k] for k in range(members)] for s in range(sections)]
 
     per_row = 8 // sizes.layers
     skew = place % 8 * sizes.chunk
@@ -381,11 +393,12 @@
             out_ref[pl.ds(start, rows, stride=sizes.depth // 8), :] = chosen
 
 
-def swap_blocks(tile, block, layers):
+def swap_blocks(tile, block, layers, mirrored):
     sub = iota(tile.shape, 0)
     spot = iota(tile.shape, 1) // block
     held = sub % layers * (8 // layers) + sub // layers
-    gathered = jnp.take_along_axis(tile, (spot - held + 8) % 8, axis=0)
+    source = (spot - held + 8) % 8
+    gathered = jnp.take_along_axis(tile, 7 - source if mirrored else source, axis=0)
     rolled = [pltpu.roll(gathered, (8 - row) % 8 * block, 1) if row else gathered for row in range(8)]
     result = rolled[0]
     for row in range(1, 8):
@@ -399,7 +412,9 @@
     for tile in range(tiles):
         for element in range(halves):
             source = pl.ds(tile * 8 * halves + element, 8, stride=halves)
-            mech_temp = swap_blocks(temps_ref[source, :], sizes.chunk, sizes.layers)
+            mech_temp = swap_blocks(
+                temps_ref[source, :], sizes.chunk, sizes.layers, tile < sizes.sections // 2
+            )
             spot = pl.ds(element * 8 * tiles + tile, 8, stride=tiles)
             trial = trial_ref[spot, :]
             rate = CREEP_RATE * jnp.exp(-ACTIVATION / (mech_temp + REFERENCE_TEMP))
@@ -475,7 +490,12 @@
         sizes,
         (near(sizes.devices * halves, LANES),),
         [pltpu.VMEM],
-        [pltpu.VMEM((sizes.members, rows * (sizes.sections + 2), LANES), jnp.float32)],
+        [
+            pltpu.VMEM((sizes.members, rows * (sizes.sections + 2), LANES), jnp.float32),
+            pltpu.VMEM((sizes.sections, sizes.members, rows, LANES), jnp.float32),
+            pltpu.VMEM((2 * sizes.sections * rows, LANES), jnp.float32),
+            pltpu.VMEM((sizes.sections * rows, LANES), jnp.float32),
+        ],
         (dealt,),
     )
     temps = temps.reshape(sizes.devices, halves, LANES)

time: 28.7 us -> 28.6 us (level)
  no operation moved by 1% of the time
where the time goes in v18:
time: 28.6 us; the launch traced here: 28.4 us
  blocking collectives  24.2 us (85%)
  Pallas kernels  2.82 us (10%)
  between operations  1.3 us (5%)
    all_to_all x1, blocking collectives, on_device(): lax.all_to_all(dealt, EVERYONE, split_axis=0, concat_axis=0, tiled=True)  14.9 us
    all_to_all x1, blocking collectives, on_device(): lax.all_to_all(temps, EVERYONE, split_axis=0, concat_axis=0, tiled=True)  9.37 us
    pallas_call x3, Pallas kernels, kernel_call(): pl.pallas_call(functools.partial(body, sizes), out_shape=out_shape, in_sp...  2.82 us

profile of v18, /device:TPU:0, one launch (start us, length us, event | category | flops | bytes accessed | tf_op | source)
XLA Modules:
  0.0 28.4 jit_solution(9672678156806687991)
XLA Ops:
  1.3 1.0 %shard_map.86 = (f32[32,8,128]{2,1,0:T(8,128)S(1)}, f32[8,128]{1,0:T(8,128)S(1)}) custom-call(s32[8]{0:T(128)} %partner_hbm.1, s32[1,8]{1,0:T(1,128)} %order_hbm.1, f32[2,1,8]{2,1,0:T(1,128)} %gap_hbm.1, f32[2,1,8,512]{3,2,1,0:T(8,128)} %temp_hbm.1, f32[2,1,8,512]{3,2,1,0:T(8,128)} %cond_hbm.1, s32[1,1]{1,0:T(1,128)S(6)} %copy.11.active_ref), custom_call_target="tpu_custom_call" | custom-call | tf_op jit(solution)/shard_map/pallas_call | solution.py:439
  2.3 14.9 %all_to_all.10.dealt_ref = f32[32,8,128]{2,1,0:T(8,128)S(1)} all-to-all(f32[32,8,128]{2,1,0:T(8,128)S(1)} %get-tuple-element.7), channel_id=1, replica_groups=mesh['slab'=2,'iface'=4,'mech'=4] {'iface','slab','mech'}, dimensions={0} | all-to-all | bytes 262144 | tf_op jit(solution)/shard_map/all_to_all | solution.py:486
  17.2 1.0 %shard_map.87 = f32[64,128]{1,0:T(8,128)S(1)} custom-call(f32[32,8,128]{2,1,0:T(8,128)S(1)} %all_to_all.10.dealt_ref), custom_call_target="tpu_custom_call" | custom-call | tf_op jit(solution)/shard_map/pallas_call | solution.py:439
  18.1 0.0 copy-start
  18.1 9.4 %all_to_all.11 = f32[32,2,128]{2,1,0:T(2,128)S(1)} all-to-all(f32[32,2,128]{2,1,0:T(2,128)S(1)} %bitcast.5), channel_id=1, replica_groups=mesh['slab'=2,'iface'=4,'mech'=4] {'iface','slab','mech'}, dimensions={0} | all-to-all | bytes 65536 | tf_op jit(solution)/shard_map/all_to_all | solution.py:502
  27.5 0.0 copy-done
  27.5 0.8 %shard_map.88 = (f32[64,128]{1,0:T(8,128)}, f32[8,128]{1,0:T(8,128)}) custom-call(f32[8,128]{1,0:T(8,128)S(1)} %get-tuple-element.6.live_ref, f32[64,128]{1,0:T(8,128)S(1)} %bitcast.6, f32[64,128]{1,0:T(8,128)S(1)} %bitcast.7), custom_call_target="tpu_custom_call" | custom-call | tf_op jit(solution)/shard_map/pallas_call | solution.py:439
Async XLA Ops:
  18.1 9.4 %copy-start = (f32[16,1,1,512]{3,2,1,0:T(1,128)S(1)}, f32[16,1,1,512]{3,2,1,0:T(1,128)}, u32[]{:S(2)}) copy-start(f32[16,1,1,512]{3,2,1,0:T(1,128)} %param.13) | copy-start | bytes 98308

commit v19 on v18

--- a/solution.py
+++ b/solution.py
@@ -209,43 +209,55 @@
     lane = iota(shape, 1)
     sub = iota(shape, 0)
     live_ref[...] = jnp.where(sub < active_ref[0, 0], 1.0, 0.0)
-    extra_at = sizes.extra_at
+    width, half_lanes = sizes.width, sizes.layer_lanes
+    spot = lane % half_lanes
     extra = jnp.zeros(shape, jnp.float32)
     for row in range(sizes.rows):
+        name = partner_ref[row].astype(jnp.float32)
+        values = jnp.where(spot == sizes.extra_at + 1, name, 0.0)
+        values = jnp.where(
+            spot == sizes.extra_at + 2, order_ref[0, row].astype(jnp.float32), values
+        )
         for layer in range(sizes.layers):
-            spot = (sub == row) & (lane == extra_at + layer * sizes.layer_lanes)
-            extra = jnp.where(spot, gap_ref[layer, 0, row], extra)
-        spot = (sub == row) & (lane == extra_at + 1)
-        extra = jnp.where(spot, partner_ref[row].astype(jnp.float32), extra)
-        extra = jnp.where(
-            lane == 2 * sizes.width + row, partner_ref[row].astype(jnp.float32), extra
-        )
-        spot = (sub == row) & (lane == extra_at + 2)
-        extra = jnp.where(spot, order_ref[0, row].astype(jnp.float32), extra)
+            values = jnp.where(
+                lane == sizes.extra_at + layer * half_lanes, gap_ref[layer, 0, row], values
+            )
+        extra = jnp.where(sub == row, values, extra)
+    for row in range(sizes.rows):
+        name = partner_ref[row].astype(jnp.float32)
+        extra = jnp.where(lane == 2 * width + row, name, extra)
     for copy in copies[3:]:
         copy.wait()
-    blocks = [
-        (
-            layer * sizes.layer_lanes + field * sizes.width,
-            [scale * ref[layer, 0, :, pl.ds(tile * LANES, LANES)] for tile in range(sizes.tiles)],
-        )
-        for field, (ref, scale) in enumerate(((temp_ref, 1.0), (cond_ref, FLUX_STEP)))
-        for layer in range(sizes.layers)
-    ]
+    bases = []
+    blocks = []
+    for layer in range(sizes.layers):
+        for field, (ref, scale) in enumerate(((temp_ref, 1.0), (cond_ref, FLUX_STEP))):
+            base = layer * half_lanes + field * width
+            bases.append(base)
+            blocks.append(
+                [
+                    pltpu.roll(scale * ref[layer, 0, :, pl.ds(tile * LANES, LANES)], base, 1)
+                    for tile in range(sizes.tiles)
+                ]
+            )
     for device in range(sizes.devices):
         chunk = chunk_of(sizes, device // sizes.members, device % sizes.members)
         first = chunk * sizes.chunk - HALO
-        packed = extra
-        for base, block in blocks:
-            for tile in range(sizes.tiles):
-                low = max(first, tile * LANES)
-                high = min(first + sizes.width, (tile + 1) * LANES)
-                if low >= high:
-                    continue
-                moved = pltpu.roll(block[tile], (base - first + tile * LANES) % LANES, 1)
-                spot = (lane >= base + low - first) & (lane < base + high - first)
-                packed = jnp.where(spot, moved, packed)
-        out_ref[device] = packed
+        tile = chunk * sizes.chunk // LANES
+        start = first - tile * LANES
+        place = (lane - start + LANES) % LANES
+        merged = None
+        for base, block in zip(bases, blocks):
+            value = block[tile]
+            if start < 0 and tile > 0:
+                value = jnp.where((place >= base) & (place < base - start), block[tile - 1], value)
+            over = start + width - LANES
+            if over > 0 and tile < sizes.tiles - 1:
+                inside = (place < base + width) & (place >= base + width - over)
+                value = jnp.where(inside, block[tile + 1], value)
+            merged = value if merged is None else jnp.where(place >= base, value, merged)
+        moved = pltpu.roll(merged, -start % LANES, 1)
+        out_ref[device] = jnp.where(spot < 2 * width, moved, extra)
 
 
 def sweep_kernel(sizes, dealt_ref, out_ref, line_ref, temp_ref, table_ref, gap_ref):

time: 28.6 us -> 28.6 us (level)
  no operation moved by 1% of the time
where the time goes in v19:
time: 28.6 us; the launch traced here: 28.3 us
  blocking collectives  24.2 us (85%)
  Pallas kernels  2.8 us (10%)
  between operations  1.3 us (5%)
    all_to_all x1, blocking collectives, on_device(): lax.all_to_all(dealt, EVERYONE, split_axis=0, concat_axis=0, tiled=True)  14.9 us
    all_to_all x1, blocking collectives, on_device(): lax.all_to_all(temps, EVERYONE, split_axis=0, concat_axis=0, tiled=True)  9.37 us
    pallas_call x3, Pallas kernels, kernel_call(): pl.pallas_call(functools.partial(body, sizes), out_shape=out_shape, in_sp...  2.8 us

profile of v19, /device:TPU:0, one launch (start us, length us, event | category | flops | bytes accessed | tf_op | source)
XLA Modules:
  0.0 28.3 jit_solution(16310577860929647281)
XLA Ops:
  1.3 1.0 %shard_map.86 = (f32[32,8,128]{2,1,0:T(8,128)S(1)}, f32[8,128]{1,0:T(8,128)S(1)}) custom-call(s32[8]{0:T(128)} %partner_hbm.1, s32[1,8]{1,0:T(1,128)} %order_hbm.1, f32[2,1,8]{2,1,0:T(1,128)} %gap_hbm.1, f32[2,1,8,512]{3,2,1,0:T(8,128)} %temp_hbm.1, f32[2,1,8,512]{3,2,1,0:T(8,128)} %cond_hbm.1, s32[1,1]{1,0:T(1,128)S(6)} %copy.11.active_ref), custom_call_target="tpu_custom_call" | custom-call | tf_op jit(solution)/shard_map/pallas_call | solution.py:451
  2.3 14.9 %all_to_all.10.dealt_ref = f32[32,8,128]{2,1,0:T(8,128)S(1)} all-to-all(f32[32,8,128]{2,1,0:T(8,128)S(1)} %get-tuple-element.7), channel_id=1, replica_groups=mesh['slab'=2,'iface'=4,'mech'=4] {'iface','slab','mech'}, dimensions={0} | all-to-all | bytes 262144 | tf_op jit(solution)/shard_map/all_to_all | solution.py:498
  17.1 1.0 %shard_map.87 = f32[64,128]{1,0:T(8,128)S(1)} custom-call(f32[32,8,128]{2,1,0:T(8,128)S(1)} %all_to_all.10.dealt_ref), custom_call_target="tpu_custom_call" | custom-call | tf_op jit(solution)/shard_map/pallas_call | solution.py:451
  18.1 0.0 copy-start
  18.1 9.4 %all_to_all.11 = f32[32,2,128]{2,1,0:T(2,128)S(1)} all-to-all(f32[32,2,128]{2,1,0:T(2,128)S(1)} %bitcast.5), channel_id=1, replica_groups=mesh['slab'=2,'iface'=4,'mech'=4] {'iface','slab','mech'}, dimensions={0} | all-to-all | bytes 65536 | tf_op jit(solution)/shard_map/all_to_all | solution.py:514
  27.5 0.0 copy-done
  27.5 0.8 %shard_map.88 = (f32[64,128]{1,0:T(8,128)}, f32[8,128]{1,0:T(8,128)}) custom-call(f32[8,128]{1,0:T(8,128)S(1)} %get-tuple-element.6.live_ref, f32[64,128]{1,0:T(8,128)S(1)} %bitcast.6, f32[64,128]{1,0:T(8,128)S(1)} %bitcast.7), custom_call_target="tpu_custom_call" | custom-call | tf_op jit(solution)/shard_map/pallas_call | solution.py:451
Async XLA Ops:
  18.1 9.4 %copy-start = (f32[16,1,1,512]{3,2,1,0:T(1,128)S(1)}, f32[16,1,1,512]{3,2,1,0:T(1,128)}, u32[]{:S(2)}) copy-start(f32[16,1,1,512]{3,2,1,0:T(1,128)} %param.13) | copy-start | bytes 98308

commit v20 on v18

--- a/solution.py
+++ b/solution.py
@@ -127,7 +127,7 @@
 
 LANES = 128
 HALO = 2
-EVERYONE = ("iface", "slab", "mech")
+EVERYONE = ("iface", "mech", "slab")
 
 
 def iota(shape, axis):
@@ -254,7 +254,8 @@
     shape = (rows, LANES)
     lane = iota(shape, 1)
     sub = iota(shape, 0)
-    member = lax.axis_index("slab") * lax.axis_size("mech") + lax.axis_index("mech")
+    slabs, per_slab = lax.axis_size("slab"), lax.axis_size("mech")
+    member = lax.axis_index("mech") * slabs + lax.axis_index("slab")
     place = chunk_of(sizes, lax.axis_index("iface"), member)
     first = place * sizes.chunk - HALO
     spot_in_layer = lane % half_lanes
@@ -272,7 +273,7 @@
     def turn(value, shift):
         return pltpu.roll(value, shift % LANES, 1)
 
-    dealt = [[dealt_ref[s * members + k] for k in range(members)] for s in range(sections)]
+    dealt = [[dealt_ref[s * members + k % per_slab * slabs + k // per_slab] for k in range(members)] for s in range(sections)]
 
     odd = lane % 2 == 1
 
@@ -389,8 +390,12 @@
                 )
                 merged = jnp.where(unskewed // sizes.chunk == k, moved, merged)
             chosen = jnp.take_along_axis(merged, order, axis=0)
-            start = s * rows * (sizes.depth // 8) + half
-            out_ref[pl.ds(start, rows, stride=sizes.depth // 8), :] = chosen
+            halves = sizes.depth // 8
+            for slab in range(slabs):
+                start = (s * members + slab) * halves + half
+                out_ref[pl.ds(start, per_slab, stride=slabs * halves), :] = chosen[
+                    slab * per_slab : (slab + 1) * per_slab
+                ]
 
 
 def swap_blocks(tile, block, layers, mirrored):

time: 28.6 us -> 28.8 us (level)
  no operation moved by 1% of the time
where the time goes in v20:
time: 28.8 us; the launch traced here: 28.5 us
  blocking collectives  24.4 us (85%)
  Pallas kernels  2.82 us (10%)
  between operations  1.3 us (5%)
    all_to_all x1, blocking collectives, on_device(): lax.all_to_all(dealt, EVERYONE, split_axis=0, concat_axis=0, tiled=True)  14.8 us
    all_to_all x1, blocking collectives, on_device(): lax.all_to_all(temps, EVERYONE, split_axis=0, concat_axis=0, tiled=True)  9.52 us
    pallas_call x3, Pallas kernels, kernel_call(): pl.pallas_call(functools.partial(body, sizes), out_shape=out_shape, in_sp...  2.82 us

profile of v20, /device:TPU:0, one launch (start us, length us, event | category | flops | bytes accessed | tf_op | source)
XLA Modules:
  0.0 28.5 jit_solution(14549773429860768076)
XLA Ops:
  1.3 1.0 %shard_map.86 = (f32[32,8,128]{2,1,0:T(8,128)S(1)}, f32[8,128]{1,0:T(8,128)S(1)}) custom-call(s32[8]{0:T(128)} %partner_hbm.1, s32[1,8]{1,0:T(1,128)} %order_hbm.1, f32[2,1,8]{2,1,0:T(1,128)} %gap_hbm.1, f32[2,1,8,512]{3,2,1,0:T(8,128)} %temp_hbm.1, f32[2,1,8,512]{3,2,1,0:T(8,128)} %cond_hbm.1, s32[1,1]{1,0:T(1,128)S(6)} %copy.11.active_ref), custom_call_target="tpu_custom_call" | custom-call | tf_op jit(solution)/shard_map/pallas_call | solution.py:444
  2.3 14.8 %all_to_all.10.dealt_ref = f32[32,8,128]{2,1,0:T(8,128)S(1)} all-to-all(f32[32,8,128]{2,1,0:T(8,128)S(1)} %get-tuple-element.7), channel_id=1, replica_groups=mesh['slab'=2,'iface'=4,'mech'=4] {'iface','mech','slab'}, dimensions={0} | all-to-all | bytes 262144 | tf_op jit(solution)/shard_map/all_to_all | solution.py:491
  17.2 1.0 %shard_map.87 = f32[64,128]{1,0:T(8,128)S(1)} custom-call(f32[32,8,128]{2,1,0:T(8,128)S(1)} %all_to_all.10.dealt_ref), custom_call_target="tpu_custom_call" | custom-call | tf_op jit(solution)/shard_map/pallas_call | solution.py:444
  18.1 0.0 copy-start
  18.1 9.5 %all_to_all.11 = f32[32,2,128]{2,1,0:T(2,128)S(1)} all-to-all(f32[32,2,128]{2,1,0:T(2,128)S(1)} %bitcast.5), channel_id=1, replica_groups=mesh['slab'=2,'iface'=4,'mech'=4] {'iface','mech','slab'}, dimensions={0} | all-to-all | bytes 65536 | tf_op jit(solution)/shard_map/all_to_all | solution.py:507
  27.7 0.0 copy-done
  27.7 0.8 %shard_map.88 = (f32[64,128]{1,0:T(8,128)}, f32[8,128]{1,0:T(8,128)}) custom-call(f32[8,128]{1,0:T(8,128)S(1)} %get-tuple-element.6.live_ref, f32[64,128]{1,0:T(8,128)S(1)} %bitcast.6, f32[64,128]{1,0:T(8,128)S(1)} %bitcast.7), custom_call_target="tpu_custom_call" | custom-call | tf_op jit(solution)/shard_map/pallas_call | solution.py:444
Async XLA Ops:
  18.1 9.5 %copy-start = (f32[16,1,1,512]{3,2,1,0:T(1,128)S(1)}, f32[16,1,1,512]{3,2,1,0:T(1,128)}, u32[]{:S(2)}) copy-start(f32[16,1,1,512]{3,2,1,0:T(1,128)} %param.13) | copy-start | bytes 98308

commit v21 on v18

--- a/solution.py
+++ b/solution.py
@@ -406,17 +406,19 @@
     return result
 
 
-def creep_kernel(sizes, live_ref, temps_ref, trial_ref, stress_ref, strain_ref):
+def creep_kernel(
+    sizes, live_ref, temps_ref, trial_ref, stress_hbm, strain_hbm, stress_ref, strain_ref, sems
+):
     tiles = sizes.tiles
     halves = sizes.depth // 8
-    for tile in range(tiles):
-        for element in range(halves):
+    copies = []
+    for element in range(halves):
+        for tile in range(tiles):
             source = pl.ds(tile * 8 * halves + element, 8, stride=halves)
             mech_temp = swap_blocks(
                 temps_ref[source, :], sizes.chunk, sizes.layers, tile < sizes.sections // 2
             )
-            spot = pl.ds(element * 8 * tiles + tile, 8, stride=tiles)
-            trial = trial_ref[spot, :]
+            trial = trial_ref[pl.ds(element * 8 * tiles + tile, 8, stride=tiles), :]
             rate = CREEP_RATE * jnp.exp(-ACTIVATION / (mech_temp + REFERENCE_TEMP))
             slip = jnp.zeros(trial.shape, jnp.float32)
             for newton_step in range(NEWTON):
@@ -424,14 +426,23 @@
                 pull = rate * left * left
                 slip = slip - (slip - pull * left) / (1.0 + 3.0 * pull)
             creep = live_ref[pl.ds(element, 1), :] * slip
-            stress_ref[spot, :] = trial - creep
+            stress_ref[element, pl.ds(tile, 8, stride=tiles), :] = trial - creep
             strain_ref[pl.ds(element * tiles + tile, 1), :] = 0.125 * jnp.sum(
                 creep, axis=0, keepdims=True
             )
-
-
-def kernel_call(body, sizes, out_shape, memories, scratch, operands):
-    out_spec = pl.BlockSpec(memory_space=pltpu.VMEM)
+        rows = pl.ds(element * 8 * tiles, 8 * tiles)
+        copies.append(
+            pltpu.make_async_copy(stress_ref.at[element], stress_hbm.at[rows], sems.at[element])
+        )
+        copies[-1].start()
+    copies.append(pltpu.make_async_copy(strain_ref, strain_hbm, sems.at[halves]))
+    copies[-1].start()
+    for copy in copies:
+        copy.wait()
+
+
+def kernel_call(body, sizes, out_shape, memories, scratch, operands, space=pltpu.VMEM):
+    out_spec = pl.BlockSpec(memory_space=space)
     pinned = [
         pltpu.with_memory_space_constraint(operand, memory) if memory is pltpu.HBM else operand
         for operand, memory in zip(operands, memories)
@@ -505,12 +516,17 @@
         sizes,
         (floats(sizes.depth * sizes.tiles, LANES), floats(halves * sizes.tiles, LANES)),
         [pltpu.VMEM, pltpu.VMEM, pltpu.VMEM],
-        [],
+        [
+            pltpu.VMEM((halves, 8 * sizes.tiles, LANES), jnp.float32),
+            pltpu.VMEM((halves * sizes.tiles, LANES), jnp.float32),
+            pltpu.SemaphoreType.DMA((halves + 1,)),
+        ],
         (
             live,
             temps.reshape(sizes.devices * halves, LANES),
             trial_stress.reshape(sizes.depth * sizes.tiles, LANES),
         ),
+        space=pltpu.HBM,
     )
     return (
         stress.reshape(sizes.depth, 1, 1, radial),

time: 28.6 us -> 28.7 us (level)
  no operation moved by 1% of the time
where the time goes in v21:
time: 28.7 us; the launch traced here: 28.4 us
  blocking collectives  24.2 us (84%)
  Pallas kernels  2.84 us (10%)
  between operations  1.3 us (5%)
    all_to_all x1, blocking collectives, on_device(): lax.all_to_all(dealt, EVERYONE, split_axis=0, concat_axis=0, tiled=True)  14.9 us
    all_to_all x1, blocking collectives, on_device(): lax.all_to_all(temps, EVERYONE, split_axis=0, concat_axis=0, tiled=True)  9.37 us
    pallas_call x3, Pallas kernels, kernel_call(): pl.pallas_call(functools.partial(body, sizes), out_shape=out_shape, in_sp...  2.84 us

profile of v21, /device:TPU:0, one launch (start us, length us, event | category | flops | bytes accessed | tf_op | source)
XLA Modules:
  0.0 28.4 jit_solution(2335375873502450628)
XLA Ops:
  1.3 1.0 %shard_map.86 = (f32[32,8,128]{2,1,0:T(8,128)S(1)}, f32[8,128]{1,0:T(8,128)S(1)}) custom-call(s32[8]{0:T(128)} %partner_hbm.1, s32[1,8]{1,0:T(1,128)} %order_hbm.1, f32[2,1,8]{2,1,0:T(1,128)} %gap_hbm.1, f32[2,1,8,512]{3,2,1,0:T(8,128)} %temp_hbm.1, f32[2,1,8,512]{3,2,1,0:T(8,128)} %cond_hbm.1, s32[1,1]{1,0:T(1,128)S(6)} %copy.11.active_ref), custom_call_target="tpu_custom_call" | custom-call | tf_op jit(solution)/shard_map/pallas_call | solution.py:450
  2.3 14.9 %all_to_all.10.dealt_ref = f32[32,8,128]{2,1,0:T(8,128)S(1)} all-to-all(f32[32,8,128]{2,1,0:T(8,128)S(1)} %get-tuple-element.7), channel_id=1, replica_groups=mesh['slab'=2,'iface'=4,'mech'=4] {'iface','slab','mech'}, dimensions={0} | all-to-all | bytes 262144 | tf_op jit(solution)/shard_map/all_to_all | solution.py:497
  17.2 1.0 %shard_map.87 = f32[64,128]{1,0:T(8,128)S(1)} custom-call(f32[32,8,128]{2,1,0:T(8,128)S(1)} %all_to_all.10.dealt_ref), custom_call_target="tpu_custom_call" | custom-call | tf_op jit(solution)/shard_map/pallas_call | solution.py:450
  18.1 0.0 copy-start
  18.1 9.4 %all_to_all.11 = f32[32,2,128]{2,1,0:T(2,128)S(1)} all-to-all(f32[32,2,128]{2,1,0:T(2,128)S(1)} %bitcast.5), channel_id=1, replica_groups=mesh['slab'=2,'iface'=4,'mech'=4] {'iface','slab','mech'}, dimensions={0} | all-to-all | bytes 65536 | tf_op jit(solution)/shard_map/all_to_all | solution.py:513
  27.5 0.0 copy-done
  27.5 0.8 %shard_map.88 = (f32[64,128]{1,0:T(8,128)}, f32[8,128]{1,0:T(8,128)}) custom-call(f32[8,128]{1,0:T(8,128)S(1)} %get-tuple-element.6.live_ref, f32[64,128]{1,0:T(8,128)S(1)} %bitcast.6, f32[64,128]{1,0:T(8,128)S(1)} %bitcast.7), custom_call_target="tpu_custom_call" | custom-call | tf_op jit(solution)/shard_map/pallas_call | solution.py:450
Async XLA Ops:
  18.1 9.4 %copy-start = (f32[16,1,1,512]{3,2,1,0:T(1,128)S(1)}, f32[16,1,1,512]{3,2,1,0:T(1,128)}, u32[]{:S(2)}) copy-start(f32[16,1,1,512]{3,2,1,0:T(1,128)} %param.13) | copy-start | bytes 98308

commit v22 on v18

--- a/solution.py
+++ b/solution.py
@@ -201,7 +201,7 @@
         pltpu.make_async_copy(source, target, sems.at[index])
         for index, (source, target) in enumerate(pairs)
     ]
-    for copy in copies:
+    for copy in copies[3:] + copies[:3]:
         copy.start()
     for copy in copies[:3]:
         copy.wait()

time: 28.6 us -> 28.7 us (level)
  no operation moved by 1% of the time
where the time goes in v22:
time: 28.7 us; the launch traced here: 28.5 us
  blocking collectives  24.2 us (84%)
  Pallas kernels  2.93 us (10%)
  between operations  1.3 us (5%)
    all_to_all x1, blocking collectives, on_device(): lax.all_to_all(dealt, EVERYONE, split_axis=0, concat_axis=0, tiled=True)  14.9 us
    all_to_all x1, blocking collectives, on_device(): lax.all_to_all(temps, EVERYONE, split_axis=0, concat_axis=0, tiled=True)  9.37 us
    pallas_call x3, Pallas kernels, kernel_call(): pl.pallas_call(functools.partial(body, sizes), out_shape=out_shape, in_sp...  2.93 us

profile of v22, /device:TPU:0, one launch (start us, length us, event | category | flops | bytes accessed | tf_op | source)
XLA Modules:
  0.0 28.5 jit_solution(308886415580724775)
XLA Ops:
  1.3 1.1 %shard_map.86 = (f32[32,8,128]{2,1,0:T(8,128)S(1)}, f32[8,128]{1,0:T(8,128)S(1)}) custom-call(s32[8]{0:T(128)} %partner_hbm.1, s32[1,8]{1,0:T(1,128)} %order_hbm.1, f32[2,1,8]{2,1,0:T(1,128)} %gap_hbm.1, f32[2,1,8,512]{3,2,1,0:T(8,128)} %temp_hbm.1, f32[2,1,8,512]{3,2,1,0:T(8,128)} %cond_hbm.1, s32[1,1]{1,0:T(1,128)S(6)} %copy.11.active_ref), custom_call_target="tpu_custom_call" | custom-call | tf_op jit(solution)/shard_map/pallas_call | solution.py:439
  2.4 14.9 %all_to_all.10.dealt_ref = f32[32,8,128]{2,1,0:T(8,128)S(1)} all-to-all(f32[32,8,128]{2,1,0:T(8,128)S(1)} %get-tuple-element.7), channel_id=1, replica_groups=mesh['slab'=2,'iface'=4,'mech'=4] {'iface','slab','mech'}, dimensions={0} | all-to-all | bytes 262144 | tf_op jit(solution)/shard_map/all_to_all | solution.py:486
  17.3 1.0 %shard_map.87 = f32[64,128]{1,0:T(8,128)S(1)} custom-call(f32[32,8,128]{2,1,0:T(8,128)S(1)} %all_to_all.10.dealt_ref), custom_call_target="tpu_custom_call" | custom-call | tf_op jit(solution)/shard_map/pallas_call | solution.py:439
  18.2 0.0 copy-start
  18.3 9.4 %all_to_all.11 = f32[32,2,128]{2,1,0:T(2,128)S(1)} all-to-all(f32[32,2,128]{2,1,0:T(2,128)S(1)} %bitcast.5), channel_id=1, replica_groups=mesh['slab'=2,'iface'=4,'mech'=4] {'iface','slab','mech'}, dimensions={0} | all-to-all | bytes 65536 | tf_op jit(solution)/shard_map/all_to_all | solution.py:502
  27.6 0.0 copy-done
  27.6 0.8 %shard_map.88 = (f32[64,128]{1,0:T(8,128)}, f32[8,128]{1,0:T(8,128)}) custom-call(f32[8,128]{1,0:T(8,128)S(1)} %get-tuple-element.6.live_ref, f32[64,128]{1,0:T(8,128)S(1)} %bitcast.6, f32[64,128]{1,0:T(8,128)S(1)} %bitcast.7), custom_call_target="tpu_custom_call" | custom-call | tf_op jit(solution)/shard_map/pallas_call | solution.py:439
Async XLA Ops:
  18.2 9.4 %copy-start = (f32[16,1,1,512]{3,2,1,0:T(1,128)S(1)}, f32[16,1,1,512]{3,2,1,0:T(1,128)}, u32[]{:S(2)}) copy-start(f32[16,1,1,512]{3,2,1,0:T(1,128)} %param.13) | copy-start | bytes 98308

commit v23 on v22

--- a/solution.py
+++ b/solution.py
@@ -201,8 +201,8 @@
         pltpu.make_async_copy(source, target, sems.at[index])
         for index, (source, target) in enumerate(pairs)
     ]
-    for copy in copies[3:] + copies[:3]:
-        copy.start()
+    for index, copy in enumerate(copies):
+        copy.start(priority=0 if index < 3 else 1)
     for copy in copies[:3]:
         copy.wait()
     shape = (sizes.rows, LANES)

time: 28.7 us -> 28.6 us (level)
  no operation moved by 1% of the time
where the time goes in v23:
time: 28.6 us; the launch traced here: 28.4 us
  blocking collectives  24.2 us (85%)
  Pallas kernels  2.82 us (10%)
  between operations  1.3 us (5%)
    all_to_all x1, blocking collectives, on_device(): lax.all_to_all(dealt, EVERYONE, split_axis=0, concat_axis=0, tiled=True)  14.9 us
    all_to_all x1, blocking collectives, on_device(): lax.all_to_all(temps, EVERYONE, split_axis=0, concat_axis=0, tiled=True)  9.37 us
    pallas_call x3, Pallas kernels, kernel_call(): pl.pallas_call(functools.partial(body, sizes), out_shape=out_shape, in_sp...  2.82 us

profile of v23, /device:TPU:0, one launch (start us, length us, event | category | flops | bytes accessed | tf_op | source)
XLA Modules:
  0.0 28.4 jit_solution(16365584312488673168)
XLA Ops:
  1.3 1.0 %shard_map.86 = (f32[32,8,128]{2,1,0:T(8,128)S(1)}, f32[8,128]{1,0:T(8,128)S(1)}) custom-call(s32[8]{0:T(128)} %partner_hbm.1, s32[1,8]{1,0:T(1,128)} %order_hbm.1, f32[2,1,8]{2,1,0:T(1,128)} %gap_hbm.1, f32[2,1,8,512]{3,2,1,0:T(8,128)} %temp_hbm.1, f32[2,1,8,512]{3,2,1,0:T(8,128)} %cond_hbm.1, s32[1,1]{1,0:T(1,128)S(6)} %copy.11.active_ref), custom_call_target="tpu_custom_call" | custom-call | tf_op jit(solution)/shard_map/pallas_call | solution.py:439
  2.3 14.9 %all_to_all.10.dealt_ref = f32[32,8,128]{2,1,0:T(8,128)S(1)} all-to-all(f32[32,8,128]{2,1,0:T(8,128)S(1)} %get-tuple-element.7), channel_id=1, replica_groups=mesh['slab'=2,'iface'=4,'mech'=4] {'iface','slab','mech'}, dimensions={0} | all-to-all | bytes 262144 | tf_op jit(solution)/shard_map/all_to_all | solution.py:486
  17.2 1.0 %shard_map.87 = f32[64,128]{1,0:T(8,128)S(1)} custom-call(f32[32,8,128]{2,1,0:T(8,128)S(1)} %all_to_all.10.dealt_ref), custom_call_target="tpu_custom_call" | custom-call | tf_op jit(solution)/shard_map/pallas_call | solution.py:439
  18.1 0.0 copy-start
  18.1 9.4 %all_to_all.11 = f32[32,2,128]{2,1,0:T(2,128)S(1)} all-to-all(f32[32,2,128]{2,1,0:T(2,128)S(1)} %bitcast.5), channel_id=1, replica_groups=mesh['slab'=2,'iface'=4,'mech'=4] {'iface','slab','mech'}, dimensions={0} | all-to-all | bytes 65536 | tf_op jit(solution)/shard_map/all_to_all | solution.py:502
  27.5 0.0 copy-done
  27.5 0.8 %shard_map.88 = (f32[64,128]{1,0:T(8,128)}, f32[8,128]{1,0:T(8,128)}) custom-call(f32[8,128]{1,0:T(8,128)S(1)} %get-tuple-element.6.live_ref, f32[64,128]{1,0:T(8,128)S(1)} %bitcast.6, f32[64,128]{1,0:T(8,128)S(1)} %bitcast.7), custom_call_target="tpu_custom_call" | custom-call | tf_op jit(solution)/shard_map/pallas_call | solution.py:439
Async XLA Ops:
  18.1 9.4 %copy-start = (f32[16,1,1,512]{3,2,1,0:T(1,128)S(1)}, f32[16,1,1,512]{3,2,1,0:T(1,128)}, u32[]{:S(2)}) copy-start(f32[16,1,1,512]{3,2,1,0:T(1,128)} %param.13) | copy-start | bytes 98308
